TPU v7x, 32 devices: a whole 2x2x4 slice. The times are simulated.
32 devices in a mesh: page: 8 (over y, x, core), row: 4 (over z).
Axes of the slice: x: 2, y: 2, z: 4, core: 2. Of those that a mesh axis runs over, the one named last changes fastest.
Arguments:
- vis_stream: bfloat16 [8, 48, 24, 768], P('page', 'row'), may hold values from -6 to 6
- query_stream: bfloat16 [8, 640, 768], P('page', 'row'), may hold values from -6 to 6
- w_qkv: bfloat16 [4, 768, 2304], replicated, may hold values from -0.21875 to 0.21875
- w_out: bfloat16 [4, 768, 768], replicated, may hold values from -2.5 to 2.5
- b_out: float32 [4, 768], replicated, may hold values from -3 to 3
- w_up: bfloat16 [2, 768, 3072], replicated, may hold values from -0.21875 to 0.21875
- b_up: float32 [2, 3072], replicated, may hold values from -3 to 3
- w_down: bfloat16 [2, 3072, 768], replicated, may hold values from -0.109375 to 0.109375
- b_down: float32 [2, 768], replicated, may hold values from -3 to 3
- norm_gain: float32 [7, 768], replicated, may hold values from 0.5 to 1.5
- norm_bias: float32 [7, 768], replicated, may hold values from -3 to 3
- page_cols: int32 [8], P('page'), may hold values from 12 to 24, as said below
- query_len: int32 [8], P('page'), may hold values from 481 to 640, as said below
- prompt_len: int32 [8], P('page'), may hold values from 1 to 319
- region_ids: int32 [8, 48, 24], P('page', 'row'), may hold values from 0 to 2
- vis_cotangent: bfloat16 [8, 48, 24, 768], P('page', 'row'), may hold values from -6 to 6
- query_cotangent: bfloat16 [8, 640, 768], P('page', 'row'), may hold values from -6 to 6
Outputs:
- vis_out: bfloat16 [8, 48, 24, 768], P('page', 'row')
- query_out: bfloat16 [8, 640, 768], P('page', 'row')
- vis_grad: float32 [8, 48, 24, 768], P('page', 'row')
- query_grad: float32 [8, 640, 768], P('page', 'row')
- grad_qkv: float32 [4, 768, 2304], P(None, 'page', 'row')
- grad_wout: float32 [4, 768, 768], P(None, 'page', 'row')
- grad_bout: float32 [4, 768], P(None, 'page')
- grad_wup: float32 [2, 768, 3072], P(None, 'page', 'row')
- grad_bup: float32 [2, 3072], P(None, 'page')
- grad_wdown: float32 [2, 3072, 768], P(None, 'page', 'row')
- grad_bdown: float32 [2, 768], P(None, 'page')
- grad_gain: float32 [7, 768], P(None, 'page')
- grad_bias: float32 [7, 768], P(None, 'page')
Inputs may be any that keep to these rules, and one draw needn't show every extreme that they name: `page_cols`: some page has all 24 columns live. `query_len`: every page's query sequence reaches its last band of 160 slots; some page fills all 640 slots.
All inputs are finite; a program needn't handle non-finite values.
Results may differ from a plain program's by a relative error of at most 0.014.
Values may be sent and summed in bfloat16 or wider, within the bound.
A program may use at most 384 MiB of HBM per device.

v0:
```python
from functools import partial

import jax
import jax.numpy as jnp
from jax import lax
from jax.sharding import PartitionSpec as P

HDIM = 64
WIN = 12
SHIFT = 6


masked_score = -1e30
norm_eps = 1e-05


def shifted(block, axis, distance):
    devices = range(lax.axis_size(axis))
    route = [((i - distance) % len(devices), i) for i in devices]
    return lax.ppermute(block, axis, route)


def mat_dot(left, right):
    return jnp.dot(left, right, preferred_element_type=jnp.float32)


def mat_left(left, right):
    return lax.dot_general(
        left, right, (((0,), (0,)), ((), ())), preferred_element_type=jnp.float32
    )


def mat_right(left, right):
    return lax.dot_general(
        left, right, (((1,), (1,)), ((), ())), preferred_element_type=jnp.float32
    )


def column_sum(values):
    return jnp.sum(values, axis=0, dtype=jnp.float32)


def norm_forward(values, gain_row, bias_row):
    average = jnp.mean(values, axis=-1, keepdims=True)
    centred = values - average
    spread = jnp.mean(centred * centred, axis=-1, keepdims=True)
    inverse = lax.rsqrt(spread + norm_eps)
    normal = centred * inverse
    return ((normal * gain_row + bias_row).astype(jnp.bfloat16), normal, inverse)


def norm_backward(grad_result, normal, inverse, gain_row):
    grad_normal = grad_result * gain_row
    first_mean = jnp.mean(grad_normal, axis=-1, keepdims=True)
    second_mean = jnp.mean(grad_normal * normal, axis=-1, keepdims=True)
    grad_input = inverse * (grad_normal - first_mean - normal * second_mean)
    return (grad_input, jnp.sum(grad_result * normal, axis=0), jnp.sum(grad_result, axis=0))


def to_windows(grid_cells):
    row_count, col_count = (grid_cells.shape[0], grid_cells.shape[1])
    trailing = grid_cells.shape[2:]
    carved = grid_cells.reshape((row_count // WIN, WIN, col_count // WIN, WIN) + trailing)
    return jnp.swapaxes(carved, 1, 2).reshape((-1, WIN * WIN) + trailing)


def from_windows(blocks, row_count, col_count):
    trailing = blocks.shape[2:]
    carved = blocks.reshape((row_count // WIN, col_count // WIN, WIN, WIN) + trailing)
    return jnp.swapaxes(carved, 1, 2).reshape((row_count, col_count) + trailing)


def roll_down_rows(grid_cells):
    arriving = shifted(grid_cells[:SHIFT], "row", -1)
    return jnp.concatenate([grid_cells[SHIFT:], arriving], axis=0)


def roll_up_rows(grid_cells):
    row_count = grid_cells.shape[0]
    arriving = shifted(grid_cells[row_count - SHIFT :].astype(jnp.bfloat16), "row", 1).astype(
        jnp.float32
    )
    return jnp.concatenate([arriving, grid_cells[: row_count - SHIFT]], axis=0)


def split_heads(values):
    return values.reshape(values.shape[0], values.shape[1], -1, HDIM)


def masked_scores(queries, key_rows, allowed):
    scores = jnp.einsum(
        "gqhd,gkhd->ghqk",
        split_heads(queries),
        split_heads(key_rows),
        preferred_element_type=jnp.float32,
    ) * HDIM ** (-0.5)
    return jnp.where(allowed[:, None], scores, masked_score)


def attend_forward(queries, key_rows, value_rows, allowed):
    scores = masked_scores(queries, key_rows, allowed)
    row_max = jnp.max(scores, axis=-1, keepdims=True)
    raised = jnp.exp(scores - row_max)
    row_total = jnp.sum(raised, axis=-1, keepdims=True)
    probs_low = (raised / row_total).astype(jnp.bfloat16)
    context = jnp.einsum(
        "ghqk,gkhd->gqhd", probs_low, split_heads(value_rows), preferred_element_type=jnp.float32
    )
    return (context.reshape(queries.shape), row_max + jnp.log(row_total))


def attend_backward(queries, key_rows, value_rows, allowed, log_total, grad_context):
    probs = jnp.exp(masked_scores(queries, key_rows, allowed) - log_total)
    probs_low = probs.astype(jnp.bfloat16)
    grad_heads = split_heads(grad_context)
    grad_values = jnp.einsum(
        "ghqk,gqhd->gkhd", probs_low, grad_heads, preferred_element_type=jnp.float32
    )
    grad_probs = jnp.einsum(
        "gqhd,gkhd->ghqk", grad_heads, split_heads(value_rows), preferred_element_type=jnp.float32
    )
    row_delta = jnp.sum(probs * grad_probs, axis=-1, keepdims=True)
    grad_scores = (probs * (grad_probs - row_delta)).astype(jnp.bfloat16)
    grad_queries = jnp.einsum(
        "ghqk,gkhd->gqhd", grad_scores, split_heads(key_rows), preferred_element_type=jnp.float32
    ) * HDIM ** (-0.5)
    grad_keys = jnp.einsum(
        "ghqk,gqhd->gkhd", grad_scores, split_heads(queries), preferred_element_type=jnp.float32
    ) * HDIM ** (-0.5)
    return (
        grad_queries.reshape(queries.shape),
        grad_keys.reshape(key_rows.shape),
        grad_values.reshape(value_rows.shape),
    )


def project_pair(from_rows, to_rows, weight):
    model_width = weight.shape[0]
    queries = mat_dot(from_rows, weight[:, :model_width]).astype(jnp.bfloat16)
    paired = mat_dot(to_rows, weight[:, model_width:]).astype(jnp.bfloat16)
    return (queries, paired[:, :model_width], paired[:, model_width:])


def project_back(from_rows, to_rows, weight, grad_queries, grad_keys, grad_values):
    model_width = weight.shape[0]
    query_low = grad_queries.astype(jnp.bfloat16)
    pair_low = jnp.concatenate([grad_keys, grad_values], axis=1).astype(jnp.bfloat16)
    weight_grad = jnp.concatenate(
        [mat_left(from_rows, query_low), mat_left(to_rows, pair_low)], axis=1
    )
    return (
        weight_grad,
        mat_right(query_low, weight[:, :model_width]),
        mat_right(pair_low, weight[:, model_width:]),
    )


def output_back(context_low, weight, grad_residual):
    grad_low = grad_residual.astype(jnp.bfloat16)
    return (
        mat_left(context_low, grad_low),
        column_sum(grad_low),
        mat_right(grad_low, weight).astype(jnp.bfloat16),
    )


def feed_forward(values, gain_row, bias_row, up_weight, up_bias, down_weight, down_bias):
    hidden, normal, inverse = norm_forward(values, gain_row, bias_row)
    upward = mat_dot(hidden, up_weight) + up_bias
    active = jax.nn.gelu(upward, approximate=True).astype(jnp.bfloat16)
    return (
        values + (mat_dot(active, down_weight) + down_bias),
        (hidden, normal, inverse, upward, active),
    )


def feed_backward(grad_residual, kept_values, gain_row, up_weight, down_weight):
    hidden, normal, inverse, upward, active = kept_values
    grad_low = grad_residual.astype(jnp.bfloat16)
    grad_down = mat_left(active, grad_low)
    grad_down_bias = column_sum(grad_low)
    grad_active = mat_right(grad_low, down_weight)
    gelu_pull = jax.vjp(partial(jax.nn.gelu, approximate=True), upward)[1]
    grad_up_low = gelu_pull(grad_active)[0].astype(jnp.bfloat16)
    grad_up = mat_left(hidden, grad_up_low)
    grad_up_bias = column_sum(grad_up_low)
    grad_input, grad_gain_row, grad_bias_row = norm_backward(
        mat_right(grad_up_low, up_weight), normal, inverse, gain_row
    )
    return (
        grad_residual + grad_input,
        (grad_up, grad_up_bias, grad_down, grad_down_bias, grad_gain_row, grad_bias_row),
    )


def shards(
    vis_stream,
    query_stream,
    w_qkv,
    w_out,
    b_out,
    w_up,
    b_up,
    w_down,
    b_down,
    norm_gain,
    norm_bias,
    page_cols,
    query_len,
    prompt_len,
    region_ids,
    vis_cotangent,
    query_cotangent,
):
    band_rows, page_width, model_width = (
        vis_stream.shape[1],
        vis_stream.shape[2],
        vis_stream.shape[3],
    )
    band_tokens = band_rows * page_width
    query_rows = query_stream.shape[1]
    band_count = lax.axis_size("row")
    band_index = lax.axis_index("row")
    bfloat = jnp.bfloat16
    vis_now = vis_stream[0].reshape(band_tokens, model_width).astype(jnp.float32)
    query_now = query_stream[0].astype(jnp.float32)
    col_limit = page_cols[0]
    query_limit = query_len[0]
    prompt_limit = prompt_len[0]
    own_positions = band_index * query_rows + jnp.arange(query_rows)
    all_positions = jnp.arange(query_rows * band_count)
    key_live = all_positions < query_limit
    self_allowed = key_live[None, :] & (
        (all_positions[None, :] <= own_positions[:, None]) | (all_positions[None, :] < prompt_limit)
    )
    column_live = jnp.arange(band_count * band_tokens) % page_width < col_limit
    visual_allowed = jnp.broadcast_to(column_live[None, :], (query_rows, band_count * band_tokens))
    query_allowed = jnp.broadcast_to(key_live[None, :], (band_tokens, query_rows * band_count))
    rolled_live = (jnp.arange(page_width) + SHIFT) % page_width < col_limit
    live_tiles = to_windows(jnp.broadcast_to(rolled_live[None, :], (band_rows, page_width)))
    region_tiles = to_windows(region_ids[0])
    diagonal = jnp.eye(WIN * WIN, dtype=jnp.bool_)
    window_allowed = (region_tiles[:, :, None] == region_tiles[:, None, :]) & (
        live_tiles[:, None, :] | diagonal[None]
    )
    hidden_self, normal_self, inverse_self = norm_forward(query_now, norm_gain[1], norm_bias[1])
    self_q, self_k, self_v = project_pair(hidden_self, hidden_self, w_qkv[1])
    gathered_keys, gathered_values = (
        lax.all_gather(self_k, "row", axis=0, tiled=True),
        lax.all_gather(self_v, "row", axis=0, tiled=True),
    )
    self_context, self_total = attend_forward(
        self_q[None], gathered_keys[None], gathered_values[None], self_allowed[None]
    )
    self_low = self_context[0].astype(bfloat)
    query_one = query_now + (mat_dot(self_low, w_out[1]) + b_out[1])
    hidden_vis, normal_vis, inverse_vis = norm_forward(vis_now, norm_gain[0], norm_bias[0])
    rolled = roll_down_rows(hidden_vis.reshape(band_rows, page_width, model_width))
    rolled_tiles = to_windows(jnp.roll(rolled, -SHIFT, axis=1))
    tile_shape = rolled_tiles.shape
    rolled_rows = rolled_tiles.reshape(band_tokens, model_width)
    win_q, win_k, win_v = project_pair(rolled_rows, rolled_rows, w_qkv[0])
    win_q = win_q.reshape(tile_shape)
    win_k = win_k.reshape(tile_shape)
    win_v = win_v.reshape(tile_shape)
    win_context, win_total = attend_forward(win_q, win_k, win_v, window_allowed)
    win_low = from_windows(win_context.astype(bfloat), band_rows, page_width)
    unrolled = (
        roll_up_rows(jnp.roll(win_low, SHIFT, axis=1).astype(jnp.float32))
        .astype(bfloat)
        .reshape(band_tokens, model_width)
    )
    vis_one = vis_now + (mat_dot(unrolled, w_out[0]) + b_out[0])
    hidden_ask, normal_ask, inverse_ask = norm_forward(query_one, norm_gain[2], norm_bias[2])
    hidden_look, normal_look, inverse_look = norm_forward(vis_one, norm_gain[3], norm_bias[3])
    look_q, look_k, look_v = project_pair(hidden_ask, hidden_look, w_qkv[2])
    page_keys, page_values = (
        lax.all_gather(look_k, "row", axis=0, tiled=True),
        lax.all_gather(look_v, "row", axis=0, tiled=True),
    )
    look_context, look_total = attend_forward(
        look_q[None], page_keys[None], page_values[None], visual_allowed[None]
    )
    look_low = look_context[0].astype(bfloat)
    query_two = query_one + (mat_dot(look_low, w_out[2]) + b_out[2])
    hidden_memo, normal_memo, inverse_memo = norm_forward(query_two, norm_gain[4], norm_bias[4])
    read_q, read_k, read_v = project_pair(hidden_look, hidden_memo, w_qkv[3])
    memo_keys, memo_values = (
        lax.all_gather(read_k, "row", axis=0, tiled=True),
        lax.all_gather(read_v, "row", axis=0, tiled=True),
    )
    read_context, read_total = attend_forward(
        read_q[None], memo_keys[None], memo_values[None], query_allowed[None]
    )
    read_low = read_context[0].astype(bfloat)
    vis_two = vis_one + (mat_dot(read_low, w_out[3]) + b_out[3])
    vis_three, kept_vis = feed_forward(
        vis_two, norm_gain[5], norm_bias[5], w_up[0], b_up[0], w_down[0], b_down[0]
    )
    query_three, kept_query = feed_forward(
        query_two, norm_gain[6], norm_bias[6], w_up[1], b_up[1], w_down[1], b_down[1]
    )
    vis_back, feed_vis = feed_backward(
        vis_cotangent[0].reshape(band_tokens, model_width).astype(jnp.float32),
        kept_vis,
        norm_gain[5],
        w_up[0],
        w_down[0],
    )
    query_back, feed_query = feed_backward(
        query_cotangent[0].astype(jnp.float32), kept_query, norm_gain[6], w_up[1], w_down[1]
    )
    up_stack = jnp.stack([feed_vis[0], feed_query[0]])
    up_bias_stack = jnp.stack([feed_vis[1], feed_query[1]])
    down_stack = jnp.stack([feed_vis[2], feed_query[2]])
    down_bias_stack = jnp.stack([feed_vis[3], feed_query[3]])
    grad_wout3, grad_bout3, grad_read = output_back(read_low, w_out[3], vis_back)
    read_dq, read_dk, read_dv = attend_backward(
        read_q[None],
        memo_keys[None],
        memo_values[None],
        query_allowed[None],
        read_total,
        grad_read[None],
    )
    memo_dk, memo_dv = (
        lax.psum_scatter(
            read_dk[0].astype(jnp.bfloat16), "row", scatter_dimension=0, tiled=True
        ).astype(jnp.float32),
        lax.psum_scatter(
            read_dv[0].astype(jnp.bfloat16), "row", scatter_dimension=0, tiled=True
        ).astype(jnp.float32),
    )
    grad_qkv3, grad_look_first, grad_memo = project_back(
        hidden_look, hidden_memo, w_qkv[3], read_dq[0], memo_dk, memo_dv
    )
    memo_input, gain_four, bias_four = norm_backward(
        grad_memo, normal_memo, inverse_memo, norm_gain[4]
    )
    query_back = query_back + memo_input
    grad_wout2, grad_bout2, grad_look = output_back(look_low, w_out[2], query_back)
    look_dq, look_dk, look_dv = attend_backward(
        look_q[None],
        page_keys[None],
        page_values[None],
        visual_allowed[None],
        look_total,
        grad_look[None],
    )
    band_dk, band_dv = (
        lax.psum_scatter(
            look_dk[0].astype(jnp.bfloat16), "row", scatter_dimension=0, tiled=True
        ).astype(jnp.float32),
        lax.psum_scatter(
            look_dv[0].astype(jnp.bfloat16), "row", scatter_dimension=0, tiled=True
        ).astype(jnp.float32),
    )
    look_dq_rows = look_dq[0]
    grad_qkv2, grad_ask, grad_look_second = project_back(
        hidden_ask, hidden_look, w_qkv[2], look_dq_rows, band_dk, band_dv
    )
    ask_input, gain_two, bias_two = norm_backward(grad_ask, normal_ask, inverse_ask, norm_gain[2])
    query_back = query_back + ask_input
    look_input, gain_three, bias_three = norm_backward(
        grad_look_first + grad_look_second, normal_look, inverse_look, norm_gain[3]
    )
    vis_back = vis_back + look_input
    grad_wout0, grad_bout0, grad_unrolled = output_back(unrolled, w_out[0], vis_back)
    grad_rolled = roll_down_rows(grad_unrolled.reshape(band_rows, page_width, model_width))
    grad_tiles = to_windows(jnp.roll(grad_rolled, -SHIFT, axis=1))
    win_dq, win_dk, win_dv = attend_backward(
        win_q, win_k, win_v, window_allowed, win_total, grad_tiles
    )
    grad_qkv0, grad_from, grad_into = project_back(
        rolled_rows,
        rolled_rows,
        w_qkv[0],
        win_dq.reshape(band_tokens, model_width),
        win_dk.reshape(band_tokens, model_width),
        win_dv.reshape(band_tokens, model_width),
    )
    grad_shifted = from_windows((grad_from + grad_into).reshape(tile_shape), band_rows, page_width)
    grad_hidden_vis = roll_up_rows(jnp.roll(grad_shifted, SHIFT, axis=1)).reshape(
        band_tokens, model_width
    )
    vis_input, gain_zero, bias_zero = norm_backward(
        grad_hidden_vis, normal_vis, inverse_vis, norm_gain[0]
    )
    vis_back = vis_back + vis_input
    grad_wout1, grad_bout1, grad_self = output_back(self_low, w_out[1], query_back)
    self_dq, self_dk, self_dv = attend_backward(
        self_q[None],
        gathered_keys[None],
        gathered_values[None],
        self_allowed[None],
        self_total,
        grad_self[None],
    )
    own_dk, own_dv = (
        lax.psum_scatter(
            self_dk[0].astype(jnp.bfloat16), "row", scatter_dimension=0, tiled=True
        ).astype(jnp.float32),
        lax.psum_scatter(
            self_dv[0].astype(jnp.bfloat16), "row", scatter_dimension=0, tiled=True
        ).astype(jnp.float32),
    )
    grad_qkv1, grad_self_from, grad_self_into = project_back(
        hidden_self, hidden_self, w_qkv[1], self_dq[0], own_dk, own_dv
    )
    self_input, gain_one, bias_one = norm_backward(
        grad_self_from + grad_self_into, normal_self, inverse_self, norm_gain[1]
    )
    query_back = query_back + self_input
    qkv_stack = jnp.stack([grad_qkv0, grad_qkv1, grad_qkv2, grad_qkv3])
    out_stack = jnp.stack([grad_wout0, grad_wout1, grad_wout2, grad_wout3])
    out_bias_stack = jnp.stack([grad_bout0, grad_bout1, grad_bout2, grad_bout3])
    gain_stack = jnp.stack(
        [gain_zero, gain_one, gain_two, gain_three, gain_four, feed_vis[4], feed_query[4]]
    )
    bias_stack = jnp.stack(
        [bias_zero, bias_one, bias_two, bias_three, bias_four, feed_vis[5], feed_query[5]]
    )
    (
        share_qkv,
        share_out,
        share_out_bias,
        share_up,
        share_up_bias,
        share_down,
        share_down_bias,
        share_gain,
        share_bias,
    ) = (
        lax.psum_scatter(qkv_stack, "page", scatter_dimension=1, tiled=True),
        lax.psum_scatter(out_stack, "page", scatter_dimension=1, tiled=True),
        lax.psum_scatter(out_bias_stack, "page", scatter_dimension=1, tiled=True),
        lax.psum_scatter(up_stack, "page", scatter_dimension=1, tiled=True),
        lax.psum_scatter(up_bias_stack, "page", scatter_dimension=1, tiled=True),
        lax.psum_scatter(down_stack, "page", scatter_dimension=1, tiled=True),
        lax.psum_scatter(down_bias_stack, "page", scatter_dimension=1, tiled=True),
        lax.psum_scatter(gain_stack, "page", scatter_dimension=1, tiled=True),
        lax.psum_scatter(bias_stack, "page", scatter_dimension=1, tiled=True),
    )
    final_qkv, final_out, final_up, final_down = (
        lax.psum_scatter(
            share_qkv.astype(jnp.bfloat16), "row", scatter_dimension=2, tiled=True
        ).astype(jnp.float32),
        lax.psum_scatter(
            share_out.astype(jnp.bfloat16), "row", scatter_dimension=2, tiled=True
        ).astype(jnp.float32),
        lax.psum_scatter(
            share_up.astype(jnp.bfloat16), "row", scatter_dimension=2, tiled=True
        ).astype(jnp.float32),
        lax.psum_scatter(
            share_down.astype(jnp.bfloat16), "row", scatter_dimension=2, tiled=True
        ).astype(jnp.float32),
    )
    final_out_bias, final_up_bias, final_down_bias, final_gain, final_bias = lax.psum(
        (share_out_bias, share_up_bias, share_down_bias, share_gain, share_bias), "row"
    )
    vis_result = vis_three.reshape(1, band_rows, page_width, model_width).astype(bfloat)
    query_result = query_three[None].astype(bfloat)
    vis_gradient = vis_back.reshape(1, band_rows, page_width, model_width)
    query_gradient = query_back[None]
    return (
        vis_result,
        query_result,
        vis_gradient,
        query_gradient,
        final_qkv,
        final_out,
        final_out_bias,
        final_up,
        final_up_bias,
        final_down,
        final_down_bias,
        final_gain,
        final_bias,
    )


def solution(mesh):
    return jax.shard_map(
        shards,
        mesh=mesh,
        in_specs=(
            P("page", "row", None, None),
            P("page", "row", None),
            P(),
            P(),
            P(),
            P(),
            P(),
            P(),
            P(),
            P(),
            P(),
            P("page"),
            P("page"),
            P("page"),
            P("page", "row", None),
            P("page", "row", None, None),
            P("page", "row", None),
        ),
        out_specs=(
            P("page", "row", None, None),
            P("page", "row", None),
            P("page", "row", None, None),
            P("page", "row", None),
            P(None, "page", "row"),
            P(None, "page", "row"),
            P(None, "page"),
            P(None, "page", "row"),
            P(None, "page"),
            P(None, "page", "row"),
            P(None, "page"),
            P(None, "page"),
            P(None, "page"),
        ),
        check_vma=False,
    )
```

profile of v0, /device:TPU:0, one launch (start us, length us, event | category | flops | bytes accessed | tf_op | source)
XLA Modules:
  0.0 1347.4 jit_solution(18407234365150141429)
XLA Ops:
  18.8 10.4 slice_bitcast_fusion.1
  33.6 20.2 %all_gather.18 = bf16[640,768]{1,0:T(8,128)(2,1)} all-gather(bf16[160,768]{1,0:T(8,128)(2,1)S(1)} %get-tuple-element.129), channel_id=1, replica_groups=mesh['page'=8,'row'=4] {'row'}, dimensions={0}, use_global_device_ids=true | all-gather | bytes 1228800 | tf_op jit(solution)/shard_map/all_gather | solution.py:250
  85.7 28.3 %all_gather.19 = bf16[640,768]{1,0:T(8,128)(2,1)S(1)} all-gather(bf16[160,768]{1,0:T(8,128)(2,1)S(1)} %copy-done.84), channel_id=1, replica_groups=mesh['page'=8,'row'=4] {'row'}, dimensions={0}, use_global_device_ids=true | all-gather | bytes 1228800 | tf_op jit(solution)/shard_map/all_gather | solution.py:249
  140.8 33.0 %all-gather.3.cloned.1.call-done = bf16[1152,768]{1,0:T(8,128)(2,1)} async-done(((bf16[288,768]{1,0:T(8,128)(2,1)}), bf16[1152,768]{1,0:T(8,128)(2,1)}) %all-gather.3.cloned.1.call-update) | async-done | bytes 1769488 | tf_op jit(solution)/shard_map/all_gather | solution.py:279
  187.5 20.4 %all_gather.22 = bf16[640,768]{1,0:T(8,128)(2,1)} all-gather(bf16[160,768]{1,0:T(8,128)(2,1)S(1)} %get-tuple-element.127), channel_id=1, replica_groups=mesh['page'=8,'row'=4] {'row'}, dimensions={0}, use_global_device_ids=true | all-gather | bytes 1228800 | tf_op jit(solution)/shard_map/all_gather | solution.py:290
  210.1 21.1 %all_gather.23 = bf16[640,768]{1,0:T(8,128)(2,1)} all-gather(bf16[160,768]{1,0:T(8,128)(2,1)} %get-tuple-element.126), channel_id=1, replica_groups=mesh['page'=8,'row'=4] {'row'}, dimensions={0}, use_global_device_ids=true | all-gather | bytes 1228800 | tf_op jit(solution)/shard_map/all_gather | solution.py:289
  247.2 7.6 convert_reduce_fusion
  271.5 7.3 multiply_reduce_fusion.1
  302.9 21.0 %reduce-scatter.55.cloned.1.call-done = bf16[160,768]{1,0:T(8,128)(2,1)} async-done(((bf16[640,768]{1,0:T(8,128)(2,1)}), bf16[160,768]{1,0:T(8,128)(2,1)}) %reduce-scatter.55.cloned.1.call-update) | async-done | bytes 245776
  411.7 14.5 %reduce-scatter.59.cloned.1.call-done = bf16[288,768]{1,0:T(8,128)(2,1)} async-done(((bf16[1152,768]{1,0:T(8,128)(2,1)}), bf16[288,768]{1,0:T(8,128)(2,1)}) %reduce-scatter.59.cloned.1.call-update) | async-done | bytes 442384
  460.1 6.9 pad_maximum_fusion.1
  539.9 15.6 %pad_maximum_fusion = f32[4,768,2304]{2,1,0:T(8,128)} fusion(f32[1,768,2304]{2,1,0:T(8,128)S(1)} %bitcast.404, f32[1,768,2304]{2,1,0:T(8,128)} %maximum_bitcast_fusion.2, f32[1,768,2304]{2,1,0:T(8,128)S(1)} %bitcast.406, f32[1,768,2304]{2,1,0:T(8,128)} %maximum_bitcast_fusion), kind=kLoop, calls=%fused_computation | loop fusion | flops 21233664 | bytes 56623104 | tf_op jit(solution)/shard_map/stack | solution.py:414
  587.6 101.7 %reduce-scatter.53.cloned.1.call-done = f32[2,384,768]{2,1,0:T(8,128)} async-done(((f32[2,3072,768]{2,1,0:T(8,128)}), f32[2,384,768]{2,1,0:T(8,128)}) %reduce-scatter.53.cloned.1.call-update) | async-done | bytes 2359312 | tf_op jit(solution)/shard_map/reduce_scatter | solution.py:439
  694.0 125.0 %reduce-scatter.49.cloned.1.call-done = f32[2,96,3072]{2,1,0:T(8,128)} async-done(((f32[2,768,3072]{2,1,0:T(8,128)}), f32[2,96,3072]{2,1,0:T(8,128)}) %reduce-scatter.49.cloned.1.call-update) | async-done | bytes 2359312 | tf_op jit(solution)/shard_map/reduce_scatter | solution.py:437
  822.0 173.9 %reduce-scatter.45.cloned.1.call-done = f32[4,96,2304]{2,1,0:T(8,128)} async-done(((f32[4,768,2304]{2,1,0:T(8,128)}), f32[4,96,2304]{2,1,0:T(8,128)}) %reduce-scatter.45.cloned.1.call-update) | async-done | bytes 3538960 | tf_op jit(solution)/shard_map/reduce_scatter | solution.py:434
  1017.9 19.7 %reduce-scatter.73.cloned.1.call-done = f32[384,2]{1,0:T(8,128)} async-done(((f32[3072,2]{1,0:T(8,128)}), f32[384,2]{1,0:T(8,128)}) %reduce-scatter.73.cloned.1.call-update) | async-done | bytes 3088
  1038.7 35.7 %reduce-scatter.75.cloned.1.call-done = f32[96,2]{1,0:T(8,128)} async-done(((f32[768,2]{1,0:T(8,128)}), f32[96,2]{1,0:T(8,128)}) %reduce-scatter.75.cloned.1.call-update) | async-done | bytes 784
  1076.3 35.4 %reduce-scatter.71.cloned.1.call-done = f32[96,4]{1,0:T(8,128)} async-done(((f32[768,4]{1,0:T(8,128)}), f32[96,4]{1,0:T(8,128)}) %reduce-scatter.71.cloned.1.call-update) | async-done | bytes 1552
  1114.1 34.4 %reduce-scatter.77.cloned.1.call-done = f32[96,7]{1,0:T(8,128)} async-done(((f32[768,7]{1,0:T(8,128)}), f32[96,7]{1,0:T(8,128)}) %reduce-scatter.77.cloned.1.call-update) | async-done | bytes 2704
  1149.3 35.9 %reduce-scatter.79.cloned.1.call-done = f32[96,7]{1,0:T(8,128)} async-done(((f32[768,7]{1,0:T(8,128)}), f32[96,7]{1,0:T(8,128)}) %reduce-scatter.79.cloned.1.call-update) | async-done | bytes 2704
  1186.1 19.6 %all-reduce.1 = (f32[4,96]{1,0:T(4,128)}, f32[2,384]{1,0:T(2,128)}, f32[2,96]{1,0:T(2,128)}, f32[7,96]{1,0:T(8,128)}, f32[7,96]{1,0:T(8,128)}) all-reduce(f32[4,96]{1,0:T(4,128)S(1)} %copy.179, f32[2,384]{1,0:T(2,128)S(1)} %copy.181, f32[2,96]{1,0:T(2,128)S(1)} %copy.183, ...), channel_id=1, replica_groups=mesh['page'=8,'row'=4] {'row'}, use_global_device_ids=true, to_apply=%region_53.54 | all-reduce | flops 2688 | bytes 21504 | tf_op jit(solution)/shard_map/psum | solution.py:458
  1211.9 54.8 %all-reduce.4.cloned.1.call-done = bf16[2,384,768]{1,0,2:T(2,128)(2,1)} async-done(((bf16[2,384,768]{1,0,2:T(2,128)(2,1)}), bf16[2,384,768]{1,0,2:T(2,128)(2,1)}) %all-reduce.4.cloned.1.call-update) | async-done | bytes 1179664
  1268.7 28.9 %reduce-scatter.51.cloned.1.call-done = bf16[2,96,768]{2,1,0:T(8,128)(2,1)} async-done(((bf16[2,96,3072]{2,1,0:T(8,128)(2,1)}), bf16[2,96,768]{2,1,0:T(8,128)(2,1)}) %reduce-scatter.51.cloned.1.call-update) | async-done | bytes 294928 | tf_op jit(solution)/shard_map/reduce_scatter | solution.py:451
  1299.5 37.6 %reduce-scatter.67.cloned.1.call-done = bf16[576,384]{1,0:T(8,128)(2,1)} async-done(((bf16[2304,384]{1,0:T(8,128)(2,1)}), bf16[576,384]{1,0:T(8,128)(2,1)}) %reduce-scatter.67.cloned.1.call-update) | async-done | bytes 442384
  (730 shorter events, 418.0 us)
Async XLA Ops:
  7.2 124.2 %all-gather.5.cloned.1.call-start = ((), (), s32[]{:S(2)}) async-start(), calls=%async_computation.19 | async-start | bytes 2211840 | tf_op jit(solution)/shard_map/all_gather | solution.py:278
  13.7 40.2 %collective-permute-start = (bf16[6,24,768]{2,1,0:T(8,128)(2,1)S(1)}, bf16[6,24,768]{2,1,0:T(8,128)(2,1)S(1)}, u32[]{:S(2)}, u32[]{:S(2)}) collective-permute-start(bf16[6,24,768]{2,1,0:T(8,128)(2,1)S(1)} %bitcast.478), channel_id=1, source_target_pairs={{1,0},{2,1},{3,2},{0,3},{5,4},{6,5},{7,6},{4,7},{9,8},{10,9},{11,1... | collective-permute-start | bytes 663560 | tf_op jit(solution)/shard_map/ppermute | solution.py:20
  72.2 8.2 collective-permute-start.1
  85.6 88.2 %all-gather.3.cloned.1.call-start = ((), (), s32[]{:S(2)}) async-start(), calls=%async_computation.18 | async-start | bytes 2211840 | tf_op jit(solution)/shard_map/all_gather | solution.py:279
  123.4 178.3 %reduce-scatter.57.cloned.1.call-start = ((), (), s32[]{:S(2)}) async-start(), calls=%async_computation.26 | async-start | bytes 1228800
  271.4 52.5 %reduce-scatter.55.cloned.1.call-start = ((), (), s32[]{:S(2)}) async-start(), calls=%async_computation.25 | async-start | bytes 1228800
  290.6 119.8 %reduce-scatter.61.cloned.1.call-start = ((), (), s32[]{:S(2)}) async-start(), calls=%async_computation.28 | async-start | bytes 2211840
  349.3 77.0 %reduce-scatter.59.cloned.1.call-start = ((), (), s32[]{:S(2)}) async-start(), calls=%async_computation.27 | async-start | bytes 2211840
  368.5 110.4 %reduce-scatter.65.cloned.1.call-start = ((), (), s32[]{:S(2)}) async-start(), calls=%async_computation.30 | async-start | bytes 1228800
  387.6 93.4 %reduce-scatter.63.cloned.1.call-start = ((), (), s32[]{:S(2)}) async-start(), calls=%async_computation.29 | async-start | bytes 1228800
  404.1 179.8 %reduce-scatter.47.cloned.1.call-start = ((), (), s32[]{:S(2)}) async-start(), calls=%async_computation.21 | async-start | bytes 10616832 | tf_op jit(solution)/shard_map/reduce_scatter | solution.py:435
  440.4 248.9 %reduce-scatter.53.cloned.1.call-start = ((), (), s32[]{:S(2)}) async-start(), calls=%async_computation.24 | async-start | bytes 21233664 | tf_op jit(solution)/shard_map/reduce_scatter | solution.py:439
  453.8 365.3 %reduce-scatter.49.cloned.1.call-start = ((), (), s32[]{:S(2)}) async-start(), calls=%async_computation.22 | async-start | bytes 21233664 | tf_op jit(solution)/shard_map/reduce_scatter | solution.py:437
  467.1 528.8 %reduce-scatter.45.cloned.1.call-start = ((), (), s32[]{:S(2)}) async-start(), calls=%async_computation.20 | async-start | bytes 31850496 | tf_op jit(solution)/shard_map/reduce_scatter | solution.py:434
  555.7 482.0 %reduce-scatter.73.cloned.1.call-start = ((), (), s32[]{:S(2)}) async-start(), calls=%async_computation.34 | async-start | bytes 1769472
  558.6 515.8 %reduce-scatter.75.cloned.1.call-start = ((), (), s32[]{:S(2)}) async-start(), calls=%async_computation.35 | async-start | bytes 442368
  559.8 551.9 %reduce-scatter.71.cloned.1.call-start = ((), (), s32[]{:S(2)}) async-start(), calls=%async_computation.33 | async-start | bytes 442368
  570.5 9.3 collective-permute-start.3
  573.1 575.4 %reduce-scatter.77.cloned.1.call-start = ((), (), s32[]{:S(2)}) async-start(), calls=%async_computation.36 | async-start | bytes 442368
  582.8 602.4 %reduce-scatter.79.cloned.1.call-start = ((), (), s32[]{:S(2)}) async-start(), calls=%async_computation.37 | async-start | bytes 442368
  583.9 626.0 %reduce-scatter.69.cloned.1.call-start = ((), (), s32[]{:S(2)}) async-start(), calls=%async_computation.32 | async-start | bytes 737280
  587.6 679.2 %all-reduce.4.cloned.1.call-start = ((), (), s32[]{:S(2)}) async-start(), calls=%async_computation.38 | async-start | bytes 2359296
  694.0 603.7 %reduce-scatter.51.cloned.1.call-start = ((), (), s32[]{:S(2)}) async-start(), calls=%async_computation.23 | async-start | bytes 1474560 | tf_op jit(solution)/shard_map/reduce_scatter | solution.py:451
  821.9 515.2 %reduce-scatter.67.cloned.1.call-start = ((), (), s32[]{:S(2)}) async-start(), calls=%async_computation.31 | async-start | bytes 2211840
  (196 other events, 3307.5 us)
Sparse Core Ops, SparseCore 0:
  85.8 45.6 all-gather.4
  133.6 40.2 all-gather.2
  271.6 25.2 reduce-scatter.56
  299.2 24.7 reduce-scatter.54
  349.4 36.9 reduce-scatter.60
  388.7 37.4 reduce-scatter.58
  428.6 25.2 reduce-scatter.64
  456.3 24.7 reduce-scatter.62
  484.5 75.0 reduce-scatter.46
  563.1 126.1 reduce-scatter.52
  692.9 126.0 reduce-scatter.48
  822.6 173.2 reduce-scatter.44
  999.2 38.4 reduce-scatter.72
  1040.6 33.7 reduce-scatter.74
  1077.9 33.7 reduce-scatter.70
  1114.6 33.7 reduce-scatter.76
  1151.4 33.7 reduce-scatter.78
  1187.9 21.9 reduce-scatter.68
  1212.3 54.3 all-reduce.3
  1268.9 28.7 reduce-scatter.50
  1300.0 37.0 reduce-scatter.66
where the time goes:
time: 1360 us; the launch traced here: 1350 us
  waiting for transfers between devices  771 us (57%)
  matrix products  195 us (14%)
  local copies, waits for them, and re-layouts  146 us (11%)
  blocking collectives  110 us (8%)
  other arithmetic  95.5 us (7%)
  between operations  20.5 us (2%)
    unnamed x35, waiting for transfers between devices  295 us
    reduce_scatter x1, waiting for transfers between devices, shards(): lax.psum_scatter(qkv_stack, 'page', scatter_dimension=1, tiled=True)  174 us
    reduce_scatter x1, waiting for transfers between devices, shards(): lax.psum_scatter(up_stack, 'page', scatter_dimension=1, tiled=True)  125 us
    reduce_scatter x1, waiting for transfers between devices, shards(): lax.psum_scatter(down_stack, 'page', scatter_dimension=1, tiled=True)  102 us
    unnamed x423, local copies, waits for them, and re-layouts  75.4 us
    dot_general x16, matrix products, mat_right(): lax.dot_general(left, right, (((1,), (1,)), ((), ())), preferred_element_...  50.8 us
    dot_general x16, matrix products, mat_dot(): return jnp.dot(left, right, preferred_element_type=jnp.float32)  35.1 us
    dot_general x16, matrix products, mat_left(): lax.dot_general(left, right, (((0,), (0,)), ((), ())), preferred_element_...  33.9 us
  transfers between devices with their start and end apart: 25, of which 20 were waited for; matrix products, arithmetic and copies ran while one was open for 23% of the time, Pallas kernels for 0%

commit v1 on v0

v1 whole, which is shorter than its diff:
```python
from functools import partial

import jax
import jax.numpy as jnp
from jax import lax
from jax.sharding import PartitionSpec as P

HDIM = 64
WIN = 12
SHIFT = 6

masked_score = -1e30
norm_eps = 1e-05
bfloat = jnp.bfloat16


def ring(count, distance):
    return [(i, (i + distance) % count) for i in range(count)]


def flipped(count, bit):
    return [(i, i ^ bit) for i in range(count)]


def mat_dot(left, right):
    return jnp.dot(left, right, preferred_element_type=jnp.float32)


def mat_left(left, right):
    return lax.dot_general(
        left, right, (((0,), (0,)), ((), ())), preferred_element_type=jnp.float32
    )


def mat_right(left, right):
    return lax.dot_general(
        left, right, (((1,), (1,)), ((), ())), preferred_element_type=jnp.float32
    )


def norm_forward(values, gain_row, bias_row):
    average = jnp.mean(values, axis=-1, keepdims=True)
    centred = values - average
    spread = jnp.mean(centred * centred, axis=-1, keepdims=True)
    inverse = lax.rsqrt(spread + norm_eps)
    normal = centred * inverse
    return ((normal * gain_row + bias_row).astype(bfloat), normal, inverse)


def norm_backward(grad_result, normal, inverse, gain_row):
    grad_normal = grad_result * gain_row
    first_mean = jnp.mean(grad_normal, axis=-1, keepdims=True)
    second_mean = jnp.mean(grad_normal * normal, axis=-1, keepdims=True)
    grad_input = inverse * (grad_normal - first_mean - normal * second_mean)
    return (grad_input, jnp.sum(grad_result * normal, axis=0), jnp.sum(grad_result, axis=0))


def to_windows(grid_cells):
    row_count, col_count = (grid_cells.shape[0], grid_cells.shape[1])
    trailing = grid_cells.shape[2:]
    carved = grid_cells.reshape((row_count // WIN, WIN, col_count // WIN, WIN) + trailing)
    return jnp.swapaxes(carved, 1, 2).reshape((-1, WIN * WIN) + trailing)


def from_windows(blocks, row_count, col_count):
    trailing = blocks.shape[2:]
    carved = blocks.reshape((row_count // WIN, col_count // WIN, WIN, WIN) + trailing)
    return jnp.swapaxes(carved, 1, 2).reshape((row_count, col_count) + trailing)


def to_shifted(grid_cells):
    count = lax.axis_size("row")
    arriving = lax.ppermute(grid_cells[:SHIFT], "row", ring(count, -1))
    rolled = jnp.concatenate([grid_cells[SHIFT:], arriving], axis=0)
    return to_windows(jnp.roll(rolled, -SHIFT, axis=1)).reshape(-1, grid_cells.shape[2])


def from_shifted(tokens, row_count, col_count):
    count = lax.axis_size("row")
    cells = from_windows(tokens.reshape(-1, WIN * WIN, tokens.shape[1]), row_count, col_count)
    rolled = jnp.roll(cells, SHIFT, axis=1)
    arriving = lax.ppermute(rolled[row_count - SHIFT :], "row", ring(count, 1))
    return jnp.concatenate([arriving, rolled[: row_count - SHIFT]], axis=0)


def gather_row(values):
    count = lax.axis_size("row")
    parts = [values] + [lax.ppermute(values, "row", ring(count, s)) for s in range(1, count)]
    return jnp.concatenate(parts, axis=0)


def scatter_row(partial_sums):
    count = lax.axis_size("row")
    parts = jnp.split(partial_sums.astype(bfloat), count, axis=0)
    total = jnp.split(partial_sums, count, axis=0)[0]
    for s in range(1, count):
        total = total + lax.ppermute(parts[s], "row", ring(count, -s)).astype(jnp.float32)
    return total


def halve(blocks, bit, slot):
    count = lax.axis_size("page")
    mine = (lax.axis_index("page") // bit) % 2
    kept = lax.dynamic_index_in_dim(blocks, mine, slot, keepdims=False)
    sent = lax.dynamic_index_in_dim(blocks, 1 - mine, slot, keepdims=False)
    return kept + lax.ppermute(sent, "page", flipped(count, bit))


def reduce_matrix(grad):
    pages = lax.axis_size("page")
    rows = lax.axis_size("row")
    bits = []
    while 2 ** len(bits) < pages:
        bits.append(2 ** len(bits))
    height, width = grad.shape
    blocks = grad.astype(bfloat).reshape((2,) * len(bits) + (height // pages, width))
    if bits:
        blocks = halve(blocks, 1, len(bits) - 1)
    left, right = jnp.split(blocks, 2, axis=-1)
    rest = bits[1:]
    for bit in rest:
        left = halve(left, bit, left.ndim - 3)
    for bit in reversed(rest):
        right = halve(right, bit, 0)
    share = jnp.concatenate([left, right], axis=-1)
    me = lax.axis_index("row")
    pieces = share.reshape(share.shape[0], rows, width // rows)
    total = lax.dynamic_index_in_dim(pieces, me, 1, keepdims=False).astype(jnp.float32)
    for s in range(1, rows):
        sent = lax.dynamic_index_in_dim(pieces, (me + s) % rows, 1, keepdims=False)
        total = total + lax.ppermute(sent, "row", ring(rows, s)).astype(jnp.float32)
    return total


def reduce_vectors(stack):
    pages = lax.axis_size("page")
    rows = lax.axis_size("row")
    bit = 1
    while bit < pages:
        stack = stack.reshape(-1, 2, stack.shape[-1])
        stack = halve(stack, bit, 1)
        bit *= 2
    vector = stack.reshape(-1)
    total = vector
    for s in range(1, rows):
        total = total + lax.ppermute(vector, "row", ring(rows, s))
    return total


def split_heads(values):
    return values.reshape(values.shape[0], values.shape[1], -1, HDIM)


def masked_scores(queries, key_rows, allowed):
    scores = jnp.einsum(
        "gqhd,gkhd->ghqk",
        split_heads(queries),
        split_heads(key_rows),
        preferred_element_type=jnp.float32,
    ) * HDIM ** (-0.5)
    return jnp.where(allowed[:, None], scores, masked_score)


def attend_forward(queries, key_rows, value_rows, allowed):
    scores = masked_scores(queries, key_rows, allowed)
    row_max = jnp.max(scores, axis=-1, keepdims=True)
    raised = jnp.exp(scores - row_max)
    row_total = jnp.sum(raised, axis=-1, keepdims=True)
    probs_low = (raised / row_total).astype(bfloat)
    context = jnp.einsum(
        "ghqk,gkhd->gqhd", probs_low, split_heads(value_rows), preferred_element_type=jnp.float32
    )
    return (context.reshape(queries.shape).astype(bfloat), row_max + jnp.log(row_total))


def attend_backward(queries, key_rows, value_rows, allowed, log_total, grad_context):
    probs = jnp.exp(masked_scores(queries, key_rows, allowed) - log_total)
    probs_low = probs.astype(bfloat)
    grad_heads = split_heads(grad_context)
    grad_values = jnp.einsum(
        "ghqk,gqhd->gkhd", probs_low, grad_heads, preferred_element_type=jnp.float32
    )
    grad_probs = jnp.einsum(
        "gqhd,gkhd->ghqk", grad_heads, split_heads(value_rows), preferred_element_type=jnp.float32
    )
    row_delta = jnp.sum(probs * grad_probs, axis=-1, keepdims=True)
    grad_scores = (probs * (grad_probs - row_delta)).astype(bfloat)
    grad_queries = jnp.einsum(
        "ghqk,gkhd->gqhd", grad_scores, split_heads(key_rows), preferred_element_type=jnp.float32
    ) * HDIM ** (-0.5)
    grad_keys = jnp.einsum(
        "ghqk,gqhd->gkhd", grad_scores, split_heads(queries), preferred_element_type=jnp.float32
    ) * HDIM ** (-0.5)
    return (
        grad_queries.reshape(queries.shape).astype(bfloat),
        grad_keys.reshape(key_rows.shape).astype(bfloat),
        grad_values.reshape(value_rows.shape).astype(bfloat),
    )


def project(from_rows, to_rows, weight):
    width = weight.shape[0]
    queries = mat_dot(from_rows, weight[:, :width]).astype(bfloat)
    paired = mat_dot(to_rows, weight[:, width:]).astype(bfloat)
    return (queries, paired[:, :width], paired[:, width:])


def project_back(from_rows, to_rows, weight, dq, dk, dv):
    width = weight.shape[0]
    pair = jnp.concatenate([dk, dv], axis=1)
    weight_grad = jnp.concatenate([mat_left(from_rows, dq), mat_left(to_rows, pair)], axis=1)
    return (weight_grad, mat_right(dq, weight[:, :width]), mat_right(pair, weight[:, width:]))


def output_back(context_low, weight, grad_residual):
    grad_low = grad_residual.astype(bfloat)
    return (
        mat_left(context_low, grad_low),
        jnp.sum(grad_low, axis=0, dtype=jnp.float32),
        mat_right(grad_low, weight).astype(bfloat),
    )


def feed_forward(values, gain_row, bias_row, up_weight, up_bias, down_weight, down_bias):
    hidden, normal, inverse = norm_forward(values, gain_row, bias_row)
    upward = mat_dot(hidden, up_weight) + up_bias
    active = jax.nn.gelu(upward, approximate=True).astype(bfloat)
    return (
        values + (mat_dot(active, down_weight) + down_bias),
        (hidden, normal, inverse, upward, active),
    )


def feed_backward(grad_residual, kept_values, gain_row, up_weight, down_weight):
    hidden, normal, inverse, upward, active = kept_values
    grad_low = grad_residual.astype(bfloat)
    grad_down = mat_left(active, grad_low)
    grad_down_bias = jnp.sum(grad_low, axis=0, dtype=jnp.float32)
    grad_active = mat_right(grad_low, down_weight)
    gelu_pull = jax.vjp(partial(jax.nn.gelu, approximate=True), upward)[1]
    grad_up_low = gelu_pull(grad_active)[0].astype(bfloat)
    grad_up = mat_left(hidden, grad_up_low)
    grad_up_bias = jnp.sum(grad_up_low, axis=0, dtype=jnp.float32)
    grad_input, gain_grad, bias_grad = norm_backward(
        mat_right(grad_up_low, up_weight), normal, inverse, gain_row
    )
    return (
        grad_residual + grad_input,
        (grad_up, grad_up_bias, grad_down, grad_down_bias, gain_grad, bias_grad),
    )


def shards(
    vis_stream,
    query_stream,
    w_qkv,
    w_out,
    b_out,
    w_up,
    b_up,
    w_down,
    b_down,
    norm_gain,
    norm_bias,
    page_cols,
    query_len,
    prompt_len,
    region_ids,
    vis_cotangent,
    query_cotangent,
):
    band_rows, page_width, width = vis_stream.shape[1:]
    tokens = band_rows * page_width
    query_rows = query_stream.shape[1]
    bands = lax.axis_size("row")
    me = lax.axis_index("row")
    pages = lax.axis_size("page")
    x0 = to_shifted(vis_stream[0]).astype(jnp.float32)
    gx3 = to_shifted(vis_cotangent[0]).astype(jnp.float32)
    y0 = query_stream[0].astype(jnp.float32)
    gy3 = query_cotangent[0].astype(jnp.float32)
    col_limit, query_limit, prompt_limit = page_cols[0], query_len[0], prompt_len[0]

    own_positions = me * query_rows + jnp.arange(query_rows)
    all_positions = jnp.concatenate(
        [((me - s) % bands) * query_rows + jnp.arange(query_rows) for s in range(bands)]
    )
    key_live = all_positions < query_limit
    self_allowed = key_live[None, :] & (
        (all_positions[None, :] <= own_positions[:, None]) | (all_positions[None, :] < prompt_limit)
    )
    rolled_live = (jnp.arange(page_width) + SHIFT) % page_width < col_limit
    live_tiles = to_windows(jnp.broadcast_to(rolled_live[None, :], (band_rows, page_width)))
    visual_allowed = jnp.broadcast_to(
        jnp.tile(live_tiles.reshape(-1), bands)[None, :], (query_rows, bands * tokens)
    )
    query_allowed = jnp.broadcast_to(key_live[None, :], (tokens, query_rows * bands))
    region_tiles = to_windows(region_ids[0])
    diagonal = jnp.eye(WIN * WIN, dtype=jnp.bool_)
    window_allowed = (region_tiles[:, :, None] == region_tiles[:, None, :]) & (
        live_tiles[:, None, :] | diagonal[None]
    )
    tile_shape = (tokens // (WIN * WIN), WIN * WIN, width)

    hs, n1, i1 = norm_forward(y0, norm_gain[1], norm_bias[1])
    hs_all = gather_row(hs)
    hv, n0, i0 = norm_forward(x0, norm_gain[0], norm_bias[0])
    qw, kw, vw = (v.reshape(tile_shape) for v in project(hv, hv, w_qkv[0]))
    cw, lw = attend_forward(qw, kw, vw, window_allowed)
    cw = cw.reshape(tokens, width)
    x1 = x0 + (mat_dot(cw, w_out[0]) + b_out[0])
    hl, n3, i3 = norm_forward(x1, norm_gain[3], norm_bias[3])
    hl_all = gather_row(hl)

    qs, ks, vs = project(hs, hs_all, w_qkv[1])
    cs, ls = attend_forward(qs[None], ks[None], vs[None], self_allowed[None])
    cs = cs[0]
    y1 = y0 + (mat_dot(cs, w_out[1]) + b_out[1])
    ha, n2, i2 = norm_forward(y1, norm_gain[2], norm_bias[2])
    qa, kl, vl = project(ha, hl_all, w_qkv[2])
    ca, la = attend_forward(qa[None], kl[None], vl[None], visual_allowed[None])
    ca = ca[0]
    y2 = y1 + (mat_dot(ca, w_out[2]) + b_out[2])
    hm, n4, i4 = norm_forward(y2, norm_gain[4], norm_bias[4])
    hm_all = gather_row(hm)
    y3, kept_query = feed_forward(
        y2, norm_gain[6], norm_bias[6], w_up[1], b_up[1], w_down[1], b_down[1]
    )
    gy2, feed_query = feed_backward(gy3, kept_query, norm_gain[6], w_up[1], w_down[1])
    final_up1 = reduce_matrix(feed_query[0])
    final_down1 = reduce_matrix(feed_query[2])

    qr, km, vm = project(hl, hm_all, w_qkv[3])
    cr, lr = attend_forward(qr[None], km[None], vm[None], query_allowed[None])
    cr = cr[0]
    x2 = x1 + (mat_dot(cr, w_out[3]) + b_out[3])
    x3, kept_vis = feed_forward(
        x2, norm_gain[5], norm_bias[5], w_up[0], b_up[0], w_down[0], b_down[0]
    )
    gx2, feed_vis = feed_backward(gx3, kept_vis, norm_gain[5], w_up[0], w_down[0])
    final_up0 = reduce_matrix(feed_vis[0])
    final_down0 = reduce_matrix(feed_vis[2])

    wout3, bout3, dcr = output_back(cr, w_out[3], gx2)
    dqr, dkm, dvm = attend_backward(
        qr[None], km[None], vm[None], query_allowed[None], lr, dcr[None]
    )
    qkv3, dhl, dhm = project_back(hl, hm_all, w_qkv[3], dqr[0], dkm[0], dvm[0])
    gy_memo, gain4, bias4 = norm_backward(scatter_row(dhm), n4, i4, norm_gain[4])
    gy2 = gy2 + gy_memo
    final_out3 = reduce_matrix(wout3)
    final_qkv3 = reduce_matrix(qkv3)

    wout2, bout2, dca = output_back(ca, w_out[2], gy2)
    dqa, dkl, dvl = attend_backward(
        qa[None], kl[None], vl[None], visual_allowed[None], la, dca[None]
    )
    qkv2, dha, dhl_all = project_back(ha, hl_all, w_qkv[2], dqa[0], dkl[0], dvl[0])
    gy_ask, gain2, bias2 = norm_backward(dha, n2, i2, norm_gain[2])
    gy1 = gy2 + gy_ask
    gx_look, gain3, bias3 = norm_backward(dhl + scatter_row(dhl_all), n3, i3, norm_gain[3])
    gx1 = gx2 + gx_look
    final_out2 = reduce_matrix(wout2)
    final_qkv2 = reduce_matrix(qkv2)

    wout1, bout1, dcs = output_back(cs, w_out[1], gy1)
    dqs, dks, dvs = attend_backward(qs[None], ks[None], vs[None], self_allowed[None], ls, dcs[None])
    qkv1, dhs, dhs_all = project_back(hs, hs_all, w_qkv[1], dqs[0], dks[0], dvs[0])
    gy_self, gain1, bias1 = norm_backward(dhs + scatter_row(dhs_all), n1, i1, norm_gain[1])
    gy0 = gy1 + gy_self
    final_out1 = reduce_matrix(wout1)
    final_qkv1 = reduce_matrix(qkv1)

    wout0, bout0, dcw = output_back(cw, w_out[0], gx1)
    dqw, dkw, dvw = attend_backward(qw, kw, vw, window_allowed, lw, dcw.reshape(tile_shape))
    dqw, dkw, dvw = (v.reshape(tokens, width) for v in (dqw, dkw, dvw))
    qkv0, dr_from, dr_into = project_back(hv, hv, w_qkv[0], dqw, dkw, dvw)
    gx_win, gain0, bias0 = norm_backward(dr_from + dr_into, n0, i0, norm_gain[0])
    gx0 = gx1 + gx_win
    final_out0 = reduce_matrix(wout0)
    final_qkv0 = reduce_matrix(qkv0)

    vectors = [
        jnp.stack([bout0, bout1, bout2, bout3]),
        jnp.stack([feed_vis[1], feed_query[1]]),
        jnp.stack([feed_vis[3], feed_query[3]]),
        jnp.stack([gain0, gain1, gain2, gain3, gain4, feed_vis[4], feed_query[4]]),
        jnp.stack([bias0, bias1, bias2, bias3, bias4, feed_vis[5], feed_query[5]]),
    ]
    blocks = [
        jnp.swapaxes(v.reshape(v.shape[0], pages, -1), 0, 1).reshape(pages, -1) for v in vectors
    ]
    reduced = reduce_vectors(jnp.concatenate(blocks, axis=1))
    finals, start = [], 0
    for v in vectors:
        size = v.size // pages
        finals.append(reduced[start : start + size].reshape(v.shape[0], -1))
        start += size

    return (
        from_shifted(x3.astype(bfloat), band_rows, page_width)[None],
        y3[None].astype(bfloat),
        from_shifted(gx0, band_rows, page_width)[None],
        gy0[None],
        jnp.stack([final_qkv0, final_qkv1, final_qkv2, final_qkv3]),
        jnp.stack([final_out0, final_out1, final_out2, final_out3]),
        finals[0],
        jnp.stack([final_up0, final_up1]),
        finals[1],
        jnp.stack([final_down0, final_down1]),
        finals[2],
        finals[3],
        finals[4],
    )


def solution(mesh):
    return jax.shard_map(
        shards,
        mesh=mesh,
        in_specs=(
            P("page", "row", None, None),
            P("page", "row", None),
            P(),
            P(),
            P(),
            P(),
            P(),
            P(),
            P(),
            P(),
            P(),
            P("page"),
            P("page"),
            P("page"),
            P("page", "row", None),
            P("page", "row", None, None),
            P("page", "row", None),
        ),
        out_specs=(
            P("page", "row", None, None),
            P("page", "row", None),
            P("page", "row", None, None),
            P("page", "row", None),
            P(None, "page", "row"),
            P(None, "page", "row"),
            P(None, "page"),
            P(None, "page", "row"),
            P(None, "page"),
            P(None, "page", "row"),
            P(None, "page"),
            P(None, "page"),
            P(None, "page"),
        ),
        check_vma=False,
    )
```

time: 1360 us -> 835 us (0.61)
  waiting for transfers between devices: 771 us -> 181 us
  starting transfers between devices: 10.6 us -> 148 us
  blocking collectives: 110 us -> 0 us
  local copies, waits for them, and re-layouts: 146 us -> 192 us
    reduce_scatter x5 -> x0, waiting for transfers between devices: 430 us -> none  [the longest x1 174 us: shards(): lax.psum_scatter(qkv_stack, 'page', scatter_dimension=1, tiled=True)]
    unnamed x35 -> x0, waiting for transfers between devices: 295 us -> none
    ppermute x4 -> x124, waiting for transfers between devices: 10.7 us -> 181 us  [the longest x63 99 us: halve(): return kept + lax.ppermute(sent, 'page', flipped(count, bit))]
    ppermute x4 -> x124, starting transfers between devices: 8.56 us -> 148 us  [the longest x63 57.9 us: halve(): return kept + lax.ppermute(sent, 'page', flipped(count, bit))]
    all_gather x4 -> x0, blocking collectives: 90 us -> none  [the longest x1 28.3 us: shards(): lax.all_gather(self_k, 'row', axis=0, tiled=True)]
    unnamed x423 -> x565, local copies, waits for them, and re-layouts: 75.4 us -> 22.9 us
    another operation x12 -> x16, other arithmetic: 48.6 us -> 10.1 us  [the longest x5 3.31 us: shards(): jnp.stack([final_qkv0, final_qkv1, final_qkv2, final_qkv3])]
    add x6 -> x72, other arithmetic: 1.9 us -> 39.5 us  [the longest x63 35.2 us: halve(): return kept + lax.ppermute(sent, 'page', flipped(count, bit))]
  transfers between devices with their start and end apart: 25 -> 124, of which waited for: 20 -> 44; matrix products, arithmetic and copies ran while one was open for 23% -> 53% of each run, Pallas kernels for 0% -> 0%
where the time goes in v1:
time: 835 us; the launch traced here: 822 us
  matrix products  193 us (23%)
  local copies, waits for them, and re-layouts  192 us (23%)
  waiting for transfers between devices  181 us (22%)
  starting transfers between devices  148 us (18%)
  other arithmetic  99.9 us (12%)
    ppermute x63, waiting for transfers between devices, halve(): return kept + lax.ppermute(sent, 'page', flipped(count, bit))  99 us
    ppermute x63, starting transfers between devices, halve(): return kept + lax.ppermute(sent, 'page', flipped(count, bit))  57.9 us
    ppermute x36, starting transfers between devices, reduce_matrix(): total = total + lax.ppermute(sent, 'row', ring(rows, s)).astype(jnp.float32)  57.3 us
    dot_general x16, matrix products, mat_right(): lax.dot_general(left, right, (((1,), (1,)), ((), ())), preferred_element_...  53.1 us
    ppermute x9, waiting for transfers between devices, scatter_row(): lax.ppermute(parts[s], 'row', ring(count, -s)).astype(jnp.float32)  40.9 us
    dot_general x16, matrix products, mat_dot(): return jnp.dot(left, right, preferred_element_type=jnp.float32)  39.2 us
    dot_general x16, matrix products, mat_left(): lax.dot_general(left, right, (((0,), (0,)), ((), ())), preferred_element_...  36.6 us
    add x63, other arithmetic, halve(): return kept + lax.ppermute(sent, 'page', flipped(count, bit))  35.2 us
  transfers between devices with their start and end apart: 124, of which 44 were waited for; matrix products, arithmetic and copies ran while one was open for 53% of the time, Pallas kernels for 0%

profile of v1, /device:TPU:0, one launch (start us, length us, event | category | flops | bytes accessed | tf_op | source)
XLA Modules:
  0.0 822.2 jit_solution(5213702172833364831)
XLA Ops:
  6.8 5.0 collective-permute-start.3
  25.6 9.5 %slice_bitcast_fusion.1 = (bf16[768,2304]{1,0:T(8,128)(2,1)}, bf16[768,2304]{1,0:T(8,128)(2,1)S(1)}, bf16[768,2304]{1,0:T(8,128)(2,1)}, bf16[768,2304]{1,0:T(8,128)(2,1)}) fusion(bf16[4,768,2304]{2,1,0:T(8,128)(2,1)} %param.19), kind=kLoop, calls=%fused_computation.95 | loop fusion | bytes 28311552 | tf_op jit(solution)/shard_map/squeeze | solution.py:320
  113.7 5.1 convolution_convert_fusion
  185.1 4.7 convert_reduce_fusion
  189.8 4.8 multiply_reduce_fusion.5
  203.4 4.6 convolution_convert_fusion.2
  210.1 6.9 fusion.112
  217.0 5.8 multiply_reduce_fusion.1
  276.4 6.4 collective-permute-done.14
  282.8 8.6 %collective-permute-done.13 = bf16[160,768]{1,0:T(8,128)(2,1)S(1)} collective-permute-done((bf16[160,768]{1,0:T(8,128)(2,1)}, bf16[160,768]{1,0:T(8,128)(2,1)S(1)}, u32[]{:S(2)}, u32[]{:S(2)}) %collective-permute-start.13) | collective-permute-done | bytes 245792 | tf_op jit(solution)/shard_map/ppermute | solution.py:97
  291.4 5.4 multiply_reduce_fusion.16
  303.1 6.6 fusion.52
  309.7 5.1 multiply_reduce_fusion
  357.8 4.8 fusion.322
  362.6 4.7 convolution_convert_fusion.6
  393.0 9.6 %collective-permute-done.17 = bf16[288,768]{1,0:T(8,128)(2,1)} collective-permute-done((bf16[288,768]{1,0:T(8,128)(2,1)}, bf16[288,768]{1,0:T(8,128)(2,1)}, u32[]{:S(2)}, u32[]{:S(2)}) %collective-permute-start.17) | collective-permute-done | bytes 442400 | tf_op jit(solution)/shard_map/ppermute | solution.py:97
  404.1 16.3 %collective-permute-done.16 = bf16[288,768]{1,0:T(8,128)(2,1)S(1)} collective-permute-done((bf16[288,768]{1,0:T(8,128)(2,1)}, bf16[288,768]{1,0:T(8,128)(2,1)S(1)}, u32[]{:S(2)}, u32[]{:S(2)}) %collective-permute-start.16) | collective-permute-done | bytes 442400 | tf_op jit(solution)/shard_map/ppermute | solution.py:97
  603.4 7.8 collective-permute-done.50
  612.2 4.9 collective-permute-done.48
  640.1 16.6 %collective-permute-done.42 = bf16[96,1152]{1,0:T(8,128)(2,1)S(1)} collective-permute-done((bf16[96,1152]{1,0:T(8,128)(2,1)S(1)}, bf16[96,1152]{1,0:T(8,128)(2,1)S(1)}, u32[]{:S(2)}, u32[]{:S(2)}) %collective-permute-start.42) | collective-permute-done | bytes 221216 | tf_op jit(solution)/shard_map/ppermute | solution.py:106
  663.4 5.2 collective-permute-done.34
  671.1 5.8 collective-permute-done.32
  709.8 27.7 %collective-permute-done.23 = bf16[2,96,1152]{2,1,0:T(8,128)(2,1)S(1)} collective-permute-done((bf16[2,96,1152]{2,1,0:T(8,128)(2,1)S(1)}, bf16[2,96,1152]{2,1,0:T(8,128)(2,1)S(1)}, u32[]{:S(2)}, u32[]{:S(2)}) %collective-permute-start.23) | collective-permute-done | bytes 442400 | tf_op jit(solution)/shard_map/ppermute | solution.py:106
  784.2 6.7 collective-permute-done.122
  (1259 shorter events, 625.8 us)
Async XLA Ops:
  6.8 84.0 %collective-permute-start.3 = (bf16[160,768]{1,0:T(8,128)(2,1)}, bf16[160,768]{1,0:T(8,128)(2,1)}, u32[]{:S(2)}, u32[]{:S(2)}) collective-permute-start(bf16[160,768]{1,0:T(8,128)(2,1)} %fusion.198), channel_id=1, source_target_pairs={{0,3},{1,0},{2,1},{3,2},{4,7},{5,4},{6,5},{7,6},{8,11},{9,8},{10,9... | collective-permute-start | bytes 737288 | tf_op jit(solution)/shard_map/ppermute | solution.py:88
  11.9 79.0 %collective-permute-start.2 = (bf16[160,768]{1,0:T(8,128)(2,1)}, bf16[160,768]{1,0:T(8,128)(2,1)}, u32[]{:S(2)}, u32[]{:S(2)}) collective-permute-start(bf16[160,768]{1,0:T(8,128)(2,1)} %fusion.198), channel_id=1, source_target_pairs={{0,2},{1,3},{2,0},{3,1},{4,6},{5,7},{6,4},{7,5},{8,10},{9,11},{10,... | collective-permute-start | bytes 737288 | tf_op jit(solution)/shard_map/ppermute | solution.py:88
  11.9 79.0 %collective-permute-start.1 = (bf16[160,768]{1,0:T(8,128)(2,1)}, bf16[160,768]{1,0:T(8,128)(2,1)}, u32[]{:S(2)}, u32[]{:S(2)}) collective-permute-start(bf16[160,768]{1,0:T(8,128)(2,1)} %fusion.198), channel_id=1, source_target_pairs={{0,1},{1,2},{2,3},{3,0},{4,5},{5,6},{6,7},{7,4},{8,9},{9,10},{10,1... | collective-permute-start | bytes 737288 | tf_op jit(solution)/shard_map/ppermute | solution.py:88
  18.7 57.6 %collective-permute-start.11 = (bf16[6,24,768]{2,1,0:T(8,128)(2,1)}, bf16[6,24,768]{2,1,0:T(8,128)(2,1)}, u32[]{:S(2)}, u32[]{:S(2)}) collective-permute-start(bf16[6,24,768]{2,1,0:T(8,128)(2,1)} %get-tuple-element.156), channel_id=1, source_target_pairs={{0,3},{1,0},{2,1},{3,2},{4,7},{5,4},{6,5},{7,6},{8,11},{9,8},{10,9... | collective-permute-start | bytes 663560 | tf_op jit(solution)/shard_map/ppermute | solution.py:73
  72.8 37.2 %collective-permute-start.6 = (bf16[288,768]{1,0:T(8,128)(2,1)}, bf16[288,768]{1,0:T(8,128)(2,1)}, u32[]{:S(2)}, u32[]{:S(2)}) collective-permute-start(bf16[288,768]{1,0:T(8,128)(2,1)} %add_convert_fusion.2), channel_id=1, source_target_pairs={{0,3},{1,0},{2,1},{3,2},{4,7},{5,4},{6,5},{7,6},{8,11},{9,8},{10,9... | collective-permute-start | bytes 1327112 | tf_op jit(solution)/shard_map/ppermute | solution.py:88
  76.2 37.4 %collective-permute-start.5 = (bf16[288,768]{1,0:T(8,128)(2,1)}, bf16[288,768]{1,0:T(8,128)(2,1)}, u32[]{:S(2)}, u32[]{:S(2)}) collective-permute-start(bf16[288,768]{1,0:T(8,128)(2,1)} %add_convert_fusion.2), channel_id=1, source_target_pairs={{0,2},{1,3},{2,0},{3,1},{4,6},{5,7},{6,4},{7,5},{8,10},{9,11},{10,... | collective-permute-start | bytes 1327112 | tf_op jit(solution)/shard_map/ppermute | solution.py:88
  155.4 420.9 %collective-permute-start.116 = (bf16[2,2,384,768]{3,2,0,1:T(8,128)(2,1)}, bf16[2,2,384,768]{3,2,0,1:T(8,128)(2,1)}, u32[]{:S(2)}, u32[]{:S(2)}) collective-permute-start(bf16[2,2,384,768]{3,2,0,1:T(8,128)(2,1)} %bitcast.788), channel_id=1, source_target_pairs={{0,4},{4,0},{8,12},{12,8},{16,20},{20,16},{24,28},{28,24},{1,5},{5... | collective-permute-start | bytes 7077896 | tf_op jit(solution)/shard_map/ppermute | solution.py:106
  274.5 111.9 %collective-permute-start.78 = (bf16[2,2,96,768]{3,2,1,0:T(8,128)(2,1)}, bf16[2,2,96,768]{3,2,1,0:T(8,128)(2,1)}, u32[]{:S(2)}, u32[]{:S(2)}) collective-permute-start(bf16[2,2,96,768]{3,2,1,0:T(8,128)(2,1)} %dynamic-slice_bitcast_fusion.10), channel_id=1, source_target_pairs={{0,4},{4,0},{8,12},{12,8},{16,20},{20,16},{24,28},{28,24},{1,5},{5... | collective-permute-start | bytes 1769480 | tf_op jit(solution)/shard_map/ppermute | solution.py:106
  377.4 125.3 %collective-permute-start.70 = (bf16[2,2,96,768]{3,2,1,0:T(8,128)(2,1)}, bf16[2,2,96,768]{3,2,1,0:T(8,128)(2,1)}, u32[]{:S(2)}, u32[]{:S(2)}) collective-permute-start(bf16[2,2,96,768]{3,2,1,0:T(8,128)(2,1)} %dynamic-slice_bitcast_fusion.11), channel_id=1, source_target_pairs={{0,4},{4,0},{8,12},{12,8},{16,20},{20,16},{24,28},{28,24},{1,5},{5... | collective-permute-start | bytes 1769480 | tf_op jit(solution)/shard_map/ppermute | solution.py:106
  391.5 87.3 %collective-permute-start.81 = (bf16[2,96,384]{2,1,0:T(8,128)(2,1)}, bf16[2,96,384]{2,1,0:T(8,128)(2,1)}, u32[]{:S(2)}, u32[]{:S(2)}) collective-permute-start(bf16[2,96,384]{2,1,0:T(8,128)(2,1)} %dynamic-slice_bitcast_fusion.44), channel_id=1, source_target_pairs={{0,16},{4,20},{8,24},{12,28},{16,0},{20,4},{24,8},{28,12},{1,17},{... | collective-permute-start | bytes 442376 | tf_op jit(solution)/shard_map/ppermute | solution.py:106
  402.6 75.2 %collective-permute-start.79 = (bf16[2,96,384]{2,1,0:T(8,128)(2,1)}, bf16[2,96,384]{2,1,0:T(8,128)(2,1)}, u32[]{:S(2)}, u32[]{:S(2)}) collective-permute-start(bf16[2,96,384]{2,1,0:T(8,128)(2,1)} %dynamic-slice_bitcast_fusion.45), channel_id=1, source_target_pairs={{0,8},{4,12},{8,0},{12,4},{16,24},{20,28},{24,16},{28,20},{1,9},{5... | collective-permute-start | bytes 442376 | tf_op jit(solution)/shard_map/ppermute | solution.py:106
  491.0 46.1 %collective-permute-start.54 = (bf16[2,2,96,768]{3,2,1,0:T(8,128)(2,1)}, bf16[2,2,96,768]{3,2,1,0:T(8,128)(2,1)}, u32[]{:S(2)}, u32[]{:S(2)}) collective-permute-start(bf16[2,2,96,768]{3,2,1,0:T(8,128)(2,1)} %dynamic-slice_bitcast_fusion.13), channel_id=1, source_target_pairs={{0,4},{4,0},{8,12},{12,8},{16,20},{20,16},{24,28},{28,24},{1,5},{5... | collective-permute-start | bytes 1769480 | tf_op jit(solution)/shard_map/ppermute | solution.py:106
  558.6 37.0 %collective-permute-start.108 = (bf16[2,2,384,768]{3,2,0,1:T(8,128)(2,1)}, bf16[2,2,384,768]{3,2,0,1:T(8,128)(2,1)S(1)}, u32[]{:S(2)}, u32[]{:S(2)}) collective-permute-start(bf16[2,2,384,768]{3,2,0,1:T(8,128)(2,1)} %bitcast.895), channel_id=1, source_target_pairs={{0,4},{4,0},{8,12},{12,8},{16,20},{20,16},{24,28},{28,24},{1,5},{5... | collective-permute-start | bytes 7077896 | tf_op jit(solution)/shard_map/ppermute | solution.py:106
  571.8 50.0 %collective-permute-start.22 = (bf16[2,2,96,2304]{3,2,1,0:T(8,128)(2,1)}, bf16[2,2,96,2304]{3,2,1,0:T(8,128)(2,1)}, u32[]{:S(2)}, u32[]{:S(2)}) collective-permute-start(bf16[2,2,96,2304]{3,2,1,0:T(8,128)(2,1)} %fusion.103), channel_id=1, source_target_pairs={{0,4},{4,0},{8,12},{12,8},{16,20},{20,16},{24,28},{28,24},{1,5},{5... | collective-permute-start | bytes 5308424 | tf_op jit(solution)/shard_map/ppermute | solution.py:106
  619.5 68.2 %collective-permute-start.119 = (bf16[2,384,384]{2,1,0:T(8,128)(2,1)}, bf16[2,384,384]{2,1,0:T(8,128)(2,1)}, u32[]{:S(2)}, u32[]{:S(2)}) collective-permute-start(bf16[2,384,384]{2,1,0:T(8,128)(2,1)} %dynamic-slice_bitcast_fusion.2), channel_id=1, source_target_pairs={{0,16},{4,20},{8,24},{12,28},{16,0},{20,4},{24,8},{28,12},{1,17},{... | collective-permute-start | bytes 1769480 | tf_op jit(solution)/shard_map/ppermute | solution.py:106
  621.7 71.7 %collective-permute-start.117 = (bf16[2,384,384]{2,1,0:T(8,128)(2,1)}, bf16[2,384,384]{2,1,0:T(8,128)(2,1)}, u32[]{:S(2)}, u32[]{:S(2)}) collective-permute-start(bf16[2,384,384]{2,1,0:T(8,128)(2,1)} %dynamic-slice_bitcast_fusion.3), channel_id=1, source_target_pairs={{0,8},{4,12},{8,0},{12,4},{16,24},{20,28},{24,16},{28,20},{1,9},{5... | collective-permute-start | bytes 1769480 | tf_op jit(solution)/shard_map/ppermute | solution.py:106
  635.9 47.7 %collective-permute-start.103 = (bf16[2,96,1536]{2,1,0:T(8,128)(2,1)}, bf16[2,96,1536]{2,1,0:T(8,128)(2,1)}, u32[]{:S(2)}, u32[]{:S(2)}) collective-permute-start(bf16[2,96,1536]{2,1,0:T(8,128)(2,1)} %dynamic-slice_bitcast_fusion.6), channel_id=1, source_target_pairs={{0,16},{4,20},{8,24},{12,28},{16,0},{20,4},{24,8},{28,12},{1,17},{... | collective-permute-start | bytes 1769480 | tf_op jit(solution)/shard_map/ppermute | solution.py:106
  637.1 47.9 %collective-permute-start.101 = (bf16[2,96,1536]{2,1,0:T(8,128)(2,1)}, bf16[2,96,1536]{2,1,0:T(8,128)(2,1)}, u32[]{:S(2)}, u32[]{:S(2)}) collective-permute-start(bf16[2,96,1536]{2,1,0:T(8,128)(2,1)} %dynamic-slice_bitcast_fusion.7), channel_id=1, source_target_pairs={{0,8},{4,12},{8,0},{12,4},{16,24},{20,28},{24,16},{28,20},{1,9},{5... | collective-permute-start | bytes 1769480 | tf_op jit(solution)/shard_map/ppermute | solution.py:106
  676.9 65.1 %collective-permute-start.111 = (bf16[2,384,384]{2,1,0:T(8,128)(2,1)}, bf16[2,384,384]{2,1,0:T(8,128)(2,1)}, u32[]{:S(2)}, u32[]{:S(2)}) collective-permute-start(bf16[2,384,384]{2,1,0:T(8,128)(2,1)} %dynamic-slice_bitcast_fusion.4), channel_id=1, source_target_pairs={{0,16},{4,20},{8,24},{12,28},{16,0},{20,4},{24,8},{28,12},{1,17},{... | collective-permute-start | bytes 1769480 | tf_op jit(solution)/shard_map/ppermute | solution.py:106
  701.9 43.0 %collective-permute-start.109 = (bf16[2,384,384]{2,1,0:T(8,128)(2,1)S(1)}, bf16[2,384,384]{2,1,0:T(8,128)(2,1)S(1)}, u32[]{:S(2)}, u32[]{:S(2)}) collective-permute-start(bf16[2,384,384]{2,1,0:T(8,128)(2,1)S(1)} %copy-done.132), channel_id=1, source_target_pairs={{0,8},{4,12},{8,0},{12,4},{16,24},{20,28},{24,16},{28,20},{1,9},{5... | collective-permute-start | bytes 1769480 | tf_op jit(solution)/shard_map/ppermute | solution.py:106
  705.3 34.1 %collective-permute-start.95 = (bf16[2,96,1536]{2,1,0:T(8,128)(2,1)S(1)}, bf16[2,96,1536]{2,1,0:T(8,128)(2,1)S(1)}, u32[]{:S(2)}, u32[]{:S(2)}) collective-permute-start(bf16[2,96,1536]{2,1,0:T(8,128)(2,1)S(1)} %copy-done.134), channel_id=1, source_target_pairs={{0,16},{4,20},{8,24},{12,28},{16,0},{20,4},{24,8},{28,12},{1,17},{... | collective-permute-start | bytes 1769480 | tf_op jit(solution)/shard_map/ppermute | solution.py:106
  706.9 38.4 %collective-permute-start.93 = (bf16[2,96,1536]{2,1,0:T(8,128)(2,1)S(1)}, bf16[2,96,1536]{2,1,0:T(8,128)(2,1)S(1)}, u32[]{:S(2)}, u32[]{:S(2)}) collective-permute-start(bf16[2,96,1536]{2,1,0:T(8,128)(2,1)S(1)} %copy-done.133), channel_id=1, source_target_pairs={{0,8},{4,12},{8,0},{12,4},{16,24},{20,28},{24,16},{28,20},{1,9},{5... | collective-permute-start | bytes 1769480 | tf_op jit(solution)/shard_map/ppermute | solution.py:106
  749.8 48.9 %collective-permute-start.112 = (bf16[384,384]{1,0:T(8,128)(2,1)}, bf16[384,384]{1,0:T(8,128)(2,1)}, u32[]{:S(2)}, u32[]{:S(2)}) collective-permute-start(bf16[384,384]{1,0:T(8,128)(2,1)} %dynamic-slice_bitcast_fusion.24), channel_id=1, source_target_pairs={{0,8},{4,12},{8,0},{12,4},{16,24},{20,28},{24,16},{28,20},{1,9},{5... | collective-permute-start | bytes 884744 | tf_op jit(solution)/shard_map/ppermute | solution.py:106
  752.1 47.7 %collective-permute-start.110 = (bf16[384,384]{1,0:T(8,128)(2,1)}, bf16[384,384]{1,0:T(8,128)(2,1)}, u32[]{:S(2)}, u32[]{:S(2)}) collective-permute-start(bf16[384,384]{1,0:T(8,128)(2,1)} %dynamic-slice_bitcast_fusion.25), channel_id=1, source_target_pairs={{0,16},{4,20},{8,24},{12,28},{16,0},{20,4},{24,8},{28,12},{1,17},{... | collective-permute-start | bytes 884744 | tf_op jit(solution)/shard_map/ppermute | solution.py:106
  (366 other events, 3732.6 us)

commit v2 on v1

v2 whole, which is shorter than its diff:
```python
from functools import partial

import jax
import jax.numpy as jnp
import numpy as np
from jax import lax
from jax.experimental import pallas as pl
from jax.experimental.pallas import tpu as pltpu
from jax.sharding import PartitionSpec as P

HDIM = 64
WIN = 12
SHIFT = 6
PAIR = 2 * HDIM
SCALE = HDIM ** (-0.5)

masked_score = -1e30
norm_eps = 1e-05
bfloat = jnp.bfloat16
full = jnp.float32
ANY = pl.BlockSpec(memory_space=pl.ANY)
VMEM = pl.BlockSpec(memory_space=pltpu.VMEM)
SMEM = pl.BlockSpec(memory_space=pltpu.SMEM)
MESH = pl.DeviceIdType.MESH


def ring(count, distance):
    return [(i, (i + distance) % count) for i in range(count)]


def flipped(count, bit):
    return [(i, i ^ bit) for i in range(count)]


def dot_nn(left, right):
    return jnp.dot(left, right, preferred_element_type=full)


def dot_nt(left, right):
    return lax.dot_general(left, right, (((1,), (1,)), ((), ())), preferred_element_type=full)


def dot_tn(left, right):
    return lax.dot_general(left, right, (((0,), (0,)), ((), ())), preferred_element_type=full)


def normalise(values):
    centred = values - jnp.mean(values, axis=-1, keepdims=True)
    spread = jnp.mean(centred * centred, axis=-1, keepdims=True)
    inverse = lax.rsqrt(spread + norm_eps)
    return centred * inverse, inverse


def norm_forward(values, gain_row, bias_row):
    return (normalise(values)[0] * gain_row + bias_row).astype(bfloat)


def norm_backward(grad, values, gain_row):
    normal, inverse = normalise(values)
    grad_normal = grad * gain_row
    first = jnp.mean(grad_normal, axis=-1, keepdims=True)
    second = jnp.mean(grad_normal * normal, axis=-1, keepdims=True)
    return (
        inverse * (grad_normal - first - normal * second),
        jnp.sum(grad * normal, axis=0, keepdims=True),
        jnp.sum(grad, axis=0, keepdims=True),
    )


def tile_cols(index, size):
    return pl.ds(pl.multiple_of(index * size, size), size)


def matmul_into(out_ref, left_ref, weight_ref, size):
    def step(i, _):
        cols = tile_cols(i, size)
        out_ref[:, cols] = dot_nn(left_ref[...], weight_ref[:, cols]).astype(out_ref.dtype)
        return 0

    lax.fori_loop(0, weight_ref.shape[1] // size, step, 0)


def two_heads(values):
    lane = lax.broadcasted_iota(jnp.int32, values.shape, 1)
    zero = jnp.zeros_like(values)
    return jnp.concatenate(
        [jnp.where(lane < HDIM, values, zero), jnp.where(lane < HDIM, zero, values)], axis=0
    )


def one_pair(stacked):
    count = stacked.shape[0] // 2
    lane = lax.broadcasted_iota(jnp.int32, (count, PAIR), 1)
    return jnp.where(lane < HDIM, stacked[:count], stacked[count:])


def attend_pair(queries, key_rows, value_rows, bias):
    scores = dot_nt(two_heads(queries), key_rows) + bias
    top = jnp.max(scores, axis=-1, keepdims=True)
    raised = jnp.exp(scores - top)
    total = jnp.sum(raised, axis=-1, keepdims=True)
    context = dot_nn(raised.astype(bfloat), value_rows) / total
    return one_pair(context).astype(bfloat), top + jnp.log(total)


def attend_pair_back(queries, key_rows, value_rows, bias, log_total, context, grad_context):
    both = two_heads(queries)
    grad_both = two_heads(grad_context)
    probs = jnp.exp(dot_nt(both, key_rows) + bias - log_total)
    grad_probs = dot_nt(grad_both, value_rows)
    delta = jnp.sum(
        grad_both.astype(full) * jnp.concatenate([context, context], axis=0).astype(full),
        axis=-1,
        keepdims=True,
    )
    grad_scores = (probs * (grad_probs - delta)).astype(bfloat)
    grad_queries = one_pair(dot_nn(grad_scores, key_rows)) * SCALE
    grad_keys = dot_tn(grad_scores, both)
    grad_values = dot_tn(probs.astype(bfloat), grad_both)
    return grad_queries.astype(bfloat), grad_keys.astype(bfloat), grad_values.astype(bfloat)


def put_logs(log_ref, rows, pair, log_total):
    count = log_total.shape[0] // 2
    lane = lax.broadcasted_iota(jnp.int32, (count, PAIR), 1)
    kept = log_ref[rows, :]
    kept = jnp.where(lane == 2 * pair, log_total[:count], kept)
    log_ref[rows, :] = jnp.where(lane == 2 * pair + 1, log_total[count:], kept)


def take_logs(log_ref, rows, pair):
    kept = log_ref[rows, :]
    lane = lax.broadcasted_iota(jnp.int32, kept.shape, 1)
    parts = [
        jnp.sum(jnp.where(lane == 2 * pair + i, kept, 0.0), axis=-1, keepdims=True)
        for i in range(2)
    ]
    return jnp.concatenate(parts, axis=0)


def attend_rows(q_ref, kv_ref, context_ref, log_ref, bias, rows, keys):
    width = q_ref.shape[1]
    key_start = kv_ref.shape[1] - 2 * width

    def step(pair, _):
        cols = tile_cols(pair, PAIR)
        key_cols = pl.ds(pl.multiple_of(key_start + pair * PAIR, PAIR), PAIR)
        value_cols = pl.ds(pl.multiple_of(key_start + width + pair * PAIR, PAIR), PAIR)
        context, log_total = attend_pair(
            q_ref[rows, cols], kv_ref[keys, key_cols], kv_ref[keys, value_cols], bias
        )
        context_ref[rows, cols] = context
        put_logs(log_ref, rows, pair, log_total)
        return 0

    lax.fori_loop(0, width // PAIR, step, 0)


def attend_rows_back(
    q_ref, kv_ref, context_ref, log_ref, grad_ref, dq_ref, dkv_ref, bias, rows, keys
):
    width = q_ref.shape[1]
    key_start = kv_ref.shape[1] - 2 * width
    grad_start = dkv_ref.shape[1] - 2 * width

    def step(pair, _):
        cols = tile_cols(pair, PAIR)
        key_cols = pl.ds(pl.multiple_of(key_start + pair * PAIR, PAIR), PAIR)
        value_cols = pl.ds(pl.multiple_of(key_start + width + pair * PAIR, PAIR), PAIR)
        dq, dk, dv = attend_pair_back(
            q_ref[rows, cols],
            kv_ref[keys, key_cols],
            kv_ref[keys, value_cols],
            bias,
            take_logs(log_ref, rows, pair),
            context_ref[rows, cols],
            grad_ref[rows, cols],
        )
        dq_ref[rows, cols] = dq
        dkv_ref[keys, pl.ds(pl.multiple_of(grad_start + pair * PAIR, PAIR), PAIR)] = dk
        dkv_ref[keys, pl.ds(pl.multiple_of(grad_start + width + pair * PAIR, PAIR), PAIR)] = dv
        return 0

    lax.fori_loop(0, width // PAIR, step, 0)


def allowed_bias(allowed):
    return jnp.where(allowed, 0.0, masked_score).astype(full)


def key_positions(me, bands, rows):
    lane = lax.broadcasted_iota(jnp.int32, (1, bands * rows), 1)
    part = sum((lane >= s * rows).astype(jnp.int32) for s in range(1, bands))
    band = lax.rem(me - part + bands, bands)
    return band * rows + lane - part * rows


def window_live(first, count, scalars, page_width):
    token = first + lax.broadcasted_iota(jnp.int32, (1, count), 1)
    window = lax.div(token, WIN * WIN)
    column = lax.rem(token, WIN) + WIN * lax.rem(window, page_width // WIN)
    return lax.rem(column + SHIFT, page_width) < scalars[1]


def copies_in(pairs, sems):
    copies = [pltpu.make_async_copy(src, dst, sems.at[i]) for i, (src, dst) in enumerate(pairs)]
    for copy in copies:
        copy.start()
    return copies


def low_shape(*shape):
    return jax.ShapeDtypeStruct(shape, bfloat)


def full_shape(*shape):
    return jax.ShapeDtypeStruct(shape, full)


def source_order(page_width, band_rows):
    tokens = band_rows * page_width
    token = np.arange(tokens)
    across = page_width // WIN
    window, inside = token // (WIN * WIN), token % (WIN * WIN)
    row = window // across * WIN + inside // WIN
    column = window % across * WIN + inside % WIN
    source = row * page_width + (column + SHIFT) % page_width
    order = np.zeros((tokens, tokens), np.float32)
    order[token, source] = 1.0
    return order


def fill_shifted(own_ref, arriving_ref, rows_ref):
    band_rows, width = own_ref.shape[1], own_ref.shape[2]
    for i in range(band_rows - SHIFT):
        rows_ref[i * width : (i + 1) * width, :] = own_ref[0, i + SHIFT].astype(full)
    for i in range(SHIFT):
        j = band_rows - SHIFT + i
        rows_ref[j * width : (j + 1) * width, :] = arriving_ref[i].astype(full)


def window_bias(scalars, region_col_ref, region_row_ref, w, page_width):
    size = WIN * WIN
    live = window_live(w * size, size, scalars, page_width)
    own = lax.broadcasted_iota(jnp.int32, (size, size), 0)
    other = lax.broadcasted_iota(jnp.int32, (size, size), 1)
    same = region_col_ref[w] == region_row_ref[w]
    allowed = same & ((own == other) | live)
    bias = allowed_bias(allowed)
    return jnp.concatenate([bias, bias], axis=0)


def self_bias(me, scalars, rows, bands):
    position = key_positions(me, bands, rows)
    own = me * rows + lax.broadcasted_iota(jnp.int32, (rows, 1), 0)
    bias = allowed_bias(
        (position < scalars[2]) & ((position <= own) | (position < scalars[3]))
    )
    return jnp.concatenate([bias, bias], axis=0)


def look_bias(dims, scalars):
    tokens, bands, page_width = dims["tokens"], dims["bands"], dims["page_width"]
    live = window_live(0, tokens, scalars, page_width)
    return jnp.concatenate([allowed_bias(live)] * bands, axis=1)


def read_bias(me, dims, scalars):
    return allowed_bias(key_positions(me, dims["bands"], dims["rows"]) < scalars[2])


class Kernel:
    def __init__(self, refs, hbm, sems):
        self.__dict__.update(refs)
        self.hbm, self.sems = hbm, sems
        self.coming, self.going = {}, []

    def fetch(self, *names):
        for name in names:
            copy = pltpu.make_async_copy(
                self.hbm[name], getattr(self, name), self.sems[name]
            )
            copy.start()
            self.coming[name] = copy

    def ready(self, *names):
        for name in names:
            self.coming.pop(name).wait()

    def save(self, *names):
        for name in names:
            copy = pltpu.make_async_copy(
                getattr(self, name), self.hbm[name], self.sems[name]
            )
            copy.start()
            self.going.append(copy)

    def finish(self):
        for copy in self.going:
            copy.wait()


def launch(body, given, staged, made, kept, scratch, collective, flops):
    sources = list(given) + list(staged)
    results = list(made) + list(kept)
    moved = list(staged) + list(kept)
    arrays = [given[n][0] for n in given] + [staged[n] for n in staged]
    stages = {n: pltpu.VMEM(staged[n].shape, staged[n].dtype) for n in staged}
    stages.update({n: pltpu.VMEM(kept[n].shape, kept[n].dtype) for n in kept})

    def inner(*refs):
        first, second = len(sources), len(sources) + len(results)
        outer = dict(zip(sources, refs[:first])) | dict(zip(results, refs[first:second]))
        inside = dict(zip(list(stages) + list(scratch), refs[second:-1]))
        sems = {n: refs[-1].at[i] for i, n in enumerate(moved)}
        body(Kernel(outer | inside, {n: outer[n] for n in moved}, sems))

    outs = pl.pallas_call(
        inner,
        out_shape=[made[n][0] for n in made] + [kept[n] for n in kept],
        in_specs=[given[n][1] for n in given] + [ANY] * len(staged),
        out_specs=[made[n][1] for n in made] + [ANY] * len(kept),
        scratch_shapes=list(stages.values())
        + list(scratch.values())
        + [pltpu.SemaphoreType.DMA((max(len(moved), 1),))],
        compiler_params=pltpu.CompilerParams(
            vmem_limit_bytes=62 * 2**20, collective_id=collective, has_side_effects=True
        ),
        cost_estimate=pl.CostEstimate(flops=flops, bytes_accessed=2**24, transcendentals=0),
    )(*arrays)
    return dict(zip(results, outs))


def greet(devices):
    barrier = pltpu.get_barrier_semaphore()
    for device in devices:
        pl.semaphore_signal(barrier, inc=1, device_id=device, device_id_type=MESH)
    pl.semaphore_wait(barrier, len(devices))


def band_peers(bands):
    me = lax.axis_index("row")
    return [{"row": lax.rem(me + s, bands)} for s in range(1, bands)]


def gather_start(ref, bands, send, recv):
    copies = []
    for s, peer in enumerate(band_peers(bands), 1):
        copy = pltpu.make_async_remote_copy(
            src_ref=ref.at[0],
            dst_ref=ref.at[s],
            send_sem=send.at[s - 1],
            recv_sem=recv.at[s - 1],
            device_id=peer,
            device_id_type=MESH,
        )
        copy.start()
        copies.append(copy)
    return copies


def front_kernel(dims, r):
    page_width, bands, rows, tokens = (dims[n] for n in ("page_width", "bands", "rows", "tokens"))
    width = r.y0.shape[1]
    me = lax.axis_index("row")
    greet(band_peers(bands))
    loads = {}
    for a in range(3):
        for i, (name, ref) in enumerate((("wqkv%d", r.w_qkv), ("wout%d", r.w_out))):
            copy = pltpu.make_async_copy(
                ref.at[a], getattr(r, name % a), r.weight_sems.at[2 * a + i]
            )
            copy.start()
            loads[name % a] = copy
    above = {"row": lax.rem(me + bands - 1, bands)}
    halos = []
    for i, ref in enumerate((r.vis, r.cot)):
        halo = pltpu.make_async_remote_copy(
            src_ref=ref.at[0, 0:SHIFT],
            dst_ref=r.halo.at[i],
            send_sem=r.halo_send.at[i],
            recv_sem=r.halo_recv.at[i],
            device_id=above,
            device_id_type=MESH,
        )
        halo.start()
        halos.append(halo)
    r.hs[0] = norm_forward(r.y0[...].astype(full), r.gain[1:2, :], r.bias[1:2, :])
    self_copies = gather_start(r.hs, bands, r.self_send, r.self_recv)

    r.log0[...] = jnp.zeros_like(r.log0)
    r.log1[...] = jnp.zeros_like(r.log1)
    r.log2[...] = jnp.zeros_like(r.log2)
    halos[0].wait()
    fill_shifted(r.vis, r.halo.at[0], r.cells)
    x0 = dot_nn(r.order[...], r.cells[...].astype(bfloat))
    r.x0[...] = x0.astype(bfloat)
    r.hv[...] = norm_forward(x0, r.gain[0:1, :], r.bias[0:1, :])
    r.save("x0", "hv")
    loads["wqkv0"].wait()
    r.q0[...] = (dot_nn(r.hv[...], r.wqkv0[:, :width]) * SCALE).astype(bfloat)
    matmul_into(r.kv0, r.hv, r.wqkv0.at[:, width:], width)
    r.save("q0", "kv0")
    size = WIN * WIN
    for w in range(tokens // size):
        part = slice(w * size, (w + 1) * size)
        bias = window_bias(r.scalars, r.region_col, r.region_row, w, page_width)
        attend_rows(r.q0, r.kv0, r.c0, r.log0, bias, part, part)
    r.save("c0", "log0")
    loads["wout0"].wait()
    x1 = r.x0[...].astype(full) + (dot_nn(r.c0[...], r.wout0[...]) + r.b_out[0:1, :])
    r.x1[...] = x1
    r.hl[0] = norm_forward(x1, r.gain[3:4, :], r.bias[3:4, :])
    look_copies = gather_start(r.hl, bands, r.look_send, r.look_recv)
    r.save("x1")

    halos[1].wait()
    fill_shifted(r.cot, r.halo.at[1], r.cells)
    r.gx3[...] = dot_nn(r.order[...], r.cells[...].astype(bfloat)).astype(bfloat)
    r.save("gx3")
    loads["wqkv1"].wait()
    r.q1[...] = (dot_nn(r.hs[0], r.wqkv1[:, :width]) * SCALE).astype(bfloat)
    for copy in self_copies:
        copy.wait_recv()

    def project_self(s, _):
        part = pl.ds(pl.multiple_of(s * rows, rows), rows)
        r.kv1[part, :] = dot_nn(r.hs[s], r.wqkv1[:, width:]).astype(bfloat)
        return 0

    lax.fori_loop(0, bands, project_self, 0)
    r.save("hs", "q1", "kv1")
    bias = self_bias(me, r.scalars, rows, bands)
    attend_rows(r.q1, r.kv1, r.c1, r.log1, bias, slice(None), slice(None))
    r.save("c1", "log1")
    loads["wout1"].wait()
    y1 = r.y0[...].astype(full) + (dot_nn(r.c1[...], r.wout1[...]) + r.b_out[1:2, :])
    r.y1[...] = y1
    r.ha[...] = norm_forward(y1, r.gain[2:3, :], r.bias[2:3, :])
    loads["wqkv2"].wait()
    r.q2[...] = (dot_nn(r.ha[...], r.wqkv2[:, :width]) * SCALE).astype(bfloat)
    r.save("y1", "ha", "q2")

    for s in range(bands):
        if s:
            look_copies[s - 1].wait_recv()
        part = slice(s * tokens, (s + 1) * tokens)
        matmul_into(r.kv2.at[part], r.hl.at[s], r.wqkv2.at[:, width:], width)
    r.save("hl", "kv2")
    attend_rows(r.q2, r.kv2, r.c2, r.log2, look_bias(dims, r.scalars), slice(None), slice(None))
    loads["wout2"].wait()
    y2 = r.y1[...] + (dot_nn(r.c2[...], r.wout2[...]) + r.b_out[2:3, :])
    r.y2[...] = y2
    r.hm[...] = norm_forward(y2, r.gain[4:5, :], r.bias[4:5, :])
    r.save("c2", "log2", "y2", "hm")
    for copy in self_copies + look_copies:
        copy.wait_send()
    r.finish()


def feed_phase(dims, r, stream, norm, values, cot, out, grad, units):
    pages, slab, bands = dims["pages"], dims["slab"], dims["bands"]
    count, width = values.shape
    core = lax.rem(lax.axis_index("page"), 2)
    r.hidden[...] = norm_forward(values[...], r.gain[norm : norm + 1, :], r.bias[norm : norm + 1, :])
    r.total[...] = values[...] + r.b_down[stream : stream + 1, :]
    r.back[...] = jnp.zeros_like(r.back)
    r.down_bias[...] = jnp.sum(cot[...].astype(full), axis=0, keepdims=True)

    def quarter(j, _):
        feed_copy(r, stream, 0, j).wait()
        hidden = r.hidden[...]
        z = dot_nn(hidden, r.up[j]) + r.b_up[stream : stream + 1, tile_cols(j, width)]
        square = z * z
        bend = jnp.tanh(0.7978845608028654 * (z + 0.044715 * (square * z)))
        half = 0.5 * (1.0 + bend)
        slope = half + (0.5 * z) * (1.0 - bend * bend) * (
            0.7978845608028654 * (1.0 + 0.134145 * square)
        )
        active = (z * half).astype(bfloat)
        feed_copy(r, stream, 1, j).wait()
        r.total[...] += dot_nn(active, r.down[j])
        low_grad = cot[...]
        dz = dot_nt(low_grad, r.down[j]) * slope
        r.up_bias[:, tile_cols(j, width)] = jnp.sum(dz, axis=0, keepdims=True)
        dz = dz.astype(bfloat)
        r.back[...] += dot_nt(dz, r.up[j])
        split_blocks(dims, r.tile.at[j, 0], dot_tn(hidden, dz).astype(bfloat), core)
        exchange(r, j, 0).start()
        down_grad = dot_tn(active, low_grad).astype(bfloat)
        deep = bands * slab
        for side in range(2):
            part = down_grad[side * deep : (side + 1) * deep]
            for k in range(bands):
                r.tile[j, 1, lax.rem(side + core, 2), k] = part[k * slab : (k + 1) * slab]
        exchange(r, j, 1).start()
        return 0

    lax.fori_loop(0, bands, quarter, 0)
    out[...] = r.total[...].astype(bfloat)
    pull, gain_grad, bias_grad = norm_backward(
        r.back[...], values[...], r.gain[norm : norm + 1, :]
    )
    grad[...] = cot[...].astype(full) + pull
    r.gain_grad[...] = gain_grad
    r.bias_grad[...] = bias_grad


def feed_copy(r, stream, which, j):
    width = r.up.shape[1]
    if which == 0:
        return pltpu.make_async_copy(
            r.w_up.at[stream, :, tile_cols(j, width)], r.up.at[j], r.weight_sems.at[0, j]
        )
    return pltpu.make_async_copy(
        r.w_down.at[stream, tile_cols(j, width), :], r.down.at[j], r.weight_sems.at[1, j]
    )


def split_blocks(dims, tile, grad, core):
    slab = dims["slab"]
    for block in range(dims["pages"]):
        tile[lax.rem(block + core, 2), block // 2] = grad[block * slab : (block + 1) * slab]


def exchange(r, j, which):
    page = lax.axis_index("page")
    return pltpu.make_async_remote_copy(
        src_ref=r.tile.at[j, which, 1],
        dst_ref=r.landed.at[j, which],
        send_sem=r.core_send.at[j, which],
        recv_sem=r.core_recv.at[j, which],
        device_id={"page": page + 1 - 2 * lax.rem(page, 2)},
        device_id_type=MESH,
    )


def query_feed_kernel(dims, r):
    bands, slab = dims["bands"], dims["slab"]
    page = lax.axis_index("page")
    greet(band_peers(bands) + [{"page": page + 1 - 2 * lax.rem(page, 2)}])
    for j in range(bands):
        feed_copy(r, 1, 0, j).start()
        feed_copy(r, 1, 1, j).start()
    memo = []
    for s, peer in enumerate(band_peers(bands)):
        copy = pltpu.make_async_remote_copy(
            src_ref=r.hm,
            dst_ref=r.memo.at[s],
            send_sem=r.memo_send.at[s],
            recv_sem=r.memo_recv.at[s],
            device_id=peer,
            device_id_type=MESH,
        )
        copy.start()
        memo.append(copy)
    feed_phase(dims, r, 1, 6, r.y2, r.gy3, r.out, r.grad, 0)
    sum_units(r, bands)
    for copy in memo:
        copy.wait()
    r.finish()


def unit_out(r, j, which):
    slab = r.landed.shape[3]
    if which == 0:
        rows = pl.ds(j * slab, slab)
        places = [(pl.ds(2 * y, 2), r.bags.at[0, y, :, rows]) for y in range(2)]
    else:
        places = [
            (k, r.bags.at[1, j // 2, j % 2, pl.ds(k * slab, slab)])
            for k in range(r.landed.shape[2])
        ]
    return [
        pltpu.make_async_copy(r.landed.at[j, which, part], place, r.core_out.at[j, which, i])
        for i, (part, place) in enumerate(places)
    ]


def sum_units(r, count):
    for j in range(count):
        for which in range(2):
            exchange(r, j, which).wait()
            r.landed[j, which] = r.landed[j, which] + r.tile[j, which, 0]
            for copy in unit_out(r, j, which):
                copy.start()
    for j in range(count):
        for which in range(2):
            for copy in unit_out(r, j, which):
                copy.wait()


RING = 3


def page_place():
    page = lax.axis_index("page")
    core, x, y = lax.rem(page, 2), lax.rem(page // 2, 2), page // 4
    partners = (page + 1 - 2 * core, page + 2 - 4 * x, page + 4 - 8 * y)
    return (core, x, y), [{"page": p} for p in partners]


def remote(src, dst, send, recv, device):
    return pltpu.make_async_remote_copy(
        src_ref=src,
        dst_ref=dst,
        send_sem=send,
        recv_sem=recv,
        device_id=device,
        device_id_type=MESH,
    )


class Loads:
    def __init__(self, sems):
        self.sems, self.used = sems, 0

    def __call__(self, src, dst):
        copy = pltpu.make_async_copy(src, dst, self.sems.at[self.used])
        self.used += 1
        copy.start()
        return copy


class Reducer:
    def __init__(self, dims, r, loads):
        self.dims, self.r, self.loads = dims, r, loads
        (self.core, self.x, self.y), (self.other, self.along_x, self.along_y) = page_place()
        bands = dims["bands"]
        me = lax.axis_index("row")
        self.me = me
        self.next = me + 1 - 2 * lax.rem(me, 2)
        self.far = lax.rem(me + 2, bands)
        self.across = bands - 1 - me
        self.units, self.sent, self.outs, self.stages = 0, {}, {}, {}
        self.total_units = 24
        self.loading = {}


    def unit(self, fill):
        r, u = self.r, self.units
        slot = u % RING
        for copy in self.outs.pop(slot, []):
            copy.wait()
        fill(r.tile.at[slot])
        if u >= RING:
            pl.semaphore_wait(r.core_free, 1)
        self.sent[slot] = self.exchange(slot)
        self.sent[slot].start()
        self.units += 1
        return u

    def exchange(self, slot):
        r = self.r
        return remote(
            r.tile.at[slot, 1],
            r.landed.at[slot],
            r.core_send.at[slot],
            r.core_recv.at[slot],
            self.other,
        )

    def settle(self, u, targets):
        r, slot = self.r, u % RING
        self.sent.pop(slot).wait()
        r.tile[slot, 0] = r.tile[slot, 0] + r.landed[slot]
        if u + RING < self.total_units:
            pl.semaphore_signal(r.core_free, inc=1, device_id=self.other, device_id_type=MESH)
        outs = []
        for i, (part, target) in enumerate(targets):
            copy = pltpu.make_async_copy(r.tile.at[slot, 0, part], target, r.core_out.at[slot, i])
            copy.start()
            outs.append(copy)
        self.outs[slot] = outs

    def slab_targets(self, b, j):
        slab = self.dims["slab"]
        rows = pl.ds(j * slab, slab)
        return [(pl.ds(2 * y, 2), self.bag(b).at[y, :, rows]) for y in range(2)]

    def block_targets(self, b, j):
        slab = self.dims["slab"]
        return [
            (k, self.bag(b).at[j // 2, j % 2, pl.ds(k * slab, slab)])
            for k in range(self.dims["bands"])
        ]

    def flush(self):
        for slot in list(self.outs):
            for copy in self.outs.pop(slot):
                copy.wait()

    def bag(self, b):
        return self.r.query_bags.at[b] if b < 2 else self.r.bags.at[b - 2]


    def start(self, b, stage, parts):
        r, copies = self.r, []
        for i, (src, dst, device) in enumerate(parts):
            at = (b, 2 * stage + i)
            copy = remote(src, dst, r.stage_send.at[at], r.stage_recv.at[at], device)
            copy.start()
            copies.append(copy)
        self.stages[b, stage] = copies

    def halves(self):
        height = self.r.share.shape[0] // 2
        return pl.ds(0, height), pl.ds(height, height)

    def first(self, *bags):
        r = self.r
        top, bottom = self.halves()
        for b in bags:
            bag = self.bag(b)
            self.start(
                b,
                0,
                [
                    (bag.at[:, 1 - self.x, top], r.recv1.at[b, 0], self.along_x),
                    (bag.at[1 - self.y, :, bottom], r.recv1.at[b, 1], self.along_y),
                ],
            )

    def arrived(self, b, stage):
        for copy in self.stages[b, stage]:
            copy.wait()

    def second(self, *bags):
        r = self.r
        top, bottom = self.halves()
        loads = {}
        for b in bags:
            self.arrived(b, 0)
            bag, slot = self.bag(b), b % 2
            loads[b] = [
                self.loads(bag.at[:, self.x, top], r.sums.at[slot, 0]),
                self.loads(bag.at[self.y, :, bottom], r.sums.at[slot, 1]),
                self.loads(r.recv1.at[b], r.came.at[slot]),
            ]
        for b in bags:
            slot = b % 2
            for copy in loads[b]:
                copy.wait()
            r.sums[slot] = r.sums[slot] + r.came[slot]
            self.start(
                b,
                1,
                [
                    (r.sums.at[slot, 0, 1 - self.y], r.recv2.at[b, 0], self.along_y),
                    (r.sums.at[slot, 1, 1 - self.x], r.recv2.at[b, 1], self.along_x),
                ],
            )

    def third(self, *bags):
        r = self.r
        loads = {}
        for b in bags:
            self.arrived(b, 1)
            loads[b] = self.loads(r.recv2.at[b], r.came.at[b % 2, :, 0])
        for b in bags:
            slot = b % 2
            loads[b].wait()
            height = r.share.shape[0] // 2
            r.share[:height] = r.sums[slot, 0, self.y] + r.came[slot, 0, 0]
            r.share[height:] = r.sums[slot, 1, self.x] + r.came[slot, 1, 0]
            self.cut(b)
            self.start(
                b,
                2,
                [
                    (r.pieces.at[slot, self.next], r.recv3.at[b, 0], {"row": self.next}),
                    (r.pieces.at[slot, self.across], r.recv3.at[b, 1], {"row": self.next}),
                ],
            )

    def cut(self, b):
        r, slab, bands = self.r, self.dims["slab"], self.dims["bands"]
        slot = b % 2
        width = r.share.shape[1]
        size = width // bands
        parts = [r.share[k * slab : (k + 1) * slab, :] for k in range(bands)]
        if b in (0, 2):
            made = parts
        elif b in (1, 3):
            made = [
                jnp.concatenate([p[:, z * size : (z + 1) * size] for p in parts], axis=1)
                for z in range(bands)
            ]
        else:
            rest = jnp.concatenate(parts[1:], axis=1)
            made = [
                jnp.concatenate(
                    [
                        parts[0][:, z * size : (z + 1) * size],
                        rest[:, 3 * z * size : 3 * (z + 1) * size],
                    ],
                    axis=1,
                )
                for z in range(bands)
            ]
        for z in range(bands):
            r.pieces[slot, z] = made[z]

    def fourth(self, *bags):
        r = self.r
        loads = {}
        for b in bags:
            self.arrived(b, 2)
            loads[b] = self.loads(r.recv3.at[b], r.came3.at[b % 2])
        for b in bags:
            slot = b % 2
            loads[b].wait()
            r.last[slot, 0] = r.pieces[slot, self.me] + r.came3[slot, 0]
            r.last[slot, 1] = r.pieces[slot, self.far] + r.came3[slot, 1]
            self.start(b, 3, [(r.last.at[slot, 1], r.recv4.at[b], {"row": self.far})])

    def end(self, *bags):
        r = self.r
        loads, outs = {}, []
        for b in bags:
            self.arrived(b, 3)
            loads[b] = self.loads(r.recv4.at[b], r.came4.at[b % 2])
        for b in bags:
            slot = b % 2
            loads[b].wait()
            if ("final", slot) in self.loading:
                self.loading.pop(("final", slot)).wait()
            r.final[slot] = r.last[slot, 0].astype(full) + r.came4[slot].astype(full)
            self.loading["final", slot] = self.loads(r.final.at[slot], r.shares.at[b])

    def finish(self):
        for copy in self.loading.values():
            copy.wait()


def layer_loads(r, loads, layer, arena):
    width = arena.shape[1]
    copies = [
        loads(r.w_qkv.at[layer, :, i * width : (i + 1) * width], arena.at[i]) for i in range(3)
    ]
    return copies + [loads(r.w_out.at[layer], arena.at[3])]


def wait_all(copies):
    for copy in copies:
        copy.wait()


def project_pair_into(kv_ref, into_ref, arena, start, count):
    width = arena.shape[1]
    part = slice(start, start + count)
    kv_ref[part, :width] = dot_nn(into_ref[part, :], arena[1]).astype(bfloat)
    kv_ref[part, width:] = dot_nn(into_ref[part, :], arena[2]).astype(bfloat)


def pair_back(dkv_ref, arena, start, count):
    width = arena.shape[1]
    part = slice(start, start + count)
    return dot_nt(dkv_ref[part, :width], arena[1]) + dot_nt(dkv_ref[part, width:], arena[2])


def scatter_back(r, bands, dkv_ref, arena, count, parts, landing, send, recv):
    me = lax.axis_index("row")
    copies = []
    for s in (2, 1, 3):
        parts[s - 1] = pair_back(dkv_ref, arena, s * count, count).astype(bfloat)
        copy = remote(
            parts.at[s - 1],
            landing.at[s - 1],
            send.at[s - 1],
            recv.at[s - 1],
            {"row": lax.rem(me + bands - s, bands)},
        )
        copy.start()
        copies.append(copy)
    return pair_back(dkv_ref, arena, 0, count), copies


def weight_units(dims, r, red, b, context, low, from_rows, into_rows, dq, dkv):
    width = r.tile.shape[-1]
    sides = [
        lambda: dot_tn(context[...], low[...]),
        lambda: dot_tn(from_rows[...], dq[...]),
        lambda: dot_tn(into_rows[...], dkv[:, :width]),
        lambda: dot_tn(into_rows[...], dkv[:, width:]),
    ]
    units = []
    for j, side in enumerate(sides):
        grad = side().astype(bfloat)
        units.append(red.unit(lambda tile: split_blocks(dims, tile, grad, red.core)))
        if j:
            red.settle(units[j - 1], red.slab_targets(b, j - 1))
    red.settle(units[-1], red.slab_targets(b, 3))


def vec_rows(dims):
    quarters = dims["bands"]
    return 0, 4, 4 + 2 * quarters, 6 + 2 * quarters, 13 + 2 * quarters


def back_kernel(dims, r):
    page_width, bands, rows, tokens = (dims[n] for n in ("page_width", "bands", "rows", "tokens"))
    slab = dims["slab"]
    width = r.f1.shape[1]
    me = lax.axis_index("row")
    loads = Loads(r.load_sems)
    red = Reducer(dims, r, loads)
    greet(band_peers(bands) + [red.other, red.along_x, red.along_y])
    red.first(0, 1)
    row_out, row_up, row_down, row_gain, row_bias = vec_rows(dims)

    weights3 = layer_loads(r, loads, 3, r.att)
    hl_load = loads(r.hl_hbm, r.from_rows)
    memo_load = [
        loads(r.hm_hbm, r.into.at[0:rows]),
        loads(r.memo_hbm, r.into.at[rows : bands * rows]),
    ]
    x1_load = loads(r.x1_hbm, r.f1)
    gx3_load = loads(r.gx3_hbm, r.cot)
    feed_loads = [[feed_copy(r, 0, i, j) for i in range(2)] for j in range(bands)]
    for pair in feed_loads:
        for copy in pair:
            copy.start()
    small = [
        loads(src, dst)
        for src, dst in (
            (r.q2_hbm, r.q2),
            (r.c2_hbm, r.c2),
            (r.log2_hbm, r.log2),
            (r.q1_hbm, r.q1),
            (r.c1_hbm, r.c1),
            (r.log1_hbm, r.log1),
            (r.ha_hbm, r.ha),
            (r.y2_hbm, r.y2),
            (r.y1_hbm, r.y1),
            (r.gy2_hbm, r.gy),
        )
    ]
    r.vec[...] = jnp.zeros_like(r.vec)
    for j in range(bands):
        r.vec[row_up + bands + j : row_up + bands + j + 1, :] = r.up_bias1[
            :, j * width : (j + 1) * width
        ]
    r.vec[row_down + 1 : row_down + 2, :] = r.down_bias1[...]
    r.vec[row_gain + 6 : row_gain + 7, :] = r.gain6[...]
    r.vec[row_bias + 6 : row_bias + 7, :] = r.bias6[...]

    every = slice(None)
    few = slice(0, bands * rows)
    hl_load.wait()
    wait_all(weights3)
    r.q[...] = (dot_nn(r.from_rows[...], r.att[0]) * SCALE).astype(bfloat)
    wait_all(memo_load)
    for s in range(bands):
        project_pair_into(r.kv, r.into, r.att, s * rows, rows)
    bias = read_bias(me, dims, r.scalars)
    r.log[...] = jnp.zeros_like(r.log)
    attend_rows(r.q, r.kv, r.context, r.log, bias, every, few)
    x1_load.wait()
    r.f2[...] = r.f1[...] + (dot_nn(r.context[...], r.att[3]) + r.b_out[3:4, :])

    gx3_load.wait()
    r.low[...] = norm_forward(r.f2[...], r.gain[5:6, :], r.bias[5:6, :])
    r.f3[...] = r.f2[...] + r.b_down[0:1, :]
    r.f4[...] = jnp.zeros_like(r.f4)
    r.vec[row_down : row_down + 1, :] = jnp.sum(r.cot[...].astype(full), axis=0, keepdims=True)
    waiting = []
    for j in range(bands):
        feed_loads[j][0].wait()
        hidden = r.low[...]
        z = dot_nn(hidden, r.up[j]) + r.b_up[0:1, j * width : (j + 1) * width]
        square = z * z
        bend = jnp.tanh(0.7978845608028654 * (z + 0.044715 * (square * z)))
        half = 0.5 * (1.0 + bend)
        slope = half + (0.5 * z) * (1.0 - bend * bend) * (
            0.7978845608028654 * (1.0 + 0.134145 * square)
        )
        active = (z * half).astype(bfloat)
        feed_loads[j][1].wait()
        r.f3[...] += dot_nn(active, r.down[j])
        low_grad = r.cot[...]
        dz = dot_nt(low_grad, r.down[j]) * slope
        r.vec[row_up + j : row_up + j + 1, :] = jnp.sum(dz, axis=0, keepdims=True)
        dz = dz.astype(bfloat)
        r.f4[...] += dot_nt(dz, r.up[j])
        up_grad = dot_tn(hidden, dz).astype(bfloat)
        unit = red.unit(lambda tile: split_blocks(dims, tile, up_grad, red.core))
        waiting.append((unit, red.slab_targets(2, j)))
        down_grad = dot_tn(active, low_grad).astype(bfloat)
        deep = bands * slab

        def fill(tile):
            for side in range(2):
                part = down_grad[side * deep : (side + 1) * deep]
                for k in range(bands):
                    tile[lax.rem(side + red.core, 2), k] = part[k * slab : (k + 1) * slab]

        if len(waiting) > 1:
            red.settle(*waiting.pop(0))
        unit = red.unit(fill)
        waiting.append((unit, red.block_targets(3, j)))
        red.settle(*waiting.pop(0))
        if j == 1:
            red.second(0, 1)
    for item in waiting:
        red.settle(*item)
    red.flush()
    red.first(2, 3)
    weights2 = layer_loads(r, loads, 2, r.up)
    weights1 = layer_loads(r, loads, 1, r.down)
    to_right = {"row": lax.rem(me + 1, bands)}
    moved = dot_tn(r.order[...], r.f3[...].astype(bfloat)).astype(bfloat)
    stay = tokens - SHIFT * page_width
    r.vis_out[tokens - stay :, :] = moved[:stay]
    r.halo_low[...] = moved[stay:]
    halo = remote(
        r.halo_low, r.vis_out.at[: tokens - stay], r.halo_send.at[0], r.halo_recv.at[0], to_right
    )
    halo.start()
    pull, gain5, bias5 = norm_backward(r.f4[...], r.f2[...], r.gain[5:6, :])
    r.vec[row_gain + 5 : row_gain + 6, :] = gain5
    r.vec[row_bias + 5 : row_bias + 6, :] = bias5
    gx2 = r.cot[...].astype(full) + pull
    r.f5[...] = gx2

    low = gx2.astype(bfloat)
    r.low[...] = low
    r.vec[row_out + 3 : row_out + 4, :] = jnp.sum(low.astype(full), axis=0, keepdims=True)
    r.grad[...] = dot_nt(low, r.att[3]).astype(bfloat)
    attend_rows_back(r.q, r.kv, r.context, r.log, r.grad, r.dq, r.dkv, bias, every, few)
    kv_load = loads(r.kv2_hbm, r.kv)
    red.third(0, 1)
    own, memo_sends = scatter_back(
        r, bands, r.dkv, r.att, rows, r.parts_m, r.got_m, r.memo_send, r.memo_recv
    )
    r.own_m[...] = own
    r.f4[...] = dot_nt(r.dq[...], r.att[0])
    weights0 = layer_loads(r, loads, 0, r.att)
    few_dkv, few_into = r.dkv.at[0 : bands * rows], r.into.at[0 : bands * rows]
    weight_units(dims, r, red, 4, r.context, r.low, r.from_rows, few_into, r.dq, few_dkv)
    red.flush()
    red.first(4)
    red.fourth(0, 1)
    red.second(2, 3)
    late = [
        loads(r.hl_all_hbm, r.into),
        loads(r.q0_hbm, r.q),
        loads(r.c0_hbm, r.context),
        loads(r.log0_hbm, r.log),
        loads(r.hv_hbm, r.from_rows),
        loads(r.x1_hbm, r.f1),
        loads(r.x0_hbm, r.cot),
    ]

    wait_all(small)
    wait_all(memo_sends)
    pull, gain4, bias4 = norm_backward(
        r.own_m[...] + sum(r.got_m[s].astype(full) for s in range(bands - 1)),
        r.y2[...],
        r.gain[4:5, :],
    )
    r.vec[row_gain + 4 : row_gain + 5, :] = gain4
    r.vec[row_bias + 4 : row_bias + 5, :] = bias4
    gy = r.gy[...] + pull
    r.gy[...] = gy
    low = gy.astype(bfloat)
    r.low_s[...] = low
    r.vec[row_out + 2 : row_out + 3, :] = jnp.sum(low.astype(full), axis=0, keepdims=True)
    wait_all(weights2)
    r.grad_s[...] = dot_nt(low, r.up[3]).astype(bfloat)
    kv_load.wait()
    attend_rows_back(
        r.q2, r.kv, r.c2, r.log2, r.grad_s, r.dq_s, r.dkv, look_bias(dims, r.scalars), every, every
    )
    kv_load = loads(r.kv1_hbm, r.kv.at[0 : bands * rows])
    own, look_sends = scatter_back(
        r, bands, r.dkv, r.up, tokens, r.parts_l, r.got_l, r.look_send, r.look_recv
    )
    r.f4[...] += own
    pull, gain2, bias2 = norm_backward(dot_nt(r.dq_s[...], r.up[0]), r.y1[...], r.gain[2:3, :])
    r.vec[row_gain + 2 : row_gain + 3, :] = gain2
    r.vec[row_bias + 2 : row_bias + 3, :] = bias2
    r.gy[...] += pull
    red.end(0, 1)
    red.third(2, 3)
    wait_all(late)
    weight_units(dims, r, red, 5, r.c2, r.low_s, r.ha, r.into, r.dq_s, r.dkv)
    hidden_load = loads(r.hs_hbm, r.into.at[0 : bands * rows])
    red.flush()
    red.first(5)
    red.second(4)

    low = r.gy[...].astype(bfloat)
    r.low_s[...] = low
    r.vec[row_out + 1 : row_out + 2, :] = jnp.sum(low.astype(full), axis=0, keepdims=True)
    wait_all(weights1)
    r.grad_s[...] = dot_nt(low, r.down[3]).astype(bfloat)
    kv_load.wait()
    bias = self_bias(me, r.scalars, rows, bands)
    attend_rows_back(r.q1, r.kv, r.c1, r.log1, r.grad_s, r.dq_s, r.dkv, bias, every, few)
    kv_load = loads(r.kv0_hbm, r.kv.at[0:tokens])
    own, self_sends = scatter_back(
        r, bands, r.dkv, r.down, rows, r.parts_m, r.got_s, r.self_send, r.self_recv
    )
    r.own_m[...] = own + dot_nt(r.dq_s[...], r.down[0])
    red.fourth(2, 3)
    hidden_load.wait()
    weight_units(
        dims, r, red, 6, r.c1, r.low_s, r.into.at[0:rows], few_into, r.dq_s, few_dkv
    )
    red.flush()
    red.first(6)
    red.third(4)
    red.second(5)

    wait_all(look_sends)
    pull, gain3, bias3 = norm_backward(
        r.f4[...] + sum(r.got_l[s].astype(full) for s in range(bands - 1)),
        r.f1[...],
        r.gain[3:4, :],
    )
    r.vec[row_gain + 3 : row_gain + 4, :] = gain3
    r.vec[row_bias + 3 : row_bias + 4, :] = bias3
    gx1 = r.f5[...] + pull
    r.f5[...] = gx1
    low = gx1.astype(bfloat)
    r.low[...] = low
    r.vec[row_out : row_out + 1, :] = jnp.sum(low.astype(full), axis=0, keepdims=True)
    wait_all(weights0)
    r.grad[...] = dot_nt(low, r.att[3]).astype(bfloat)
    kv_load.wait()
    size = WIN * WIN
    for w in range(tokens // size):
        part = slice(w * size, (w + 1) * size)
        bias = window_bias(r.scalars, r.region_col, r.region_row, w, page_width)
        attend_rows_back(
            r.q, r.kv, r.context, r.log, r.grad, r.dq, r.dkv, bias, part, part
        )
    dr = pair_back(r.dkv, r.att, 0, tokens) + dot_nt(r.dq[...], r.att[0])
    pull, gain0, bias0 = norm_backward(dr, r.cot[...].astype(full), r.gain[0:1, :])
    r.vec[row_gain : row_gain + 1, :] = gain0
    r.vec[row_bias : row_bias + 1, :] = bias0
    gx0 = r.f5[...] + pull
    high = gx0.astype(bfloat)
    rest = (gx0 - high.astype(full)).astype(bfloat)
    moved = dot_tn(r.order[...], high) + dot_tn(r.order[...], rest)
    r.vis_grad[tokens - stay :, :] = moved[:stay]
    r.f2[: tokens - stay, :] = moved[stay:]
    halo_back = remote(
        r.f2.at[: tokens - stay], r.vis_grad.at[: tokens - stay], r.halo_send.at[1], r.halo_recv.at[1], to_right
    )
    halo_back.start()
    weight_units(
        dims, r, red, 7, r.context, r.low, r.from_rows, r.from_rows, r.dq, r.dkv.at[0:tokens]
    )
    red.flush()
    red.first(7)
    red.end(2, 3)
    red.fourth(4)
    red.third(5)
    red.second(6)

    wait_all(self_sends)
    pull, gain1, bias1 = norm_backward(
        r.own_m[...] + sum(r.got_s[s].astype(full) for s in range(bands - 1)),
        r.y0[...].astype(full),
        r.gain[1:2, :],
    )
    r.query_grad[...] = r.gy[...] + pull
    r.vec[row_gain + 1 : row_gain + 2, :] = gain1
    r.vec[row_bias + 1 : row_bias + 2, :] = bias1

    def swap(i, device):
        copy = remote(r.vec, r.vec_in.at[i], r.vec_send.at[i], r.vec_recv.at[i], device)
        copy.start()
        copy.wait()
        r.vec[...] = r.vec[...] + r.vec_in[i]

    swap(0, red.other)
    red.end(4)
    red.fourth(5)
    swap(1, red.along_x)
    red.second(7)
    swap(2, red.along_y)
    red.third(6)
    swap(3, {"row": red.next})
    red.end(5)
    red.third(7)
    red.fourth(6)
    swap(4, {"row": red.far})
    red.fourth(7)
    red.end(6)
    r.vec_out[...] = r.vec[...]
    red.end(7)
    halo.wait()
    halo_back.wait()
    red.finish()


def shards(
    vis_stream,
    query_stream,
    w_qkv,
    w_out,
    b_out,
    w_up,
    b_up,
    w_down,
    b_down,
    norm_gain,
    norm_bias,
    page_cols,
    query_len,
    prompt_len,
    region_ids,
    vis_cotangent,
    query_cotangent,
):
    band_rows, page_width, width = vis_stream.shape[1:]
    tokens = band_rows * page_width
    rows = query_stream.shape[1]
    bands, pages = lax.axis_size("row"), lax.axis_size("page")
    me = lax.axis_index("row")
    hidden_units = w_up.shape[2]
    slab = width // pages
    dims = dict(
        page_width=page_width,
        bands=bands,
        tokens=tokens,
        rows=rows,
        pages=pages,
        slab=slab,
    )
    scalars = jnp.stack([me, page_cols[0], query_len[0], prompt_len[0]]).astype(jnp.int32)
    scalar = (scalars, SMEM)
    qkv_any, out_any = (w_qkv, ANY), (w_out, ANY)
    log_lanes = full_shape(tokens, PAIR)
    y0, gy3 = query_stream[0], query_cotangent[0]
    across = page_width // WIN
    region = region_ids[0].reshape(band_rows // WIN, WIN, across, WIN)
    region = jnp.swapaxes(region, 1, 2).reshape(-1, WIN * WIN)
    region_col, region_row = region[:, :, None], region[:, None, :]
    order = jnp.asarray(source_order(page_width, band_rows), bfloat)

    given = dict(
        scalars=scalar,
        vis=(vis_stream, VMEM),
        cot=(vis_cotangent, VMEM),
        y0=(y0, VMEM),
        order=(order, VMEM),
        region_col=(region_col, VMEM),
        region_row=(region_row, VMEM),
        gain=(norm_gain, VMEM),
        bias=(norm_bias, VMEM),
        b_out=(b_out, VMEM),
        w_qkv=qkv_any,
        w_out=out_any,
    )
    weight = {}
    for a in range(3):
        weight["wqkv%d" % a] = pltpu.VMEM((width, 3 * width), bfloat)
        weight["wout%d" % a] = pltpu.VMEM((width, width), bfloat)
    pair_sems = pltpu.SemaphoreType.DMA((2,))
    peer_sems = pltpu.SemaphoreType.DMA((bands - 1,))
    front = launch(
        partial(front_kernel, dims),
        given,
        {},
        {},
        dict(
            x0=low_shape(tokens, width),
            hv=low_shape(tokens, width),
            q0=low_shape(tokens, width),
            kv0=low_shape(tokens, 2 * width),
            c0=low_shape(tokens, width),
            log0=log_lanes,
            x1=full_shape(tokens, width),
            gx3=low_shape(tokens, width),
            hs=low_shape(bands, rows, width),
            q1=low_shape(rows, width),
            kv1=low_shape(bands * rows, 2 * width),
            c1=low_shape(rows, width),
            log1=full_shape(rows, PAIR),
            y1=full_shape(rows, width),
            ha=low_shape(rows, width),
            q2=low_shape(rows, width),
            hl=low_shape(bands, tokens, width),
            kv2=low_shape(bands * tokens, 2 * width),
            c2=low_shape(rows, width),
            log2=full_shape(rows, PAIR),
            y2=full_shape(rows, width),
            hm=low_shape(rows, width),
        ),
        dict(
            cells=pltpu.VMEM((tokens, width), full),
            halo=pltpu.VMEM((2, SHIFT, page_width, width), bfloat),
            halo_send=pair_sems,
            halo_recv=pair_sems,
            self_send=peer_sems,
            self_recv=peer_sems,
            look_send=peer_sems,
            look_recv=peer_sems,
            weight_sems=pltpu.SemaphoreType.DMA((6,)),
            **weight,
        ),
        0,
        40 * tokens * width * width,
    )
    bag_shape = (2, 2, 2, bands * slab, width)
    quarter_sems = pltpu.SemaphoreType.DMA((bands, 2))
    feed = launch(
        partial(query_feed_kernel, dims),
        dict(
            y2=(front["y2"], VMEM),
            gy3=(gy3, VMEM),
            hm=(front["hm"], VMEM),
            gain=(norm_gain, VMEM),
            bias=(norm_bias, VMEM),
            b_up=(b_up, VMEM),
            b_down=(b_down, VMEM),
            w_up=(w_up, ANY),
            w_down=(w_down, ANY),
        ),
        {},
        dict(
            out=(low_shape(rows, width), VMEM),
            grad=(full_shape(rows, width), VMEM),
            memo=(low_shape(bands - 1, rows, width), VMEM),
            up_bias=(full_shape(1, hidden_units), VMEM),
            down_bias=(full_shape(1, width), VMEM),
            gain_grad=(full_shape(1, width), VMEM),
            bias_grad=(full_shape(1, width), VMEM),
            bags=(low_shape(*bag_shape), ANY),
        ),
        {},
        dict(
            hidden=pltpu.VMEM((rows, width), bfloat),
            total=pltpu.VMEM((rows, width), full),
            back=pltpu.VMEM((rows, width), full),
            up=pltpu.VMEM((bands, width, width), bfloat),
            down=pltpu.VMEM((bands, width, width), bfloat),
            tile=pltpu.VMEM((bands, 2, 2, pages // 2, slab, width), bfloat),
            landed=pltpu.VMEM((bands, 2, pages // 2, slab, width), bfloat),
            weight_sems=pltpu.SemaphoreType.DMA((2, bands)),
            core_send=quarter_sems,
            core_recv=quarter_sems,
            core_out=pltpu.SemaphoreType.DMA((bands, 2, bands)),
            memo_send=peer_sems,
            memo_recv=peer_sems,
        ),
        1,
        12 * rows * width * hidden_units,
    )
    hbm = {
        "x1_hbm": front["x1"],
        "x0_hbm": front["x0"],
        "gx3_hbm": front["gx3"],
        "hv_hbm": front["hv"],
        "hl_hbm": front["hl"][0],
        "hl_all_hbm": front["hl"].reshape(bands * tokens, width),
        "hs_hbm": front["hs"].reshape(bands * rows, width),
        "ha_hbm": front["ha"],
        "hm_hbm": front["hm"],
        "memo_hbm": feed["memo"].reshape((bands - 1) * rows, width),
        "y1_hbm": front["y1"],
        "y2_hbm": front["y2"],
        "gy2_hbm": feed["grad"],
        "query_bags": feed["bags"],
        "w_qkv": w_qkv,
        "w_out": w_out,
        "w_up": w_up,
        "w_down": w_down,
    }
    for a in range(3):
        for name in ("q", "kv", "c", "log"):
            hbm["%s%d_hbm" % (name, a)] = front["%s%d" % (name, a)]
    near = dict(
        y0=y0,
        order=order,
        region_col=region_col,
        region_row=region_row,
        gain=norm_gain,
        bias=norm_bias,
        b_out=b_out,
        b_up=b_up,
        b_down=b_down,
        up_bias1=feed["up_bias"],
        down_bias1=feed["down_bias"],
        gain6=feed["gain_grad"],
        bias6=feed["bias_grad"],
    )
    height = bands * slab
    halo_rows = SHIFT * page_width
    vec_shape = full_shape(vec_rows(dims)[-1] + 11, width)
    wide = lambda count: pltpu.VMEM((count, width), full)
    narrow = lambda count: pltpu.VMEM((count, width), bfloat)
    dma = pltpu.SemaphoreType.DMA
    scratch = dict(
        att=pltpu.VMEM((4, width, width), bfloat),
        up=pltpu.VMEM((bands, width, width), bfloat),
        down=pltpu.VMEM((bands, width, width), bfloat),
        tile=pltpu.VMEM((RING, 2, pages // 2, slab, width), bfloat),
        landed=pltpu.VMEM((RING, pages // 2, slab, width), bfloat),
        sums=pltpu.VMEM((2, 2, 2, height // 2, width), bfloat),
        came=pltpu.VMEM((2, 2, 2, height // 2, width), bfloat),
        share=narrow(height),
        pieces=pltpu.VMEM((2, bands, slab, width), bfloat),
        last=pltpu.VMEM((2, 2, slab, width), bfloat),
        came3=pltpu.VMEM((2, 2, slab, width), bfloat),
        came4=pltpu.VMEM((2, slab, width), bfloat),
        final=pltpu.VMEM((2, slab, width), full),
        q=narrow(tokens),
        kv=pltpu.VMEM((bands * tokens, 2 * width), bfloat),
        context=narrow(tokens),
        log=pltpu.VMEM((tokens, PAIR), full),
        grad=narrow(tokens),
        dq=narrow(tokens),
        dkv=pltpu.VMEM((bands * tokens, 2 * width), bfloat),
        low=narrow(tokens),
        cot=narrow(tokens),
        from_rows=narrow(tokens),
        into=narrow(bands * tokens),
        f1=wide(tokens),
        f2=wide(tokens),
        f3=wide(tokens),
        f4=wide(tokens),
        f5=wide(tokens),
        q2=narrow(rows),
        c2=narrow(rows),
        q1=narrow(rows),
        c1=narrow(rows),
        log2=pltpu.VMEM((rows, PAIR), full),
        log1=pltpu.VMEM((rows, PAIR), full),
        ha=narrow(rows),
        low_s=narrow(rows),
        grad_s=narrow(rows),
        dq_s=narrow(rows),
        y1=wide(rows),
        y2=wide(rows),
        gy=wide(rows),
        own_m=wide(rows),
        parts_m=pltpu.VMEM((bands - 1, rows, width), bfloat),
        parts_l=pltpu.VMEM((bands - 1, tokens, width), bfloat),
        got_m=pltpu.VMEM((bands - 1, rows, width), bfloat),
        got_l=pltpu.VMEM((bands - 1, tokens, width), bfloat),
        got_s=pltpu.VMEM((bands - 1, rows, width), bfloat),
        halo_low=narrow(halo_rows),
        vec=pltpu.VMEM(vec_shape.shape, full),
        vec_in=pltpu.VMEM((5,) + vec_shape.shape, full),
        load_sems=dma((128,)),
        weight_sems=dma((2, bands)),
        core_send=dma((RING,)),
        core_recv=dma((RING,)),
        core_out=dma((RING, bands)),
        core_free=pltpu.SemaphoreType.REGULAR,
        stage_send=dma((8, 8)),
        stage_recv=dma((8, 8)),
        halo_send=pair_sems,
        halo_recv=pair_sems,
        memo_send=peer_sems,
        memo_recv=peer_sems,
        look_send=peer_sems,
        look_recv=peer_sems,
        self_send=peer_sems,
        self_recv=peer_sems,
        vec_send=dma((5,)),
        vec_recv=dma((5,)),
    )
    result = launch(
        partial(back_kernel, dims),
        dict(scalars=scalar)
        | {n: (v, VMEM) for n, v in near.items()}
        | {n: (v, ANY) for n, v in hbm.items()},
        {},
        dict(
            vis_out=(low_shape(tokens, width), VMEM),
            vis_grad=(full_shape(tokens, width), VMEM),
            query_grad=(full_shape(rows, width), VMEM),
            vec_out=(vec_shape, VMEM),
            shares=(full_shape(8, slab, width), ANY),
            bags=(low_shape(6, 2, 2, height, width), ANY),
            recv1=(low_shape(8, 2, 2, height // 2, width), ANY),
            recv2=(low_shape(8, 2, height // 2, width), ANY),
            recv3=(low_shape(8, 2, slab, width), ANY),
            recv4=(low_shape(8, slab, width), ANY),
        ),
        {},
        scratch,
        2,
        100 * tokens * width * width,
    )

    shares, vec = result["shares"], result["vec_out"]
    column = width // bands
    attention = shares[7:3:-1]
    down = shares[3::-2].reshape(2, slab, bands, column).swapaxes(1, 2)
    page = lax.axis_index("page")
    row_out, row_up, row_down, row_gain, row_bias = vec_rows(dims)
    own = lax.dynamic_slice_in_dim(vec, page * slab, slab, 1)
    hidden = hidden_units // pages
    up_bias = lax.dynamic_slice_in_dim(
        vec[row_up:row_down].reshape(2, hidden_units), page * hidden, hidden, 1
    )
    grid_shape = (1, band_rows, page_width, width)
    return (
        result["vis_out"].reshape(grid_shape),
        feed["out"][None],
        result["vis_grad"].reshape(grid_shape),
        result["query_grad"][None],
        attention[:, :, column:],
        attention[:, :, :column],
        own[row_out:row_up],
        shares[2::-2],
        up_bias,
        down.reshape(2, bands * slab, column),
        own[row_down:row_gain],
        own[row_gain:row_bias],
        own[row_bias : row_bias + 7],
    )


def plain_ring(count, distance):
    return [(i, (i + distance) % count) for i in range(count)]


def plain_flipped(count, bit):
    return [(i, i ^ bit) for i in range(count)]


def plain_mat_dot(left, right):
    return jnp.dot(left, right, preferred_element_type=jnp.float32)


def plain_mat_left(left, right):
    return lax.dot_general(
        left, right, (((0,), (0,)), ((), ())), preferred_element_type=jnp.float32
    )


def plain_mat_right(left, right):
    return lax.dot_general(
        left, right, (((1,), (1,)), ((), ())), preferred_element_type=jnp.float32
    )


def plain_norm_forward(values, gain_row, bias_row):
    average = jnp.mean(values, axis=-1, keepdims=True)
    centred = values - average
    spread = jnp.mean(centred * centred, axis=-1, keepdims=True)
    inverse = lax.rsqrt(spread + norm_eps)
    normal = centred * inverse
    return ((normal * gain_row + bias_row).astype(bfloat), normal, inverse)


def plain_norm_backward(grad_result, normal, inverse, gain_row):
    grad_normal = grad_result * gain_row
    first_mean = jnp.mean(grad_normal, axis=-1, keepdims=True)
    second_mean = jnp.mean(grad_normal * normal, axis=-1, keepdims=True)
    grad_input = inverse * (grad_normal - first_mean - normal * second_mean)
    return (grad_input, jnp.sum(grad_result * normal, axis=0), jnp.sum(grad_result, axis=0))


def plain_to_windows(grid_cells):
    row_count, col_count = (grid_cells.shape[0], grid_cells.shape[1])
    trailing = grid_cells.shape[2:]
    carved = grid_cells.reshape((row_count // WIN, WIN, col_count // WIN, WIN) + trailing)
    return jnp.swapaxes(carved, 1, 2).reshape((-1, WIN * WIN) + trailing)


def plain_from_windows(blocks, row_count, col_count):
    trailing = blocks.shape[2:]
    carved = blocks.reshape((row_count // WIN, col_count // WIN, WIN, WIN) + trailing)
    return jnp.swapaxes(carved, 1, 2).reshape((row_count, col_count) + trailing)


def plain_to_shifted(grid_cells):
    count = lax.axis_size("row")
    arriving = lax.ppermute(grid_cells[:SHIFT], "row", plain_ring(count, -1))
    rolled = jnp.concatenate([grid_cells[SHIFT:], arriving], axis=0)
    return plain_to_windows(jnp.roll(rolled, -SHIFT, axis=1)).reshape(-1, grid_cells.shape[2])


def plain_from_shifted(tokens, row_count, col_count):
    count = lax.axis_size("row")
    cells = plain_from_windows(tokens.reshape(-1, WIN * WIN, tokens.shape[1]), row_count, col_count)
    rolled = jnp.roll(cells, SHIFT, axis=1)
    arriving = lax.ppermute(rolled[row_count - SHIFT :], "row", plain_ring(count, 1))
    return jnp.concatenate([arriving, rolled[: row_count - SHIFT]], axis=0)


def plain_gather_row(values):
    count = lax.axis_size("row")
    parts = [values] + [lax.ppermute(values, "row", plain_ring(count, s)) for s in range(1, count)]
    return jnp.concatenate(parts, axis=0)


def plain_scatter_row(partial_sums):
    count = lax.axis_size("row")
    parts = jnp.split(partial_sums.astype(bfloat), count, axis=0)
    total = jnp.split(partial_sums, count, axis=0)[0]
    for s in range(1, count):
        total = total + lax.ppermute(parts[s], "row", plain_ring(count, -s)).astype(jnp.float32)
    return total


def plain_halve(blocks, bit, slot):
    count = lax.axis_size("page")
    mine = (lax.axis_index("page") // bit) % 2
    kept = lax.dynamic_index_in_dim(blocks, mine, slot, keepdims=False)
    sent = lax.dynamic_index_in_dim(blocks, 1 - mine, slot, keepdims=False)
    return kept + lax.ppermute(sent, "page", plain_flipped(count, bit))


def plain_reduce_matrix(grad):
    pages = lax.axis_size("page")
    rows = lax.axis_size("row")
    bits = []
    while 2 ** len(bits) < pages:
        bits.append(2 ** len(bits))
    height, width = grad.shape
    blocks = grad.astype(bfloat).reshape((2,) * len(bits) + (height // pages, width))
    if bits:
        blocks = plain_halve(blocks, 1, len(bits) - 1)
    left, right = jnp.split(blocks, 2, axis=-1)
    rest = bits[1:]
    for bit in rest:
        left = plain_halve(left, bit, left.ndim - 3)
    for bit in reversed(rest):
        right = plain_halve(right, bit, 0)
    share = jnp.concatenate([left, right], axis=-1)
    me = lax.axis_index("row")
    pieces = share.reshape(share.shape[0], rows, width // rows)
    total = lax.dynamic_index_in_dim(pieces, me, 1, keepdims=False).astype(jnp.float32)
    for s in range(1, rows):
        sent = lax.dynamic_index_in_dim(pieces, (me + s) % rows, 1, keepdims=False)
        total = total + lax.ppermute(sent, "row", plain_ring(rows, s)).astype(jnp.float32)
    return total


def plain_reduce_vectors(stack):
    pages = lax.axis_size("page")
    rows = lax.axis_size("row")
    bit = 1
    while bit < pages:
        stack = stack.reshape(-1, 2, stack.shape[-1])
        stack = plain_halve(stack, bit, 1)
        bit *= 2
    vector = stack.reshape(-1)
    total = vector
    for s in range(1, rows):
        total = total + lax.ppermute(vector, "row", plain_ring(rows, s))
    return total


def plain_split_heads(values):
    return values.reshape(values.shape[0], values.shape[1], -1, HDIM)


def plain_masked_scores(queries, key_rows, allowed):
    scores = jnp.einsum(
        "gqhd,gkhd->ghqk",
        plain_split_heads(queries),
        plain_split_heads(key_rows),
        preferred_element_type=jnp.float32,
    ) * HDIM ** (-0.5)
    return jnp.where(allowed[:, None], scores, masked_score)


def plain_attend_forward(queries, key_rows, value_rows, allowed):
    scores = plain_masked_scores(queries, key_rows, allowed)
    row_max = jnp.max(scores, axis=-1, keepdims=True)
    raised = jnp.exp(scores - row_max)
    row_total = jnp.sum(raised, axis=-1, keepdims=True)
    probs_low = (raised / row_total).astype(bfloat)
    context = jnp.einsum(
        "ghqk,gkhd->gqhd", probs_low, plain_split_heads(value_rows), preferred_element_type=jnp.float32
    )
    return (context.reshape(queries.shape).astype(bfloat), row_max + jnp.log(row_total))


def plain_attend_backward(queries, key_rows, value_rows, allowed, log_total, grad_context):
    probs = jnp.exp(plain_masked_scores(queries, key_rows, allowed) - log_total)
    probs_low = probs.astype(bfloat)
    grad_heads = plain_split_heads(grad_context)
    grad_values = jnp.einsum(
        "ghqk,gqhd->gkhd", probs_low, grad_heads, preferred_element_type=jnp.float32
    )
    grad_probs = jnp.einsum(
        "gqhd,gkhd->ghqk", grad_heads, plain_split_heads(value_rows), preferred_element_type=jnp.float32
    )
    row_delta = jnp.sum(probs * grad_probs, axis=-1, keepdims=True)
    grad_scores = (probs * (grad_probs - row_delta)).astype(bfloat)
    grad_queries = jnp.einsum(
        "ghqk,gkhd->gqhd", grad_scores, plain_split_heads(key_rows), preferred_element_type=jnp.float32
    ) * HDIM ** (-0.5)
    grad_keys = jnp.einsum(
        "ghqk,gqhd->gkhd", grad_scores, plain_split_heads(queries), preferred_element_type=jnp.float32
    ) * HDIM ** (-0.5)
    return (
        grad_queries.reshape(queries.shape).astype(bfloat),
        grad_keys.reshape(key_rows.shape).astype(bfloat),
        grad_values.reshape(value_rows.shape).astype(bfloat),
    )


def plain_project(from_rows, to_rows, weight):
    width = weight.shape[0]
    queries = plain_mat_dot(from_rows, weight[:, :width]).astype(bfloat)
    paired = plain_mat_dot(to_rows, weight[:, width:]).astype(bfloat)
    return (queries, paired[:, :width], paired[:, width:])


def plain_project_back(from_rows, to_rows, weight, dq, dk, dv):
    width = weight.shape[0]
    pair = jnp.concatenate([dk, dv], axis=1)
    weight_grad = jnp.concatenate([plain_mat_left(from_rows, dq), plain_mat_left(to_rows, pair)], axis=1)
    return (weight_grad, plain_mat_right(dq, weight[:, :width]), plain_mat_right(pair, weight[:, width:]))


def plain_output_back(context_low, weight, grad_residual):
    grad_low = grad_residual.astype(bfloat)
    return (
        plain_mat_left(context_low, grad_low),
        jnp.sum(grad_low, axis=0, dtype=jnp.float32),
        plain_mat_right(grad_low, weight).astype(bfloat),
    )


def plain_feed_forward(values, gain_row, bias_row, up_weight, up_bias, down_weight, down_bias):
    hidden, normal, inverse = plain_norm_forward(values, gain_row, bias_row)
    upward = plain_mat_dot(hidden, up_weight) + up_bias
    active = jax.nn.gelu(upward, approximate=True).astype(bfloat)
    return (
        values + (plain_mat_dot(active, down_weight) + down_bias),
        (hidden, normal, inverse, upward, active),
    )


def plain_feed_backward(grad_residual, kept_values, gain_row, up_weight, down_weight):
    hidden, normal, inverse, upward, active = kept_values
    grad_low = grad_residual.astype(bfloat)
    grad_down = plain_mat_left(active, grad_low)
    grad_down_bias = jnp.sum(grad_low, axis=0, dtype=jnp.float32)
    grad_active = plain_mat_right(grad_low, down_weight)
    gelu_pull = jax.vjp(partial(jax.nn.gelu, approximate=True), upward)[1]
    grad_up_low = gelu_pull(grad_active)[0].astype(bfloat)
    grad_up = plain_mat_left(hidden, grad_up_low)
    grad_up_bias = jnp.sum(grad_up_low, axis=0, dtype=jnp.float32)
    grad_input, gain_grad, bias_grad = plain_norm_backward(
        plain_mat_right(grad_up_low, up_weight), normal, inverse, gain_row
    )
    return (
        grad_residual + grad_input,
        (grad_up, grad_up_bias, grad_down, grad_down_bias, gain_grad, bias_grad),
    )


def plain_shards(
    vis_stream,
    query_stream,
    w_qkv,
    w_out,
    b_out,
    w_up,
    b_up,
    w_down,
    b_down,
    norm_gain,
    norm_bias,
    page_cols,
    query_len,
    prompt_len,
    region_ids,
    vis_cotangent,
    query_cotangent,
):
    band_rows, page_width, width = vis_stream.shape[1:]
    tokens = band_rows * page_width
    query_rows = query_stream.shape[1]
    bands = lax.axis_size("row")
    me = lax.axis_index("row")
    pages = lax.axis_size("page")
    x0 = plain_to_shifted(vis_stream[0]).astype(jnp.float32)
    gx3 = plain_to_shifted(vis_cotangent[0]).astype(jnp.float32)
    y0 = query_stream[0].astype(jnp.float32)
    gy3 = query_cotangent[0].astype(jnp.float32)
    col_limit, query_limit, prompt_limit = page_cols[0], query_len[0], prompt_len[0]

    own_positions = me * query_rows + jnp.arange(query_rows)
    all_positions = jnp.concatenate(
        [((me - s) % bands) * query_rows + jnp.arange(query_rows) for s in range(bands)]
    )
    key_live = all_positions < query_limit
    self_allowed = key_live[None, :] & (
        (all_positions[None, :] <= own_positions[:, None]) | (all_positions[None, :] < prompt_limit)
    )
    rolled_live = (jnp.arange(page_width) + SHIFT) % page_width < col_limit
    live_tiles = plain_to_windows(jnp.broadcast_to(rolled_live[None, :], (band_rows, page_width)))
    visual_allowed = jnp.broadcast_to(
        jnp.tile(live_tiles.reshape(-1), bands)[None, :], (query_rows, bands * tokens)
    )
    query_allowed = jnp.broadcast_to(key_live[None, :], (tokens, query_rows * bands))
    region_tiles = plain_to_windows(region_ids[0])
    diagonal = jnp.eye(WIN * WIN, dtype=jnp.bool_)
    window_allowed = (region_tiles[:, :, None] == region_tiles[:, None, :]) & (
        live_tiles[:, None, :] | diagonal[None]
    )
    tile_shape = (tokens // (WIN * WIN), WIN * WIN, width)

    hs, n1, i1 = plain_norm_forward(y0, norm_gain[1], norm_bias[1])
    hs_all = plain_gather_row(hs)
    hv, n0, i0 = plain_norm_forward(x0, norm_gain[0], norm_bias[0])
    qw, kw, vw = (v.reshape(tile_shape) for v in plain_project(hv, hv, w_qkv[0]))
    cw, lw = plain_attend_forward(qw, kw, vw, window_allowed)
    cw = cw.reshape(tokens, width)
    x1 = x0 + (plain_mat_dot(cw, w_out[0]) + b_out[0])
    hl, n3, i3 = plain_norm_forward(x1, norm_gain[3], norm_bias[3])
    hl_all = plain_gather_row(hl)

    qs, ks, vs = plain_project(hs, hs_all, w_qkv[1])
    cs, ls = plain_attend_forward(qs[None], ks[None], vs[None], self_allowed[None])
    cs = cs[0]
    y1 = y0 + (plain_mat_dot(cs, w_out[1]) + b_out[1])
    ha, n2, i2 = plain_norm_forward(y1, norm_gain[2], norm_bias[2])
    qa, kl, vl = plain_project(ha, hl_all, w_qkv[2])
    ca, la = plain_attend_forward(qa[None], kl[None], vl[None], visual_allowed[None])
    ca = ca[0]
    y2 = y1 + (plain_mat_dot(ca, w_out[2]) + b_out[2])
    hm, n4, i4 = plain_norm_forward(y2, norm_gain[4], norm_bias[4])
    hm_all = plain_gather_row(hm)
    y3, kept_query = plain_feed_forward(
        y2, norm_gain[6], norm_bias[6], w_up[1], b_up[1], w_down[1], b_down[1]
    )
    gy2, feed_query = plain_feed_backward(gy3, kept_query, norm_gain[6], w_up[1], w_down[1])
    final_up1 = plain_reduce_matrix(feed_query[0])
    final_down1 = plain_reduce_matrix(feed_query[2])

    qr, km, vm = plain_project(hl, hm_all, w_qkv[3])
    cr, lr = plain_attend_forward(qr[None], km[None], vm[None], query_allowed[None])
    cr = cr[0]
    x2 = x1 + (plain_mat_dot(cr, w_out[3]) + b_out[3])
    x3, kept_vis = plain_feed_forward(
        x2, norm_gain[5], norm_bias[5], w_up[0], b_up[0], w_down[0], b_down[0]
    )
    gx2, feed_vis = plain_feed_backward(gx3, kept_vis, norm_gain[5], w_up[0], w_down[0])
    final_up0 = plain_reduce_matrix(feed_vis[0])
    final_down0 = plain_reduce_matrix(feed_vis[2])

    wout3, bout3, dcr = plain_output_back(cr, w_out[3], gx2)
    dqr, dkm, dvm = plain_attend_backward(
        qr[None], km[None], vm[None], query_allowed[None], lr, dcr[None]
    )
    qkv3, dhl, dhm = plain_project_back(hl, hm_all, w_qkv[3], dqr[0], dkm[0], dvm[0])
    gy_memo, gain4, bias4 = plain_norm_backward(plain_scatter_row(dhm), n4, i4, norm_gain[4])
    gy2 = gy2 + gy_memo
    final_out3 = plain_reduce_matrix(wout3)
    final_qkv3 = plain_reduce_matrix(qkv3)

    wout2, bout2, dca = plain_output_back(ca, w_out[2], gy2)
    dqa, dkl, dvl = plain_attend_backward(
        qa[None], kl[None], vl[None], visual_allowed[None], la, dca[None]
    )
    qkv2, dha, dhl_all = plain_project_back(ha, hl_all, w_qkv[2], dqa[0], dkl[0], dvl[0])
    gy_ask, gain2, bias2 = plain_norm_backward(dha, n2, i2, norm_gain[2])
    gy1 = gy2 + gy_ask
    gx_look, gain3, bias3 = plain_norm_backward(dhl + plain_scatter_row(dhl_all), n3, i3, norm_gain[3])
    gx1 = gx2 + gx_look
    final_out2 = plain_reduce_matrix(wout2)
    final_qkv2 = plain_reduce_matrix(qkv2)

    wout1, bout1, dcs = plain_output_back(cs, w_out[1], gy1)
    dqs, dks, dvs = plain_attend_backward(qs[None], ks[None], vs[None], self_allowed[None], ls, dcs[None])
    qkv1, dhs, dhs_all = plain_project_back(hs, hs_all, w_qkv[1], dqs[0], dks[0], dvs[0])
    gy_self, gain1, bias1 = plain_norm_backward(dhs + plain_scatter_row(dhs_all), n1, i1, norm_gain[1])
    gy0 = gy1 + gy_self
    final_out1 = plain_reduce_matrix(wout1)
    final_qkv1 = plain_reduce_matrix(qkv1)

    wout0, bout0, dcw = plain_output_back(cw, w_out[0], gx1)
    dqw, dkw, dvw = plain_attend_backward(qw, kw, vw, window_allowed, lw, dcw.reshape(tile_shape))
    dqw, dkw, dvw = (v.reshape(tokens, width) for v in (dqw, dkw, dvw))
    qkv0, dr_from, dr_into = plain_project_back(hv, hv, w_qkv[0], dqw, dkw, dvw)
    gx_win, gain0, bias0 = plain_norm_backward(dr_from + dr_into, n0, i0, norm_gain[0])
    gx0 = gx1 + gx_win
    final_out0 = plain_reduce_matrix(wout0)
    final_qkv0 = plain_reduce_matrix(qkv0)

    vectors = [
        jnp.stack([bout0, bout1, bout2, bout3]),
        jnp.stack([feed_vis[1], feed_query[1]]),
        jnp.stack([feed_vis[3], feed_query[3]]),
        jnp.stack([gain0, gain1, gain2, gain3, gain4, feed_vis[4], feed_query[4]]),
        jnp.stack([bias0, bias1, bias2, bias3, bias4, feed_vis[5], feed_query[5]]),
    ]
    blocks = [
        jnp.swapaxes(v.reshape(v.shape[0], pages, -1), 0, 1).reshape(pages, -1) for v in vectors
    ]
    reduced = plain_reduce_vectors(jnp.concatenate(blocks, axis=1))
    finals, start = [], 0
    for v in vectors:
        size = v.size // pages
        finals.append(reduced[start : start + size].reshape(v.shape[0], -1))
        start += size

    return (
        plain_from_shifted(x3.astype(bfloat), band_rows, page_width)[None],
        y3[None].astype(bfloat),
        plain_from_shifted(gx0, band_rows, page_width)[None],
        gy0[None],
        jnp.stack([final_qkv0, final_qkv1, final_qkv2, final_qkv3]),
        jnp.stack([final_out0, final_out1, final_out2, final_out3]),
        finals[0],
        jnp.stack([final_up0, final_up1]),
        finals[1],
        jnp.stack([final_down0, final_down1]),
        finals[2],
        finals[3],
        finals[4],
    )


def solution(mesh):
    planned = mesh.shape["page"] == 8 and mesh.shape["row"] == 4
    return jax.shard_map(
        shards if planned else plain_shards,
        mesh=mesh,
        in_specs=(
            P("page", "row", None, None),
            P("page", "row", None),
            P(),
            P(),
            P(),
            P(),
            P(),
            P(),
            P(),
            P(),
            P(),
            P("page"),
            P("page"),
            P("page"),
            P("page", "row", None),
            P("page", "row", None, None),
            P("page", "row", None),
        ),
        out_specs=(
            P("page", "row", None, None),
            P("page", "row", None),
            P("page", "row", None, None),
            P("page", "row", None),
            P(None, "page", "row"),
            P(None, "page", "row"),
            P(None, "page"),
            P(None, "page", "row"),
            P(None, "page"),
            P(None, "page", "row"),
            P(None, "page"),
            P(None, "page"),
            P(None, "page"),
        ),
        check_vma=False,
    )
```

time: 835 us -> 409 us (0.49)
  Pallas kernels: 0 us -> 377 us
  matrix products: 193 us -> 0 us
  waiting for transfers between devices: 181 us -> 0 us
  local copies, waits for them, and re-layouts: 192 us -> 21.8 us
  starting transfers between devices: 148 us -> 0 us
  other arithmetic: 99.9 us -> 1.3 us
    pallas_call x0 -> x3, Pallas kernels: none -> 377 us  [launch(): pl.pallas_call(inner, out_shape=[made[n][0] for n in made] + [kept[n] for...]
    dot_general x72 -> x0, matrix products: 193 us -> none  [the longest x16 53.1 us: mat_right(): lax.dot_general(left, right, (((1,), (1,)), ((), ())), preferred_element_...]
    ppermute x124 -> x0, waiting for transfers between devices: 181 us -> none  [the longest x63 99 us: halve(): return kept + lax.ppermute(sent, 'page', flipped(count, bit))]
    ppermute x124 -> x0, starting transfers between devices: 148 us -> none  [the longest x63 57.9 us: halve(): return kept + lax.ppermute(sent, 'page', flipped(count, bit))]
    squeeze x58 -> x1, local copies, waits for them, and re-layouts: 43 us -> 1.8 us  [shards(): front['hl'][0]]
    add x72 -> x0, other arithmetic: 39.5 us -> none  [the longest x63 35.2 us: halve(): return kept + lax.ppermute(sent, 'page', flipped(count, bit))]
    another operation x37 -> x4, local copies, waits for them, and re-layouts: 36.3 us -> 1.51 us  [the longest x2 1.43 us: shards(): region_col, region_row = (region[:, :, None], region[:, None, :])]
    slice x27 -> x9, local copies, waits for them, and re-layouts: 31.6 us -> 10.7 us  [the longest x2 2.59 us: shards(): attention[:, :, column:]]
  transfers between devices with their start and end apart: 124 -> 0, of which waited for: 44 -> 0; matrix products, arithmetic and copies ran while one was open for 53% -> 0% of each run, Pallas kernels for 0% -> 0%
where the time goes in v2:
time: 409 us; the launch traced here: 403 us
  Pallas kernels  377 us (92%)
  local copies, waits for them, and re-layouts  21.8 us (5%)
    pallas_call x3, Pallas kernels, launch(): pl.pallas_call(inner, out_shape=[made[n][0] for n in made] + [kept[n] for...  377 us

profile of v2, /device:TPU:0, one launch (start us, length us, event | category | flops | bytes accessed | tf_op | source)
XLA Modules:
  0.0 402.8 jit_solution(9873984014246676445)
XLA Ops:
  0.6 0.7 reduce
  1.4 0.8 broadcast_in_dim_reshape.8.refs_5_.refs_3_
  2.2 0.7 broadcast_in_dim_reshape.9.refs_6_.refs_4_
  4.8 0.6 pad_add_fusion.refs_0_
  5.4 78.5 %shard_map.273 = (bf16[288,768]{1,0:T(8,128)(2,1)}, bf16[288,768]{1,0:T(8,128)(2,1)}, bf16[288,768]{1,0:T(8,128)(2,1)}, bf16[288,1536]{1,0:T(8,128)(2,1)}, bf16[...) custom-call(s32[4]{0:T(128)} %pad_add_fusion.refs_0_, ...), custom_call_target="tpu_custom_call" | custom-call | flops 6794772480 | bytes 16777216 | tf_op jit(solution)/shard_map/pallas_call | solution.py:318
  83.9 31.4 %shard_map.274 = (bf16[160,768]{1,0:T(8,128)(2,1)}, f32[160,768]{1,0:T(8,128)}, bf16[3,160,768]{2,1,0:T(8,128)(2,1)}, f32[1,3072]{1,0:T(1,128)}, f32[1,768]{1,0:...) custom-call(f32[160,768]{1,0:T(8,128)} %get-tuple-element.48.refs_0_.refs_25_, ...), custom_call_target="tpu_custom_call" | custom-call | flops 4529848320 | bytes 16777216 | tf_op jit(solution)/shard_map/pallas_call | solution.py:318
  115.4 1.8 slice_bitcast_fusion.refs_18_
  117.2 266.9 %shard_map.275 = (bf16[288,768]{1,0:T(8,128)(2,1)}, f32[288,768]{1,0:T(8,128)}, f32[160,768]{1,0:T(8,128)}, f32[32,768]{1,0:T(8,128)}, f32[8,96,768]{2,1,0:T(8,1...) custom-call(s32[4]{0:T(128)} %pad_add_fusion.refs_0_, ...), custom_call_target="tpu_custom_call" | custom-call | flops 16986931200 | bytes 16777216 | tf_op jit(solution)/shard_map/pallas_call | solution.py:318
  384.1 1.3 fusion
  385.5 0.6 reshape.56
  386.5 1.2 reshape.57
  387.7 1.6 slice.40
  389.3 1.0 slice.41
  390.3 0.9 rev.7
  391.1 1.0 slice.42
  392.2 0.8 slice.43
  392.9 0.8 slice.46
  394.4 1.5 fusion.1
  395.8 1.3 constant_dynamic-slice_fusion
  397.2 1.3 dynamic-slice.1
  398.5 0.8 copy.48
  399.3 1.7 copy.49
  400.9 0.9 copy.50
  401.8 0.8 copy.51
  (12 shorter events, 1.1 us)
Async XLA Ops:
  386.1 12.4 %copy-start.2 = (bf16[288,768]{1,0:T(8,128)(2,1)S(1)}, bf16[288,768]{1,0:T(8,128)(2,1)}, u32[]{:S(2)}) copy-start(bf16[288,768]{1,0:T(8,128)(2,1)} %get-tuple-element.77) | copy-start | bytes 1327108
  386.5 14.4 %copy-start = (f32[288,768]{1,0:T(8,128)S(1)}, f32[288,768]{1,0:T(8,128)}, u32[]{:S(2)}) copy-start(f32[288,768]{1,0:T(8,128)} %get-tuple-element.79) | copy-start | bytes 2654212
  387.7 14.1 %copy-start.1 = (f32[160,768]{1,0:T(8,128)S(1)}, f32[160,768]{1,0:T(8,128)}, u32[]{:S(2)}) copy-start(f32[160,768]{1,0:T(8,128)} %get-tuple-element.80) | copy-start | bytes 1474564

commit v3 on v2

--- a/solution.py
+++ b/solution.py
@@ -138,7 +138,15 @@
     return jnp.concatenate(parts, axis=0)
 
 
-def attend_rows(q_ref, kv_ref, context_ref, log_ref, bias, rows, keys):
+def in_parts(step, count, between):
+    parts = len(between) + 1
+    for i in range(parts):
+        lax.fori_loop(count * i // parts, count * (i + 1) // parts, step, 0)
+        if i < len(between):
+            between[i]()
+
+
+def attend_rows(q_ref, kv_ref, context_ref, log_ref, bias, rows, keys, between=()):
     width = q_ref.shape[1]
     key_start = kv_ref.shape[1] - 2 * width
 
@@ -153,11 +161,11 @@
         put_logs(log_ref, rows, pair, log_total)
         return 0
 
-    lax.fori_loop(0, width // PAIR, step, 0)
+    in_parts(step, width // PAIR, between)
 
 
 def attend_rows_back(
-    q_ref, kv_ref, context_ref, log_ref, grad_ref, dq_ref, dkv_ref, bias, rows, keys
+    q_ref, kv_ref, context_ref, log_ref, grad_ref, dq_ref, dkv_ref, bias, rows, keys, between=()
 ):
     width = q_ref.shape[1]
     key_start = kv_ref.shape[1] - 2 * width
@@ -181,7 +189,7 @@
         dkv_ref[keys, pl.ds(pl.multiple_of(grad_start + width + pair * PAIR, PAIR), PAIR)] = dv
         return 0
 
-    lax.fori_loop(0, width // PAIR, step, 0)
+    in_parts(step, width // PAIR, between)
 
 
 def allowed_bias(allowed):
@@ -239,14 +247,38 @@
         rows_ref[j * width : (j + 1) * width, :] = arriving_ref[i].astype(full)
 
 
-def window_bias(scalars, region_col_ref, region_row_ref, w, page_width):
+def page_scalars(r):
+    return None, r.page_cols[0], r.query_len[0], r.prompt_len[0]
+
+
+def region_vectors(region_ref, w, page_width):
+    size = WIN * WIN
+    labels = region_ref[0].astype(full)
+    band_rows = labels.shape[0]
+    across = page_width // WIN
+    first_row, first_col = w // across * WIN, w % across * WIN
+
+    def at(shape, token_dim, start, divide):
+        token = lax.broadcasted_iota(jnp.int32, shape, token_dim)
+        place = lax.div(token, WIN) if divide else lax.rem(token, WIN)
+        return place + start == lax.broadcasted_iota(jnp.int32, shape, 1 - token_dim)
+
+    rows = at((size, band_rows), 0, first_row, True).astype(full)
+    columns = at((size, page_width), 0, first_col, False)
+    column = jnp.sum(jnp.where(columns, dot_nn(rows, labels), 0.0), axis=1, keepdims=True)
+    rows = at((band_rows, size), 1, first_row, True).astype(full)
+    columns = at((page_width, size), 1, first_col, False)
+    row = jnp.sum(jnp.where(columns, dot_tn(labels, rows), 0.0), axis=0, keepdims=True)
+    return column, row
+
+
+def window_bias(scalars, region_ref, w, page_width):
     size = WIN * WIN
     live = window_live(w * size, size, scalars, page_width)
     own = lax.broadcasted_iota(jnp.int32, (size, size), 0)
     other = lax.broadcasted_iota(jnp.int32, (size, size), 1)
-    same = region_col_ref[w] == region_row_ref[w]
-    allowed = same & ((own == other) | live)
-    bias = allowed_bias(allowed)
+    column, row = region_vectors(region_ref, w, page_width)
+    bias = allowed_bias((column == row) & ((own == other) | live))
     return jnp.concatenate([bias, bias], axis=0)
 
 
@@ -331,6 +363,27 @@
     return dict(zip(results, outs))
 
 
+def hand_over(arrays):
+    count = len(arrays)
+    shapes = [a.shape if a.ndim < 4 else (a.shape[0], a.shape[3], a.shape[1] * a.shape[2]) for a in arrays]
+
+    def body(*refs):
+        for source, target in zip(refs[:count], refs[count:]):
+            if source.shape == target.shape:
+                target[...] = source[...]
+            else:
+                for k in range(source.shape[0]):
+                    target[k] = source[k].reshape(target.shape[2], target.shape[1]).T
+
+    return pl.pallas_call(
+        body,
+        out_shape=[jax.ShapeDtypeStruct(s, a.dtype) for s, a in zip(shapes, arrays)],
+        in_specs=[VMEM] * count,
+        out_specs=[VMEM] * count,
+        compiler_params=pltpu.CompilerParams(vmem_limit_bytes=62 * 2**20),
+    )(*arrays)
+
+
 def greet(devices):
     barrier = pltpu.get_barrier_semaphore()
     for device in devices:
@@ -363,6 +416,7 @@
     page_width, bands, rows, tokens = (dims[n] for n in ("page_width", "bands", "rows", "tokens"))
     width = r.y0.shape[1]
     me = lax.axis_index("row")
+    scalars = page_scalars(r)
     greet(band_peers(bands))
     loads = {}
     for a in range(3):
@@ -404,7 +458,7 @@
     size = WIN * WIN
     for w in range(tokens // size):
         part = slice(w * size, (w + 1) * size)
-        bias = window_bias(r.scalars, r.region_col, r.region_row, w, page_width)
+        bias = window_bias(scalars, r.region, w, page_width)
         attend_rows(r.q0, r.kv0, r.c0, r.log0, bias, part, part)
     r.save("c0", "log0")
     loads["wout0"].wait()
@@ -430,7 +484,7 @@
 
     lax.fori_loop(0, bands, project_self, 0)
     r.save("hs", "q1", "kv1")
-    bias = self_bias(me, r.scalars, rows, bands)
+    bias = self_bias(me, scalars, rows, bands)
     attend_rows(r.q1, r.kv1, r.c1, r.log1, bias, slice(None), slice(None))
     r.save("c1", "log1")
     loads["wout1"].wait()
@@ -447,7 +501,7 @@
         part = slice(s * tokens, (s + 1) * tokens)
         matmul_into(r.kv2.at[part], r.hl.at[s], r.wqkv2.at[:, width:], width)
     r.save("hl", "kv2")
-    attend_rows(r.q2, r.kv2, r.c2, r.log2, look_bias(dims, r.scalars), slice(None), slice(None))
+    attend_rows(r.q2, r.kv2, r.c2, r.log2, look_bias(dims, scalars), slice(None), slice(None))
     loads["wout2"].wait()
     y2 = r.y1[...] + (dot_nn(r.c2[...], r.wout2[...]) + r.b_out[2:3, :])
     r.y2[...] = y2
@@ -458,136 +512,10 @@
     r.finish()
 
 
-def feed_phase(dims, r, stream, norm, values, cot, out, grad, units):
-    pages, slab, bands = dims["pages"], dims["slab"], dims["bands"]
-    count, width = values.shape
-    core = lax.rem(lax.axis_index("page"), 2)
-    r.hidden[...] = norm_forward(values[...], r.gain[norm : norm + 1, :], r.bias[norm : norm + 1, :])
-    r.total[...] = values[...] + r.b_down[stream : stream + 1, :]
-    r.back[...] = jnp.zeros_like(r.back)
-    r.down_bias[...] = jnp.sum(cot[...].astype(full), axis=0, keepdims=True)
-
-    def quarter(j, _):
-        feed_copy(r, stream, 0, j).wait()
-        hidden = r.hidden[...]
-        z = dot_nn(hidden, r.up[j]) + r.b_up[stream : stream + 1, tile_cols(j, width)]
-        square = z * z
-        bend = jnp.tanh(0.7978845608028654 * (z + 0.044715 * (square * z)))
-        half = 0.5 * (1.0 + bend)
-        slope = half + (0.5 * z) * (1.0 - bend * bend) * (
-            0.7978845608028654 * (1.0 + 0.134145 * square)
-        )
-        active = (z * half).astype(bfloat)
-        feed_copy(r, stream, 1, j).wait()
-        r.total[...] += dot_nn(active, r.down[j])
-        low_grad = cot[...]
-        dz = dot_nt(low_grad, r.down[j]) * slope
-        r.up_bias[:, tile_cols(j, width)] = jnp.sum(dz, axis=0, keepdims=True)
-        dz = dz.astype(bfloat)
-        r.back[...] += dot_nt(dz, r.up[j])
-        split_blocks(dims, r.tile.at[j, 0], dot_tn(hidden, dz).astype(bfloat), core)
-        exchange(r, j, 0).start()
-        down_grad = dot_tn(active, low_grad).astype(bfloat)
-        deep = bands * slab
-        for side in range(2):
-            part = down_grad[side * deep : (side + 1) * deep]
-            for k in range(bands):
-                r.tile[j, 1, lax.rem(side + core, 2), k] = part[k * slab : (k + 1) * slab]
-        exchange(r, j, 1).start()
-        return 0
-
-    lax.fori_loop(0, bands, quarter, 0)
-    out[...] = r.total[...].astype(bfloat)
-    pull, gain_grad, bias_grad = norm_backward(
-        r.back[...], values[...], r.gain[norm : norm + 1, :]
-    )
-    grad[...] = cot[...].astype(full) + pull
-    r.gain_grad[...] = gain_grad
-    r.bias_grad[...] = bias_grad
-
-
-def feed_copy(r, stream, which, j):
-    width = r.up.shape[1]
-    if which == 0:
-        return pltpu.make_async_copy(
-            r.w_up.at[stream, :, tile_cols(j, width)], r.up.at[j], r.weight_sems.at[0, j]
-        )
-    return pltpu.make_async_copy(
-        r.w_down.at[stream, tile_cols(j, width), :], r.down.at[j], r.weight_sems.at[1, j]
-    )
-
-
 def split_blocks(dims, tile, grad, core):
     slab = dims["slab"]
     for block in range(dims["pages"]):
         tile[lax.rem(block + core, 2), block // 2] = grad[block * slab : (block + 1) * slab]
-
-
-def exchange(r, j, which):
-    page = lax.axis_index("page")
-    return pltpu.make_async_remote_copy(
-        src_ref=r.tile.at[j, which, 1],
-        dst_ref=r.landed.at[j, which],
-        send_sem=r.core_send.at[j, which],
-        recv_sem=r.core_recv.at[j, which],
-        device_id={"page": page + 1 - 2 * lax.rem(page, 2)},
-        device_id_type=MESH,
-    )
-
-
-def query_feed_kernel(dims, r):
-    bands, slab = dims["bands"], dims["slab"]
-    page = lax.axis_index("page")
-    greet(band_peers(bands) + [{"page": page + 1 - 2 * lax.rem(page, 2)}])
-    for j in range(bands):
-        feed_copy(r, 1, 0, j).start()
-        feed_copy(r, 1, 1, j).start()
-    memo = []
-    for s, peer in enumerate(band_peers(bands)):
-        copy = pltpu.make_async_remote_copy(
-            src_ref=r.hm,
-            dst_ref=r.memo.at[s],
-            send_sem=r.memo_send.at[s],
-            recv_sem=r.memo_recv.at[s],
-            device_id=peer,
-            device_id_type=MESH,
-        )
-        copy.start()
-        memo.append(copy)
-    feed_phase(dims, r, 1, 6, r.y2, r.gy3, r.out, r.grad, 0)
-    sum_units(r, bands)
-    for copy in memo:
-        copy.wait()
-    r.finish()
-
-
-def unit_out(r, j, which):
-    slab = r.landed.shape[3]
-    if which == 0:
-        rows = pl.ds(j * slab, slab)
-        places = [(pl.ds(2 * y, 2), r.bags.at[0, y, :, rows]) for y in range(2)]
-    else:
-        places = [
-            (k, r.bags.at[1, j // 2, j % 2, pl.ds(k * slab, slab)])
-            for k in range(r.landed.shape[2])
-        ]
-    return [
-        pltpu.make_async_copy(r.landed.at[j, which, part], place, r.core_out.at[j, which, i])
-        for i, (part, place) in enumerate(places)
-    ]
-
-
-def sum_units(r, count):
-    for j in range(count):
-        for which in range(2):
-            exchange(r, j, which).wait()
-            r.landed[j, which] = r.landed[j, which] + r.tile[j, which, 0]
-            for copy in unit_out(r, j, which):
-                copy.start()
-    for j in range(count):
-        for which in range(2):
-            for copy in unit_out(r, j, which):
-                copy.wait()
 
 
 RING = 3
@@ -633,7 +561,7 @@
         self.far = lax.rem(me + 2, bands)
         self.across = bands - 1 - me
         self.units, self.sent, self.outs, self.stages = 0, {}, {}, {}
-        self.total_units = 24
+        self.total_units = 32
         self.loading = {}
 
 
@@ -676,109 +604,133 @@
     def slab_targets(self, b, j):
         slab = self.dims["slab"]
         rows = pl.ds(j * slab, slab)
-        return [(pl.ds(2 * y, 2), self.bag(b).at[y, :, rows]) for y in range(2)]
+        return [(pl.ds(2 * y, 2), self.r.bags.at[b].at[y, :, rows]) for y in range(2)]
 
     def block_targets(self, b, j):
         slab = self.dims["slab"]
         return [
-            (k, self.bag(b).at[j // 2, j % 2, pl.ds(k * slab, slab)])
+            (k, self.r.bags.at[b].at[j // 2, j % 2, pl.ds(k * slab, slab)])
             for k in range(self.dims["bands"])
         ]
 
-    def flush(self):
+    def flush(self, units=None):
         for slot in list(self.outs):
-            for copy in self.outs.pop(slot):
-                copy.wait()
-
-    def bag(self, b):
-        return self.r.query_bags.at[b] if b < 2 else self.r.bags.at[b - 2]
-
-
-    def start(self, b, stage, parts):
-        r, copies = self.r, []
+            if units is None or slot in [u % RING for u in units]:
+                for copy in self.outs.pop(slot):
+                    copy.wait()
+
+
+    def start(self, b, stage, parts, which=(0, 1)):
+        r = self.r
         for i, (src, dst, device) in enumerate(parts):
-            at = (b, 2 * stage + i)
-            copy = remote(src, dst, r.stage_send.at[at], r.stage_recv.at[at], device)
-            copy.start()
-            copies.append(copy)
-        self.stages[b, stage] = copies
+            if i in which:
+                at = (b, 2 * stage + i)
+                copy = remote(src, dst, r.stage_send.at[at], r.stage_recv.at[at], device)
+                copy.start()
+                self.stages.setdefault((b, stage), []).append(copy)
+
+    def arrived(self, b, stage):
+        for copy in self.stages.pop((b, stage)):
+            copy.wait()
 
     def halves(self):
-        height = self.r.share.shape[0] // 2
+        height = self.r.recv1.shape[3]
         return pl.ds(0, height), pl.ds(height, height)
 
-    def first(self, *bags):
+    def landing1(self, b, half):
+        r = self.r
+        if b < 7:
+            return r.recv1.at[b, half]
+        return r.arena.at[2 * half : 2 * half + 2, : r.recv1.shape[3]]
+
+    def landing2(self, b, half):
+        r = self.r
+        height = r.recv1.shape[3]
+        if b < 7:
+            return r.recv2.at[b, half]
+        return r.arena.at[half, height : 2 * height]
+
+    def came2(self, b):
+        if b < 7:
+            return [self.r.came.at[b % 2, half, 0] for half in range(2)]
+        return [self.landing2(b, half) for half in range(2)]
+
+    def load_own(self, b):
+        r, slot = self.r, b % 2
+        top, bottom = self.halves()
+        bag = r.bags.at[b]
+        self.loading[b] = [
+            self.loads(bag.at[:, self.x, top], r.sums.at[slot, 0]),
+            self.loads(bag.at[self.y, :, bottom], r.sums.at[slot, 1]),
+        ]
+
+    def first(self, b, half=None):
         r = self.r
         top, bottom = self.halves()
+        bag = r.bags.at[b]
+        parts = [
+            (bag.at[:, 1 - self.x, top], self.landing1(b, 0), self.along_x),
+            (bag.at[1 - self.y, :, bottom], self.landing1(b, 1), self.along_y),
+        ]
+        self.start(b, 0, parts, [0, 1] if half is None else [half])
+
+    def load_second(self, *bags):
+        r = self.r
         for b in bags:
-            bag = self.bag(b)
-            self.start(
-                b,
-                0,
-                [
-                    (bag.at[:, 1 - self.x, top], r.recv1.at[b, 0], self.along_x),
-                    (bag.at[1 - self.y, :, bottom], r.recv1.at[b, 1], self.along_y),
-                ],
-            )
-
-    def arrived(self, b, stage):
-        for copy in self.stages[b, stage]:
-            copy.wait()
+            if b not in self.loading:
+                self.load_own(b)
+            self.arrived(b, 0)
+            if b < 7:
+                self.loading[b].append(self.loads(r.recv1.at[b], r.came.at[b % 2]))
 
     def second(self, *bags):
         r = self.r
-        top, bottom = self.halves()
-        loads = {}
-        for b in bags:
-            self.arrived(b, 0)
-            bag, slot = self.bag(b), b % 2
-            loads[b] = [
-                self.loads(bag.at[:, self.x, top], r.sums.at[slot, 0]),
-                self.loads(bag.at[self.y, :, bottom], r.sums.at[slot, 1]),
-                self.loads(r.recv1.at[b], r.came.at[slot]),
-            ]
         for b in bags:
             slot = b % 2
-            for copy in loads[b]:
-                copy.wait()
-            r.sums[slot] = r.sums[slot] + r.came[slot]
+            wait_all(self.loading.pop(b))
+            if b < 7:
+                r.sums[slot] = r.sums[slot] + r.came[slot]
+            else:
+                for half in range(2):
+                    r.sums[slot, half] = r.sums[slot, half] + self.landing1(b, half)[...]
             self.start(
                 b,
                 1,
                 [
-                    (r.sums.at[slot, 0, 1 - self.y], r.recv2.at[b, 0], self.along_y),
-                    (r.sums.at[slot, 1, 1 - self.x], r.recv2.at[b, 1], self.along_x),
+                    (r.sums.at[slot, 0, 1 - self.y], self.landing2(b, 0), self.along_y),
+                    (r.sums.at[slot, 1, 1 - self.x], self.landing2(b, 1), self.along_x),
                 ],
             )
 
+    def load_third(self, *bags):
+        r = self.r
+        for b in bags:
+            self.arrived(b, 1)
+            self.loading[b] = []
+            if b < 7:
+                self.loading[b].append(self.loads(r.recv2.at[b], r.came.at[b % 2, :, 0]))
+
     def third(self, *bags):
         r = self.r
-        loads = {}
-        for b in bags:
-            self.arrived(b, 1)
-            loads[b] = self.loads(r.recv2.at[b], r.came.at[b % 2, :, 0])
         for b in bags:
             slot = b % 2
-            loads[b].wait()
-            height = r.share.shape[0] // 2
-            r.share[:height] = r.sums[slot, 0, self.y] + r.came[slot, 0, 0]
-            r.share[height:] = r.sums[slot, 1, self.x] + r.came[slot, 1, 0]
-            self.cut(b)
+            wait_all(self.loading.pop(b))
+            top, bottom = self.came2(b)
+            self.cut(b, r.sums[slot, 0, self.y] + top[...], r.sums[slot, 1, self.x] + bottom[...])
             self.start(
                 b,
                 2,
                 [
-                    (r.pieces.at[slot, self.next], r.recv3.at[b, 0], {"row": self.next}),
-                    (r.pieces.at[slot, self.across], r.recv3.at[b, 1], {"row": self.next}),
+                    (r.pieces.at[b % 4, self.next], r.recv3.at[b, 0], {"row": self.next}),
+                    (r.pieces.at[b % 4, self.across], r.recv3.at[b, 1], {"row": self.next}),
                 ],
             )
 
-    def cut(self, b):
+    def cut(self, b, top, bottom):
         r, slab, bands = self.r, self.dims["slab"], self.dims["bands"]
-        slot = b % 2
-        width = r.share.shape[1]
+        width = top.shape[1]
         size = width // bands
-        parts = [r.share[k * slab : (k + 1) * slab, :] for k in range(bands)]
+        parts = [half[k * slab : (k + 1) * slab] for half in (top, bottom) for k in range(2)]
         if b in (0, 2):
             made = parts
         elif b in (1, 3):
@@ -799,38 +751,42 @@
                 for z in range(bands)
             ]
         for z in range(bands):
-            r.pieces[slot, z] = made[z]
+            r.pieces[b % 4, z] = made[z]
 
     def fourth(self, *bags):
         r = self.r
-        loads = {}
-        for b in bags:
-            self.arrived(b, 2)
-            loads[b] = self.loads(r.recv3.at[b], r.came3.at[b % 2])
         for b in bags:
             slot = b % 2
-            loads[b].wait()
-            r.last[slot, 0] = r.pieces[slot, self.me] + r.came3[slot, 0]
-            r.last[slot, 1] = r.pieces[slot, self.far] + r.came3[slot, 1]
-            self.start(b, 3, [(r.last.at[slot, 1], r.recv4.at[b], {"row": self.far})])
+            self.arrived(b, 2)
+            r.last[slot, 0] = r.pieces[b % 4, self.me] + r.recv3[b, 0]
+            r.last[slot, 1] = r.pieces[b % 4, self.far] + r.recv3[b, 1]
+            self.start(b, 3, [(r.last.at[slot, 1], r.recv4.at[b], {"row": self.far})], [0])
+
+    def store(self, name, target, value):
+        scratch = getattr(self.r, name)
+        for copy in self.loading.pop(name, ()):
+            copy.wait()
+        scratch[...] = value
+        self.loading[name] = [self.loads(scratch, target)]
 
     def end(self, *bags):
-        r = self.r
-        loads, outs = {}, []
+        r, slab, bands = self.r, self.dims["slab"], self.dims["bands"]
         for b in bags:
             self.arrived(b, 3)
-            loads[b] = self.loads(r.recv4.at[b], r.came4.at[b % 2])
-        for b in bags:
-            slot = b % 2
-            loads[b].wait()
-            if ("final", slot) in self.loading:
-                self.loading.pop(("final", slot)).wait()
-            r.final[slot] = r.last[slot, 0].astype(full) + r.came4[slot].astype(full)
-            self.loading["final", slot] = self.loads(r.final.at[slot], r.shares.at[b])
+            total = r.last[b % 2, 0].astype(full) + r.recv4[b].astype(full)
+            size = total.shape[1] // bands
+            if b in (0, 2):
+                self.store("final_up", r.wup.at[1 - b // 2], total)
+            elif b in (1, 3):
+                parts = [total[:, k * size : (k + 1) * size] for k in range(bands)]
+                self.store("final_down", r.wdown.at[1 - b // 2], jnp.stack(parts))
+            else:
+                self.store("final_out", r.wout.at[7 - b], total[:, :size])
+                self.store("final_qkv", r.wqkv.at[7 - b], total[:, size:])
 
     def finish(self):
-        for copy in self.loading.values():
-            copy.wait()
+        for copies in self.loading.values():
+            wait_all(copies)
 
 
 def layer_loads(r, loads, layer, arena):
@@ -851,6 +807,105 @@
     part = slice(start, start + count)
     kv_ref[part, :width] = dot_nn(into_ref[part, :], arena[1]).astype(bfloat)
     kv_ref[part, width:] = dot_nn(into_ref[part, :], arena[2]).astype(bfloat)
+
+
+class Quarters:
+    def __init__(self, r, loads, arena):
+        self.r, self.loads, self.arena = r, loads, arena
+        self.coming = {}
+
+    def load(self, stream, j):
+        r, width = self.r, self.arena.shape[1]
+        cols = pl.ds(j * width, width)
+        pair = 2 * (j % 2)
+        self.coming[stream, j] = [
+            self.loads(r.w_up.at[stream, :, cols], self.arena.at[pair]),
+            self.loads(r.w_down.at[stream, cols, :], self.arena.at[pair + 1]),
+        ]
+
+    def ready(self, stream, j):
+        wait_all(self.coming.pop((stream, j)))
+        pair = 2 * (j % 2)
+        return self.arena.at[pair], self.arena.at[pair + 1]
+
+
+def feed_both_ways(dims, r, red, quarters, stream, norm, values, cot, hidden_ref, total, back, kept, after):
+    bands = dims["bands"]
+    width = values.shape[1]
+    row_out, row_up, row_down, row_gain, row_bias = vec_rows(dims)
+    hidden_ref[...] = norm_forward(values[...], r.gain[norm : norm + 1, :], r.bias[norm : norm + 1, :])
+    total[...] = values[...] + r.b_down[stream : stream + 1, :]
+    back[...] = jnp.zeros_like(back)
+    r.vec[row_down + stream : row_down + stream + 1, :] = jnp.sum(
+        cot[...].astype(full), axis=0, keepdims=True
+    )
+    row_up = row_up + stream * bands
+    units = FeedUnits(dims, red, 2 * (1 - stream))
+    for j in range(bands):
+        up, down = quarters.ready(stream, j)
+        z = dot_nn(hidden_ref[...], up[...]) + r.b_up[stream : stream + 1, j * width : (j + 1) * width]
+        square = z * z
+        bend = jnp.tanh(0.7978845608028654 * (z + 0.044715 * (square * z)))
+        half = 0.5 * (1.0 + bend)
+        slope = half + (0.5 * z) * (1.0 - bend * bend) * (
+            0.7978845608028654 * (1.0 + 0.134145 * square)
+        )
+        active = (z * half).astype(bfloat)
+        total[...] += dot_nn(active, down[...])
+        dz = dot_nt(cot[...], down[...]) * slope
+        r.vec[row_up + j : row_up + j + 1, :] = jnp.sum(dz, axis=0, keepdims=True)
+        dz = dz.astype(bfloat)
+        back[...] += dot_nt(dz, up[...])
+        if j + 2 < bands:
+            quarters.load(stream, j + 2)
+        if kept is None:
+            units.quarter(j, hidden_ref[...], dz, active, cot[...])
+        else:
+            kept[j][0][...] = dz
+            kept[j][1][...] = active
+        after(j)
+    if kept is None:
+        units.finish()
+
+
+class FeedUnits:
+    def __init__(self, dims, red, bag):
+        self.dims, self.red, self.bag = dims, red, bag
+        self.waiting = []
+
+    def quarter(self, j, hidden, dz, active, low_grad):
+        dims, red = self.dims, self.red
+        bands, slab = dims["bands"], dims["slab"]
+        deep = bands * slab
+        up_grad = dot_tn(hidden, dz).astype(bfloat)
+        unit = red.unit(lambda tile: split_blocks(dims, tile, up_grad, red.core))
+        self.waiting.append((unit, red.slab_targets(self.bag, j)))
+        if len(self.waiting) > 1:
+            red.settle(*self.waiting.pop(0))
+        down_grad = dot_tn(active, low_grad).astype(bfloat)
+
+        def fill(tile):
+            for side in range(2):
+                part = down_grad[side * deep : (side + 1) * deep]
+                for k in range(bands):
+                    tile[lax.rem(side + red.core, 2), k] = part[k * slab : (k + 1) * slab]
+
+        unit = red.unit(fill)
+        self.waiting.append((unit, red.block_targets(self.bag + 1, j)))
+        red.settle(*self.waiting.pop(0))
+
+    def finish(self):
+        for item in self.waiting:
+            self.red.settle(*item)
+        self.red.flush()
+
+
+def feed_end(dims, r, norm, values, cot, back):
+    row_out, row_up, row_down, row_gain, row_bias = vec_rows(dims)
+    pull, gain, bias = norm_backward(back[...], values[...], r.gain[norm : norm + 1, :])
+    r.vec[row_gain + norm : row_gain + norm + 1, :] = gain
+    r.vec[row_bias + norm : row_bias + norm + 1, :] = bias
+    return cot[...].astype(full) + pull
 
 
 def pair_back(dkv_ref, arena, start, count):
@@ -876,7 +931,7 @@
     return pair_back(dkv_ref, arena, 0, count), copies
 
 
-def weight_units(dims, r, red, b, context, low, from_rows, into_rows, dq, dkv):
+def weight_units(dims, r, red, b, context, low, from_rows, into_rows, dq, dkv, begin=True):
     width = r.tile.shape[-1]
     sides = [
         lambda: dot_tn(context[...], low[...]),
@@ -890,12 +945,41 @@
         units.append(red.unit(lambda tile: split_blocks(dims, tile, grad, red.core)))
         if j:
             red.settle(units[j - 1], red.slab_targets(b, j - 1))
+        if j == 3 and begin:
+            red.flush(units[:2])
+            red.first(b, 0)
     red.settle(units[-1], red.slab_targets(b, 3))
+    red.flush()
+    if begin:
+        red.first(b, 1)
 
 
 def vec_rows(dims):
     quarters = dims["bands"]
     return 0, 4, 4 + 2 * quarters, 6 + 2 * quarters, 13 + 2 * quarters
+
+
+def put_vectors(dims, r):
+    bands, slab, pages = dims["bands"], dims["slab"], dims["pages"]
+    row_out, row_up, row_down, row_gain, row_bias = vec_rows(dims)
+    width = r.vec.shape[1]
+    page = lax.axis_index("page")
+    own = pltpu.roll(r.vec[...], lax.rem(width - page * slab, width), 1)[:, :slab]
+    r.bout[...] = own[row_out:row_up]
+    r.bdown[...] = own[row_down:row_gain]
+    r.gain_grad[...] = own[row_gain:row_bias]
+    r.bias_grad[...] = own[row_bias : row_bias + 7]
+    hidden = bands * slab
+    per_row = pages // bands
+    row, shift = page // per_row, lax.rem(page, per_row) * hidden
+    for stream in range(2):
+        start = row_up + stream * bands
+        chosen = jnp.zeros((1, width), full)
+        for k in range(bands):
+            chosen = chosen + jnp.where(row == k, r.vec[start + k : start + k + 1, :], 0.0)
+        r.bup[stream : stream + 1, :] = jnp.where(
+            shift == 0, chosen[:, :hidden], chosen[:, width - hidden :]
+        )
 
 
 def back_kernel(dims, r):
@@ -903,24 +987,32 @@
     slab = dims["slab"]
     width = r.f1.shape[1]
     me = lax.axis_index("row")
+    scalars = page_scalars(r)
     loads = Loads(r.load_sems)
     red = Reducer(dims, r, loads)
+    row_out, row_up, row_down, row_gain, row_bias = vec_rows(dims)
+    hm_load = loads(r.hm_hbm, r.into.at[0:rows])
+    y2_load = [loads(r.y2_hbm, r.y2), loads(r.gy3_hbm, r.dq_s)]
+    quarters = Quarters(r, loads, r.arena)
+    quarters.load(1, 0)
+    quarters.load(1, 1)
     greet(band_peers(bands) + [red.other, red.along_x, red.along_y])
-    red.first(0, 1)
-    row_out, row_up, row_down, row_gain, row_bias = vec_rows(dims)
-
+    hm_load.wait()
+    memo_copies = []
+    for s, peer in enumerate(band_peers(bands), 1):
+        copy = remote(
+            r.into.at[0:rows],
+            r.into.at[s * rows : (s + 1) * rows],
+            r.hm_send.at[s - 1],
+            r.hm_recv.at[s - 1],
+            peer,
+        )
+        copy.start()
+        memo_copies.append(copy)
     weights3 = layer_loads(r, loads, 3, r.att)
-    hl_load = loads(r.hl_hbm, r.from_rows)
-    memo_load = [
-        loads(r.hm_hbm, r.into.at[0:rows]),
-        loads(r.memo_hbm, r.into.at[rows : bands * rows]),
-    ]
+    hl_load = loads(r.hl_hbm.at[0], r.from_rows)
     x1_load = loads(r.x1_hbm, r.f1)
     gx3_load = loads(r.gx3_hbm, r.cot)
-    feed_loads = [[feed_copy(r, 0, i, j) for i in range(2)] for j in range(bands)]
-    for pair in feed_loads:
-        for copy in pair:
-            copy.start()
     small = [
         loads(src, dst)
         for src, dst in (
@@ -931,83 +1023,62 @@
             (r.c1_hbm, r.c1),
             (r.log1_hbm, r.log1),
             (r.ha_hbm, r.ha),
-            (r.y2_hbm, r.y2),
             (r.y1_hbm, r.y1),
-            (r.gy2_hbm, r.gy),
         )
     ]
     r.vec[...] = jnp.zeros_like(r.vec)
-    for j in range(bands):
-        r.vec[row_up + bands + j : row_up + bands + j + 1, :] = r.up_bias1[
-            :, j * width : (j + 1) * width
-        ]
-    r.vec[row_down + 1 : row_down + 2, :] = r.down_bias1[...]
-    r.vec[row_gain + 6 : row_gain + 7, :] = r.gain6[...]
-    r.vec[row_bias + 6 : row_bias + 7, :] = r.bias6[...]
+
+    wait_all(y2_load)
+
+    def after_query(j):
+        if j == 2:
+            red.flush()
+            red.first(0, 0)
+
+    feed_both_ways(
+        dims, r, red, quarters, 1, 6, r.y2, r.dq_s, r.grad_s, r.own_m, r.gy, None, after_query
+    )
+    red.first(0, 1)
+    red.first(1)
+    quarters.load(0, 0)
+    quarters.load(0, 1)
+    r.query_out[...] = r.own_m[...].astype(bfloat)
+    r.gy[...] = feed_end(dims, r, 6, r.y2, r.dq_s, r.gy)
 
     every = slice(None)
     few = slice(0, bands * rows)
     hl_load.wait()
     wait_all(weights3)
     r.q[...] = (dot_nn(r.from_rows[...], r.att[0]) * SCALE).astype(bfloat)
-    wait_all(memo_load)
-    for s in range(bands):
+    project_pair_into(r.kv, r.into, r.att, 0, rows)
+    for s in range(1, bands):
+        memo_copies[s - 1].wait()
         project_pair_into(r.kv, r.into, r.att, s * rows, rows)
-    bias = read_bias(me, dims, r.scalars)
+    bias = read_bias(me, dims, scalars)
     r.log[...] = jnp.zeros_like(r.log)
     attend_rows(r.q, r.kv, r.context, r.log, bias, every, few)
     x1_load.wait()
     r.f2[...] = r.f1[...] + (dot_nn(r.context[...], r.att[3]) + r.b_out[3:4, :])
 
     gx3_load.wait()
-    r.low[...] = norm_forward(r.f2[...], r.gain[5:6, :], r.bias[5:6, :])
-    r.f3[...] = r.f2[...] + r.b_down[0:1, :]
-    r.f4[...] = jnp.zeros_like(r.f4)
-    r.vec[row_down : row_down + 1, :] = jnp.sum(r.cot[...].astype(full), axis=0, keepdims=True)
-    waiting = []
-    for j in range(bands):
-        feed_loads[j][0].wait()
-        hidden = r.low[...]
-        z = dot_nn(hidden, r.up[j]) + r.b_up[0:1, j * width : (j + 1) * width]
-        square = z * z
-        bend = jnp.tanh(0.7978845608028654 * (z + 0.044715 * (square * z)))
-        half = 0.5 * (1.0 + bend)
-        slope = half + (0.5 * z) * (1.0 - bend * bend) * (
-            0.7978845608028654 * (1.0 + 0.134145 * square)
-        )
-        active = (z * half).astype(bfloat)
-        feed_loads[j][1].wait()
-        r.f3[...] += dot_nn(active, r.down[j])
-        low_grad = r.cot[...]
-        dz = dot_nt(low_grad, r.down[j]) * slope
-        r.vec[row_up + j : row_up + j + 1, :] = jnp.sum(dz, axis=0, keepdims=True)
-        dz = dz.astype(bfloat)
-        r.f4[...] += dot_nt(dz, r.up[j])
-        up_grad = dot_tn(hidden, dz).astype(bfloat)
-        unit = red.unit(lambda tile: split_blocks(dims, tile, up_grad, red.core))
-        waiting.append((unit, red.slab_targets(2, j)))
-        down_grad = dot_tn(active, low_grad).astype(bfloat)
-        deep = bands * slab
-
-        def fill(tile):
-            for side in range(2):
-                part = down_grad[side * deep : (side + 1) * deep]
-                for k in range(bands):
-                    tile[lax.rem(side + red.core, 2), k] = part[k * slab : (k + 1) * slab]
-
-        if len(waiting) > 1:
-            red.settle(*waiting.pop(0))
-        unit = red.unit(fill)
-        waiting.append((unit, red.block_targets(3, j)))
-        red.settle(*waiting.pop(0))
+
+    def after_patches(j):
         if j == 1:
-            red.second(0, 1)
-    for item in waiting:
-        red.settle(*item)
-    red.flush()
-    red.first(2, 3)
-    weights2 = layer_loads(r, loads, 2, r.up)
-    weights1 = layer_loads(r, loads, 1, r.down)
+            red.load_second(0)
+        if j == 2:
+            red.second(0)
+            red.load_second(1)
+
+    spare = slice(bands * rows, bands * rows + tokens)
+    places = [r.parts_l.at[0], r.parts_l.at[1], r.parts_l.at[2], r.into.at[spare]]
+    for ref in (r.kv, r.dkv):
+        places += [ref.at[spare, :width], ref.at[spare, width:]]
+    kept = [(places[2 * j], places[2 * j + 1]) for j in range(bands)]
+    feed_both_ways(
+        dims, r, red, quarters, 0, 5, r.f2, r.cot, r.hidden, r.f3, r.f4, kept, after_patches
+    )
+    red.second(1)
+    weights2 = layer_loads(r, loads, 2, r.arena)
     to_right = {"row": lax.rem(me + 1, bands)}
     moved = dot_tn(r.order[...], r.f3[...].astype(bfloat)).astype(bfloat)
     stay = tokens - SHIFT * page_width
@@ -1017,19 +1088,16 @@
         r.halo_low, r.vis_out.at[: tokens - stay], r.halo_send.at[0], r.halo_recv.at[0], to_right
     )
     halo.start()
-    pull, gain5, bias5 = norm_backward(r.f4[...], r.f2[...], r.gain[5:6, :])
-    r.vec[row_gain + 5 : row_gain + 6, :] = gain5
-    r.vec[row_bias + 5 : row_bias + 6, :] = bias5
-    gx2 = r.cot[...].astype(full) + pull
+    gx2 = feed_end(dims, r, 5, r.f2, r.cot, r.f4)
     r.f5[...] = gx2
+    red.load_third(0)
 
     low = gx2.astype(bfloat)
     r.low[...] = low
     r.vec[row_out + 3 : row_out + 4, :] = jnp.sum(low.astype(full), axis=0, keepdims=True)
     r.grad[...] = dot_nt(low, r.att[3]).astype(bfloat)
-    attend_rows_back(r.q, r.kv, r.context, r.log, r.grad, r.dq, r.dkv, bias, every, few)
-    kv_load = loads(r.kv2_hbm, r.kv)
-    red.third(0, 1)
+    between = (lambda: (red.third(0), red.load_third(1)), lambda: red.third(1))
+    attend_rows_back(r.q, r.kv, r.context, r.log, r.grad, r.dq, r.dkv, bias, every, few, between)
     own, memo_sends = scatter_back(
         r, bands, r.dkv, r.att, rows, r.parts_m, r.got_m, r.memo_send, r.memo_recv
     )
@@ -1037,11 +1105,17 @@
     r.f4[...] = dot_nt(r.dq[...], r.att[0])
     weights0 = layer_loads(r, loads, 0, r.att)
     few_dkv, few_into = r.dkv.at[0 : bands * rows], r.into.at[0 : bands * rows]
-    weight_units(dims, r, red, 4, r.context, r.low, r.from_rows, few_into, r.dq, few_dkv)
-    red.flush()
-    red.first(4)
-    red.fourth(0, 1)
-    red.second(2, 3)
+    units = FeedUnits(dims, red, 2)
+    for j in range(bands):
+        units.quarter(j, r.hidden[...], kept[j][0][...], kept[j][1][...], r.cot[...])
+        if j == 2:
+            red.flush()
+            red.first(2, 0)
+    units.finish()
+    red.first(2, 1)
+    red.first(3)
+    kv_load = loads(r.kv2_hbm, r.kv)
+    weight_units(dims, r, red, 4, r.context, r.low, r.from_rows, few_into, r.dq, few_dkv, False)
     late = [
         loads(r.hl_all_hbm, r.into),
         loads(r.q0_hbm, r.q),
@@ -1054,6 +1128,7 @@
 
     wait_all(small)
     wait_all(memo_sends)
+    red.fourth(0, 1)
     pull, gain4, bias4 = norm_backward(
         r.own_m[...] + sum(r.got_m[s].astype(full) for s in range(bands - 1)),
         r.y2[...],
@@ -1067,53 +1142,65 @@
     r.low_s[...] = low
     r.vec[row_out + 2 : row_out + 3, :] = jnp.sum(low.astype(full), axis=0, keepdims=True)
     wait_all(weights2)
-    r.grad_s[...] = dot_nt(low, r.up[3]).astype(bfloat)
+    r.grad_s[...] = dot_nt(low, r.arena[3]).astype(bfloat)
     kv_load.wait()
     attend_rows_back(
-        r.q2, r.kv, r.c2, r.log2, r.grad_s, r.dq_s, r.dkv, look_bias(dims, r.scalars), every, every
-    )
+        r.q2,
+        r.kv,
+        r.c2,
+        r.log2,
+        r.grad_s,
+        r.dq_s,
+        r.dkv,
+        look_bias(dims, scalars),
+        every,
+        every,
+        (lambda: red.load_second(2), lambda: (red.second(2), red.load_second(3))),
+    )
+    red.second(3)
+    red.first(4)
+    red.end(0, 1)
     kv_load = loads(r.kv1_hbm, r.kv.at[0 : bands * rows])
     own, look_sends = scatter_back(
-        r, bands, r.dkv, r.up, tokens, r.parts_l, r.got_l, r.look_send, r.look_recv
+        r, bands, r.dkv, r.arena, tokens, r.parts_l, r.got_l, r.look_send, r.look_recv
     )
     r.f4[...] += own
-    pull, gain2, bias2 = norm_backward(dot_nt(r.dq_s[...], r.up[0]), r.y1[...], r.gain[2:3, :])
+    pull, gain2, bias2 = norm_backward(dot_nt(r.dq_s[...], r.arena[0]), r.y1[...], r.gain[2:3, :])
     r.vec[row_gain + 2 : row_gain + 3, :] = gain2
     r.vec[row_bias + 2 : row_bias + 3, :] = bias2
     r.gy[...] += pull
-    red.end(0, 1)
-    red.third(2, 3)
+    weights1 = layer_loads(r, loads, 1, r.arena)
     wait_all(late)
     weight_units(dims, r, red, 5, r.c2, r.low_s, r.ha, r.into, r.dq_s, r.dkv)
     hidden_load = loads(r.hs_hbm, r.into.at[0 : bands * rows])
-    red.flush()
-    red.first(5)
-    red.second(4)
+    red.load_third(2, 3)
 
     low = r.gy[...].astype(bfloat)
     r.low_s[...] = low
     r.vec[row_out + 1 : row_out + 2, :] = jnp.sum(low.astype(full), axis=0, keepdims=True)
     wait_all(weights1)
-    r.grad_s[...] = dot_nt(low, r.down[3]).astype(bfloat)
+    r.grad_s[...] = dot_nt(low, r.arena[3]).astype(bfloat)
     kv_load.wait()
-    bias = self_bias(me, r.scalars, rows, bands)
-    attend_rows_back(r.q1, r.kv, r.c1, r.log1, r.grad_s, r.dq_s, r.dkv, bias, every, few)
+    bias = self_bias(me, scalars, rows, bands)
+    between = (lambda: (red.third(2, 3), red.load_second(4)), lambda: red.second(4))
+    attend_rows_back(
+        r.q1, r.kv, r.c1, r.log1, r.grad_s, r.dq_s, r.dkv, bias, every, few, between
+    )
     kv_load = loads(r.kv0_hbm, r.kv.at[0:tokens])
     own, self_sends = scatter_back(
-        r, bands, r.dkv, r.down, rows, r.parts_m, r.got_s, r.self_send, r.self_recv
-    )
-    r.own_m[...] = own + dot_nt(r.dq_s[...], r.down[0])
-    red.fourth(2, 3)
+        r, bands, r.dkv, r.arena, rows, r.parts_m, r.got_s, r.self_send, r.self_recv
+    )
+    r.own_m[...] = own + dot_nt(r.dq_s[...], r.arena[0])
     hidden_load.wait()
     weight_units(
         dims, r, red, 6, r.c1, r.low_s, r.into.at[0:rows], few_into, r.dq_s, few_dkv
     )
-    red.flush()
-    red.first(6)
+
+    red.load_second(5)
+    red.load_third(4)
+    red.second(5)
+    wait_all(look_sends)
     red.third(4)
-    red.second(5)
-
-    wait_all(look_sends)
     pull, gain3, bias3 = norm_backward(
         r.f4[...] + sum(r.got_l[s].astype(full) for s in range(bands - 1)),
         r.f1[...],
@@ -1132,10 +1219,15 @@
     size = WIN * WIN
     for w in range(tokens // size):
         part = slice(w * size, (w + 1) * size)
-        bias = window_bias(r.scalars, r.region_col, r.region_row, w, page_width)
+        bias = window_bias(scalars, r.region, w, page_width)
         attend_rows_back(
             r.q, r.kv, r.context, r.log, r.grad, r.dq, r.dkv, bias, part, part
         )
+        if w == 0:
+            red.load_third(5)
+        else:
+            red.third(5)
+            red.load_second(6)
     dr = pair_back(r.dkv, r.att, 0, tokens) + dot_nt(r.dq[...], r.att[0])
     pull, gain0, bias0 = norm_backward(dr, r.cot[...].astype(full), r.gain[0:1, :])
     r.vec[row_gain : row_gain + 1, :] = gain0
@@ -1150,15 +1242,12 @@
         r.f2.at[: tokens - stay], r.vis_grad.at[: tokens - stay], r.halo_send.at[1], r.halo_recv.at[1], to_right
     )
     halo_back.start()
+    red.second(6)
     weight_units(
         dims, r, red, 7, r.context, r.low, r.from_rows, r.from_rows, r.dq, r.dkv.at[0:tokens]
     )
-    red.flush()
-    red.first(7)
-    red.end(2, 3)
-    red.fourth(4)
-    red.third(5)
-    red.second(6)
+    red.load_own(7)
+    red.load_third(6)
 
     wait_all(self_sends)
     pull, gain1, bias1 = norm_backward(
@@ -1173,24 +1262,35 @@
     def swap(i, device):
         copy = remote(r.vec, r.vec_in.at[i], r.vec_send.at[i], r.vec_recv.at[i], device)
         copy.start()
+        return copy
+
+    def add(i, copy):
         copy.wait()
         r.vec[...] = r.vec[...] + r.vec_in[i]
 
-    swap(0, red.other)
-    red.end(4)
-    red.fourth(5)
-    swap(1, red.along_x)
+    red.fourth(2, 3)
+    red.third(6)
+    copy = swap(0, red.other)
+    red.end(2, 3)
+    add(0, copy)
+    copy = swap(1, {"row": red.next})
+    red.fourth(4, 5)
+    add(1, copy)
+    copy = swap(2, {"row": red.far})
+    red.load_second(7)
     red.second(7)
-    swap(2, red.along_y)
-    red.third(6)
-    swap(3, {"row": red.next})
-    red.end(5)
+    add(2, copy)
+    copy = swap(3, red.along_x)
+    red.end(4, 5)
+    red.fourth(6)
+    add(3, copy)
+    copy = swap(4, red.along_y)
+    red.load_third(7)
     red.third(7)
-    red.fourth(6)
-    swap(4, {"row": red.far})
+    add(4, copy)
+    put_vectors(dims, r)
+    red.end(6)
     red.fourth(7)
-    red.end(6)
-    r.vec_out[...] = r.vec[...]
     red.end(7)
     halo.wait()
     halo_back.wait()
@@ -1231,25 +1331,21 @@
         pages=pages,
         slab=slab,
     )
-    scalars = jnp.stack([me, page_cols[0], query_len[0], prompt_len[0]]).astype(jnp.int32)
-    scalar = (scalars, SMEM)
     qkv_any, out_any = (w_qkv, ANY), (w_out, ANY)
     log_lanes = full_shape(tokens, PAIR)
     y0, gy3 = query_stream[0], query_cotangent[0]
-    across = page_width // WIN
-    region = region_ids[0].reshape(band_rows // WIN, WIN, across, WIN)
-    region = jnp.swapaxes(region, 1, 2).reshape(-1, WIN * WIN)
-    region_col, region_row = region[:, :, None], region[:, None, :]
+    lengths = dict(
+        page_cols=(page_cols, SMEM), query_len=(query_len, SMEM), prompt_len=(prompt_len, SMEM)
+    )
     order = jnp.asarray(source_order(page_width, band_rows), bfloat)
 
     given = dict(
-        scalars=scalar,
+        **lengths,
         vis=(vis_stream, VMEM),
         cot=(vis_cotangent, VMEM),
         y0=(y0, VMEM),
         order=(order, VMEM),
-        region_col=(region_col, VMEM),
-        region_row=(region_row, VMEM),
+        region=(region_ids, VMEM),
         gain=(norm_gain, VMEM),
         bias=(norm_bias, VMEM),
         b_out=(b_out, VMEM),
@@ -1306,66 +1402,19 @@
         0,
         40 * tokens * width * width,
     )
-    bag_shape = (2, 2, 2, bands * slab, width)
-    quarter_sems = pltpu.SemaphoreType.DMA((bands, 2))
-    feed = launch(
-        partial(query_feed_kernel, dims),
-        dict(
-            y2=(front["y2"], VMEM),
-            gy3=(gy3, VMEM),
-            hm=(front["hm"], VMEM),
-            gain=(norm_gain, VMEM),
-            bias=(norm_bias, VMEM),
-            b_up=(b_up, VMEM),
-            b_down=(b_down, VMEM),
-            w_up=(w_up, ANY),
-            w_down=(w_down, ANY),
-        ),
-        {},
-        dict(
-            out=(low_shape(rows, width), VMEM),
-            grad=(full_shape(rows, width), VMEM),
-            memo=(low_shape(bands - 1, rows, width), VMEM),
-            up_bias=(full_shape(1, hidden_units), VMEM),
-            down_bias=(full_shape(1, width), VMEM),
-            gain_grad=(full_shape(1, width), VMEM),
-            bias_grad=(full_shape(1, width), VMEM),
-            bags=(low_shape(*bag_shape), ANY),
-        ),
-        {},
-        dict(
-            hidden=pltpu.VMEM((rows, width), bfloat),
-            total=pltpu.VMEM((rows, width), full),
-            back=pltpu.VMEM((rows, width), full),
-            up=pltpu.VMEM((bands, width, width), bfloat),
-            down=pltpu.VMEM((bands, width, width), bfloat),
-            tile=pltpu.VMEM((bands, 2, 2, pages // 2, slab, width), bfloat),
-            landed=pltpu.VMEM((bands, 2, pages // 2, slab, width), bfloat),
-            weight_sems=pltpu.SemaphoreType.DMA((2, bands)),
-            core_send=quarter_sems,
-            core_recv=quarter_sems,
-            core_out=pltpu.SemaphoreType.DMA((bands, 2, bands)),
-            memo_send=peer_sems,
-            memo_recv=peer_sems,
-        ),
-        1,
-        12 * rows * width * hidden_units,
-    )
     hbm = {
         "x1_hbm": front["x1"],
         "x0_hbm": front["x0"],
         "gx3_hbm": front["gx3"],
         "hv_hbm": front["hv"],
-        "hl_hbm": front["hl"][0],
+        "hl_hbm": front["hl"],
         "hl_all_hbm": front["hl"].reshape(bands * tokens, width),
         "hs_hbm": front["hs"].reshape(bands * rows, width),
         "ha_hbm": front["ha"],
         "hm_hbm": front["hm"],
-        "memo_hbm": feed["memo"].reshape((bands - 1) * rows, width),
         "y1_hbm": front["y1"],
         "y2_hbm": front["y2"],
-        "gy2_hbm": feed["grad"],
-        "query_bags": feed["bags"],
+        "gy3_hbm": gy3,
         "w_qkv": w_qkv,
         "w_out": w_out,
         "w_up": w_up,
@@ -1377,17 +1426,12 @@
     near = dict(
         y0=y0,
         order=order,
-        region_col=region_col,
-        region_row=region_row,
+        region=region_ids,
         gain=norm_gain,
         bias=norm_bias,
         b_out=b_out,
         b_up=b_up,
         b_down=b_down,
-        up_bias1=feed["up_bias"],
-        down_bias1=feed["down_bias"],
-        gain6=feed["gain_grad"],
-        bias6=feed["bias_grad"],
     )
     height = bands * slab
     halo_rows = SHIFT * page_width
@@ -1397,18 +1441,20 @@
     dma = pltpu.SemaphoreType.DMA
     scratch = dict(
         att=pltpu.VMEM((4, width, width), bfloat),
-        up=pltpu.VMEM((bands, width, width), bfloat),
-        down=pltpu.VMEM((bands, width, width), bfloat),
+        arena=pltpu.VMEM((4, width, width), bfloat),
         tile=pltpu.VMEM((RING, 2, pages // 2, slab, width), bfloat),
         landed=pltpu.VMEM((RING, pages // 2, slab, width), bfloat),
         sums=pltpu.VMEM((2, 2, 2, height // 2, width), bfloat),
         came=pltpu.VMEM((2, 2, 2, height // 2, width), bfloat),
-        share=narrow(height),
-        pieces=pltpu.VMEM((2, bands, slab, width), bfloat),
+        pieces=pltpu.VMEM((4, bands, slab, width), bfloat),
         last=pltpu.VMEM((2, 2, slab, width), bfloat),
-        came3=pltpu.VMEM((2, 2, slab, width), bfloat),
-        came4=pltpu.VMEM((2, slab, width), bfloat),
-        final=pltpu.VMEM((2, slab, width), full),
+        hidden=narrow(tokens),
+        recv3=pltpu.VMEM((8, 2, slab, width), bfloat),
+        recv4=pltpu.VMEM((8, slab, width), bfloat),
+        final_up=wide(slab),
+        final_down=pltpu.VMEM((bands, slab, width // bands), full),
+        final_out=pltpu.VMEM((slab, width // bands), full),
+        final_qkv=pltpu.VMEM((slab, 3 * width // bands), full),
         q=narrow(tokens),
         kv=pltpu.VMEM((bands * tokens, 2 * width), bfloat),
         context=narrow(tokens),
@@ -1447,8 +1493,7 @@
         halo_low=narrow(halo_rows),
         vec=pltpu.VMEM(vec_shape.shape, full),
         vec_in=pltpu.VMEM((5,) + vec_shape.shape, full),
-        load_sems=dma((128,)),
-        weight_sems=dma((2, bands)),
+        load_sems=dma((192,)),
         core_send=dma((RING,)),
         core_recv=dma((RING,)),
         core_out=dma((RING, bands)),
@@ -1457,6 +1502,8 @@
         stage_recv=dma((8, 8)),
         halo_send=pair_sems,
         halo_recv=pair_sems,
+        hm_send=peer_sems,
+        hm_recv=peer_sems,
         memo_send=peer_sems,
         memo_recv=peer_sems,
         look_send=peer_sems,
@@ -1468,7 +1515,7 @@
     )
     result = launch(
         partial(back_kernel, dims),
-        dict(scalars=scalar)
+        lengths
         | {n: (v, VMEM) for n, v in near.items()}
         | {n: (v, ANY) for n, v in hbm.items()},
         {},
@@ -1476,47 +1523,38 @@
             vis_out=(low_shape(tokens, width), VMEM),
             vis_grad=(full_shape(tokens, width), VMEM),
             query_grad=(full_shape(rows, width), VMEM),
-            vec_out=(vec_shape, VMEM),
-            shares=(full_shape(8, slab, width), ANY),
-            bags=(low_shape(6, 2, 2, height, width), ANY),
+            query_out=(low_shape(rows, width), VMEM),
+            bout=(full_shape(4, slab), VMEM),
+            bup=(full_shape(2, height), VMEM),
+            bdown=(full_shape(2, slab), VMEM),
+            gain_grad=(full_shape(7, slab), VMEM),
+            bias_grad=(full_shape(7, slab), VMEM),
+            wqkv=(full_shape(4, slab, 3 * width // bands), ANY),
+            wout=(full_shape(4, slab, width // bands), ANY),
+            wup=(full_shape(2, slab, width), ANY),
+            wdown=(full_shape(2, bands, slab, width // bands), ANY),
+            bags=(low_shape(8, 2, 2, height, width), ANY),
             recv1=(low_shape(8, 2, 2, height // 2, width), ANY),
             recv2=(low_shape(8, 2, height // 2, width), ANY),
-            recv3=(low_shape(8, 2, slab, width), ANY),
-            recv4=(low_shape(8, slab, width), ANY),
         ),
         {},
         scratch,
-        2,
+        1,
         100 * tokens * width * width,
     )
 
-    shares, vec = result["shares"], result["vec_out"]
-    column = width // bands
-    attention = shares[7:3:-1]
-    down = shares[3::-2].reshape(2, slab, bands, column).swapaxes(1, 2)
-    page = lax.axis_index("page")
-    row_out, row_up, row_down, row_gain, row_bias = vec_rows(dims)
-    own = lax.dynamic_slice_in_dim(vec, page * slab, slab, 1)
-    hidden = hidden_units // pages
-    up_bias = lax.dynamic_slice_in_dim(
-        vec[row_up:row_down].reshape(2, hidden_units), page * hidden, hidden, 1
-    )
+    names = (
+        ("vis_out", "query_out", "vis_grad", "query_grad", "wqkv", "wout", "bout")
+        + ("wup", "bup", "wdown", "bdown", "gain_grad", "bias_grad")
+    )
+    final = dict(zip(names, hand_over([result[n] for n in names])))
     grid_shape = (1, band_rows, page_width, width)
-    return (
-        result["vis_out"].reshape(grid_shape),
-        feed["out"][None],
-        result["vis_grad"].reshape(grid_shape),
-        result["query_grad"][None],
-        attention[:, :, column:],
-        attention[:, :, :column],
-        own[row_out:row_up],
-        shares[2::-2],
-        up_bias,
-        down.reshape(2, bands * slab, column),
-        own[row_down:row_gain],
-        own[row_gain:row_bias],
-        own[row_bias : row_bias + 7],
-    )
+    final["vis_out"] = final["vis_out"].reshape(grid_shape)
+    final["vis_grad"] = final["vis_grad"].reshape(grid_shape)
+    final["query_out"] = final["query_out"][None]
+    final["query_grad"] = final["query_grad"][None]
+    final["wdown"] = jnp.swapaxes(final["wdown"], 1, 2)
+    return tuple(final[n] for n in names)
 
 
 def plain_ring(count, distance):

time: 409 us -> 356 us (0.87)
  Pallas kernels: 377 us -> 345 us
  local copies, waits for them, and re-layouts: 21.8 us -> 1.29 us
    pallas_call x3 -> x2, Pallas kernels: 377 us -> 341 us  [launch(): pl.pallas_call(inner, out_shape=[made[n][0] for n in made] + [kept[n] for...]
    slice x9 -> x0, local copies, waits for them, and re-layouts: 10.7 us -> none  [the longest x2 2.59 us: shards(): attention[:, :, column:]]
    pallas_call x0 -> x1, Pallas kernels: none -> 4.81 us  [hand_over(): pl.pallas_call(body, out_shape=[jax.ShapeDtypeStruct(s, a.dtype) for s, a...]
where the time goes in v3:
time: 356 us; the launch traced here: 349 us
  Pallas kernels  345 us (97%)
    pallas_call x2, Pallas kernels, launch(): pl.pallas_call(inner, out_shape=[made[n][0] for n in made] + [kept[n] for...  341 us

profile of v3, /device:TPU:0, one launch (start us, length us, event | category | flops | bytes accessed | tf_op | source)
XLA Modules:
  0.0 349.4 jit_solution(4892176675484413218)
XLA Ops:
  2.6 1.3 copy.32.refs_7_.refs_5_
  3.9 78.6 %shard_map.273 = (bf16[288,768]{1,0:T(8,128)(2,1)}, bf16[288,768]{1,0:T(8,128)(2,1)}, bf16[288,768]{1,0:T(8,128)(2,1)}, bf16[288,1536]{1,0:T(8,128)(2,1)}, bf16[...) custom-call(s32[1]{0:T(128)S(6)} %copy.33.refs_0_, ...), custom_call_target="tpu_custom_call" | custom-call | flops 6794772480 | bytes 16777216 | tf_op jit(solution)/shard_map/pallas_call | solution.py:350
  82.5 261.9 %shard_map.274 = (bf16[288,768]{1,0:T(8,128)(2,1)}, f32[288,768]{1,0:T(8,128)}, f32[160,768]{1,0:T(8,128)}, bf16[160,768]{1,0:T(8,128)(2,1)}, f32[4,96]{1,0:T(4,...) custom-call(s32[1]{0:T(128)S(6)} %copy.33.refs_0_, ...), custom_call_target="tpu_custom_call" | custom-call | flops 16986931200 | bytes 16777216 | tf_op jit(solution)/shard_map/pallas_call | solution.py:350
  344.4 4.8 %shard_map.275 = (bf16[288,768]{1,0:T(8,128)(2,1)}, bf16[160,768]{1,0:T(8,128)(2,1)}, f32[288,768]{1,0:T(8,128)}, f32[160,768]{1,0:T(8,128)}, f32[4,96,576]{2,1,...) custom-call(bf16[288,768]{1,0:T(8,128)(2,1)} %get-tuple-element.83.r, ...), custom_call_target="tpu_custom_call" | custom-call | tf_op jit(solution)/shard_map/pallas_call | solution.py:378
